TPU v7x, 32 devices: a whole 2x2x4 slice. The times are simulated.
32 devices in a mesh: crops: 8 (over z, x), rows: 4 (over y, core).
Axes of the slice: x: 2, y: 2, z: 4, core: 2. Of those that a mesh axis runs over, the one named last changes fastest.
Arguments:
- features: bfloat16 [640, 8, 8, 2048], P('crops', 'rows'), may hold values from -6 to 6
- pixel_mask: int32 [640, 8, 8], P('crops', 'rows'), may hold values from 0 to 1, as said below
- partners: int32 [640], P('crops'), may hold values from 0 to 639, as said below
- queued: float32 [3840, 128], P(('crops', 'rows')), as said below
- w_reduce: bfloat16 [2048, 512], P('crops'), may hold values from -0.125 to 0.125
- w_spatial: bfloat16 [4608, 512], P('crops'), may hold values from -0.09375 to 0.09375
- w_expand: bfloat16 [512, 2048], P('crops'), may hold values from -0.25 to 0.25
- w_hidden: bfloat16 [2048, 2048], P('crops'), may hold values from -0.125 to 0.125
- w_embed: bfloat16 [2048, 128], P('crops'), may hold values from -0.125 to 0.125
- prototypes: float32 [128, 3000], replicated, may hold values from -0.75 to 0.75
- gain_one: float32 [512], replicated, may hold values from 0.1 to 1.9
- bias_one: float32 [512], replicated, may hold values from -2.5 to 2.5
- gain_two: float32 [512], replicated, may hold values from 0.1 to 1.9
- bias_two: float32 [512], replicated, may hold values from -2.5 to 2.5
- gain_three: float32 [2048], replicated, may hold values from 0.1 to 1.9
- bias_three: float32 [2048], replicated, may hold values from -2.5 to 2.5
- gain_head: float32 [2048], replicated, may hold values from 0.1 to 1.9
- bias_head: float32 [2048], replicated, may hold values from -2.5 to 2.5
Outputs:
- swav_loss: float32 [], replicated
- grad_features: bfloat16 [640, 8, 8, 2048], P('crops', 'rows')
- grad_w_reduce: float32 [2048, 512], P('crops')
- grad_w_spatial: float32 [4608, 512], P('crops')
- grad_w_expand: float32 [512, 2048], P('crops')
- grad_w_hidden: float32 [2048, 2048], P('crops')
- grad_w_embed: float32 [2048, 128], P('crops')
- grad_prototypes: float32 [128, 3000], replicated
- grad_gain_one: float32 [512], replicated
- grad_bias_one: float32 [512], replicated
- grad_gain_two: float32 [512], replicated
- grad_bias_two: float32 [512], replicated
- grad_gain_three: float32 [2048], replicated
- grad_bias_three: float32 [2048], replicated
- grad_gain_head: float32 [2048], replicated
- grad_bias_head: float32 [2048], replicated
Inputs may be any that keep to these rules, and one draw needn't show every extreme that they name: `pixel_mask`: each crop's valid pixels form one rectangle of 7 x 7 or 6 x 8 pixels inside its map. partners[n] != n, partners[partners[n]] == n, and n and partners[n] lie in the same aligned block of 80 crops. `queued`: every row has a nonzero entry.
All inputs are finite; a program needn't handle non-finite values.
Results may differ from a plain program's by a relative error of at most 0.012.
Values may be sent and summed in bfloat16 or wider, within the bound.
No kernel may reach another device: no remote copies, remote signals or barrier semaphores. Data moves between devices by JAX's collectives and lax.ppermute only.
A program may use at most 192 MiB of HBM per device.

v0:
```python
import jax
import jax.numpy as jnp
from jax import lax
from jax.sharding import PartitionSpec as P

EPS_NORM = 1e-05
EPS_UNIT = 1e-06
SHARPNESS = 0.05
SOFTMAX_TEMPER = 0.1
PRECISE = lax.Precision.HIGHEST


def with_halo(cells, sides, width):
    for axis, dim in sides:
        count = lax.axis_size(axis)
        ends = count - 1
        head = lax.slice_in_dim(cells, 0, width, axis=dim)
        tail = lax.slice_in_dim(cells, cells.shape[dim] - width, cells.shape[dim], axis=dim)
        cells = jnp.concatenate(
            [
                lax.ppermute(tail, axis, [(i, (i + 1) % count) for i in range(ends)]),
                cells,
                lax.ppermute(head, axis, [((i + 1) % count, i) for i in range(ends)]),
            ],
            axis=dim,
        )
    return cells


def moments(value_entries, weights):
    first_sum = jnp.sum(value_entries * weights, axis=0)
    second_sum = jnp.sum(value_entries * value_entries * weights, axis=0)
    total_sum, square_sum, valid_count = lax.psum(
        (first_sum, second_sum, jnp.sum(weights)), ("crops", "rows")
    )
    col_mean = total_sum / valid_count
    spread = lax.rsqrt(square_sum / valid_count - col_mean * col_mean + EPS_NORM)
    return (col_mean, spread, valid_count)


def norm_back(upstream, normed, weights, gain, spread, valid_count):
    grad_gain, grad_bias = lax.psum(
        (jnp.sum(upstream * normed, axis=0), jnp.sum(upstream, axis=0)), ("crops", "rows")
    )
    grad_input = (
        weights * (gain * spread) * (upstream - (grad_bias + normed * grad_gain) / valid_count)
    )
    return (grad_input, grad_gain, grad_bias)


def gelu_back(inputs, upstream):
    return jax.vjp(jax.nn.gelu, inputs)[1](upstream)[0]


def tap_columns(extended, height, breadth):
    padded = jnp.pad(extended, ((0, 0), (0, 0), (1, 1), (0, 0)))
    pieces = [
        padded[:, tap_row : tap_row + height, tap_col : tap_col + breadth, :]
        for tap_row in range(3)
        for tap_col in range(3)
    ]
    return jnp.concatenate(pieces, axis=-1).reshape(-1, 9 * extended.shape[3])


def block_forward(features, pixel_mask, weights, params, kept_stats):
    w_reduce, w_spatial, w_expand = weights
    gain_one, bias_one, gain_two, bias_two, gain_three, bias_three = params
    local_crops, height, breadth, channels = features.shape
    masked = features * pixel_mask.astype(jnp.bfloat16)[..., None]
    flat_in = masked.reshape(-1, channels)
    weight_col = pixel_mask.reshape(-1, 1).astype(jnp.float32)
    pre_one = jnp.dot(flat_in, w_reduce, preferred_element_type=jnp.float32)
    stat_one = moments(pre_one, weight_col) if kept_stats is None else kept_stats[0]
    norm_one = (pre_one - stat_one[0]) * stat_one[1]
    act_one = gain_one * norm_one + bias_one
    hidden_one = (jax.nn.gelu(act_one) * weight_col).astype(jnp.bfloat16)
    grid_one = hidden_one.reshape(local_crops, height, breadth, -1)
    extended = with_halo(grid_one, (("rows", 1),), 1)
    columns = tap_columns(extended, height, breadth)
    pre_two = jnp.dot(columns, w_spatial, preferred_element_type=jnp.float32)
    stat_two = moments(pre_two, weight_col) if kept_stats is None else kept_stats[1]
    norm_two = (pre_two - stat_two[0]) * stat_two[1]
    act_two = gain_two * norm_two + bias_two
    hidden_two = (jax.nn.gelu(act_two) * weight_col).astype(jnp.bfloat16)
    pre_three = jnp.dot(hidden_two, w_expand, preferred_element_type=jnp.float32)
    stat_three = moments(pre_three, weight_col) if kept_stats is None else kept_stats[2]
    norm_three = (pre_three - stat_three[0]) * stat_three[1]
    summed = gain_three * norm_three + bias_three + flat_in.astype(jnp.float32)
    output = jax.nn.gelu(summed) * weight_col
    kept = (
        flat_in,
        weight_col,
        columns,
        norm_one,
        act_one,
        norm_two,
        act_two,
        hidden_two,
        norm_three,
        summed,
        output,
    )
    return (kept, (stat_one, stat_two, stat_three))


def shards(
    features,
    pixel_mask,
    partners,
    queued,
    w_reduce,
    w_spatial,
    w_expand,
    w_hidden,
    w_embed,
    prototypes,
    gain_one,
    bias_one,
    gain_two,
    bias_two,
    gain_three,
    bias_three,
    gain_head,
    bias_head,
):
    full_reduce, full_spatial, full_expand, full_hidden, full_embed = (
        lax.all_gather(w_reduce, "crops", axis=0, tiled=True),
        lax.all_gather(w_spatial, "crops", axis=0, tiled=True),
        lax.all_gather(w_expand, "crops", axis=0, tiled=True),
        lax.all_gather(w_hidden, "crops", axis=0, tiled=True),
        lax.all_gather(w_embed, "crops", axis=0, tiled=True),
    )
    block_weights = (full_reduce, full_spatial, full_expand)
    block_params = (gain_one, bias_one, gain_two, bias_two, gain_three, bias_three)
    local_crops, height, breadth, channels = features.shape
    kept, stats = block_forward(features, pixel_mask, block_weights, block_params, None)
    output = kept[10]
    crop_sums = jnp.sum(output.reshape(local_crops, height * breadth, channels), axis=1)
    crop_valid = jnp.sum(pixel_mask.reshape(local_crops, -1), axis=1).astype(jnp.float32)
    pooled_sum, crop_count = (
        lax.psum_scatter(crop_sums, "rows", scatter_dimension=0, tiled=True),
        lax.psum_scatter(crop_valid, "rows", scatter_dimension=0, tiled=True),
    )
    pooled = pooled_sum / crop_count[:, None]
    head_matrix = full_hidden.astype(jnp.float32)
    embed_matrix = full_embed.astype(jnp.float32)
    pre_head = jnp.dot(pooled, head_matrix, precision=PRECISE)
    head_ones = jnp.ones((pre_head.shape[0], 1), jnp.float32)
    stat_head = moments(pre_head, head_ones)
    norm_head = (pre_head - stat_head[0]) * stat_head[1]
    projector_activation = gain_head * norm_head + bias_head
    hidden_head = jax.nn.gelu(projector_activation)
    embedding = jnp.dot(hidden_head, embed_matrix, precision=PRECISE)
    inverse = lax.rsqrt(jnp.sum(embedding * embedding, axis=1, keepdims=True) + EPS_UNIT)
    unit_embed = embedding * inverse
    centroid_similarity = jnp.dot(unit_embed, prototypes, precision=PRECISE)
    queue_unit = queued * lax.rsqrt(jnp.sum(queued * queued, axis=1, keepdims=True) + EPS_UNIT)
    stored_similarity = jnp.dot(queue_unit, prototypes, precision=PRECISE)
    total_crops = local_crops * lax.axis_size("crops")
    row_total = total_crops + queued.shape[0] * lax.axis_size("crops") * lax.axis_size("rows")
    proto_total = centroid_similarity.shape[1]
    plan_mass = jnp.exp(centroid_similarity / SHARPNESS)
    queue_mass = jnp.exp(stored_similarity / SHARPNESS)
    for iteration in range(3):
        column = lax.psum(
            jnp.sum(plan_mass, axis=0) + jnp.sum(queue_mass, axis=0), ("crops", "rows")
        )
        plan_mass = plan_mass / (proto_total * column)
        queue_mass = queue_mass / (proto_total * column)
        plan_mass = plan_mass / (row_total * jnp.sum(plan_mass, axis=1, keepdims=True))
        queue_mass = queue_mass / (row_total * jnp.sum(queue_mass, axis=1, keepdims=True))
    balanced_cluster_labels = row_total * plan_mass
    everyone = lax.all_gather(balanced_cluster_labels, "rows", axis=0, tiled=True)
    share_rows = balanced_cluster_labels.shape[0]
    partner_rows = (
        lax.dynamic_slice_in_dim(partners, lax.axis_index("rows") * share_rows, share_rows)
        - lax.axis_index("crops") * local_crops
    )
    swapped_cluster_labels = jnp.take(everyone, partner_rows, axis=0)
    log_probability = jax.nn.log_softmax(centroid_similarity / SOFTMAX_TEMPER, axis=1)
    loss_part = -jnp.sum(swapped_cluster_labels * log_probability) / total_crops
    grad_scores = (
        jnp.exp(log_probability) * jnp.sum(swapped_cluster_labels, axis=1, keepdims=True)
        - swapped_cluster_labels
    ) / (SOFTMAX_TEMPER * total_crops)
    grad_proto_part = jnp.dot(unit_embed.T, grad_scores, precision=PRECISE)
    grad_unit = jnp.dot(grad_scores, prototypes.T, precision=PRECISE)
    grad_embedding = inverse * (
        grad_unit - unit_embed * jnp.sum(unit_embed * grad_unit, axis=1, keepdims=True)
    )
    grad_w_embed = jnp.dot(hidden_head.T, grad_embedding, precision=PRECISE)
    grad_hidden_head = jnp.dot(grad_embedding, embed_matrix.T, precision=PRECISE)
    grad_act_head = gelu_back(projector_activation, grad_hidden_head)
    grad_gain_head, grad_bias_head, grad_prototypes, swav_loss = lax.psum(
        (
            jnp.sum(grad_act_head * norm_head, axis=0),
            jnp.sum(grad_act_head, axis=0),
            grad_proto_part,
            loss_part,
        ),
        ("crops", "rows"),
    )
    grad_pre_head = (
        gain_head
        * stat_head[1]
        * (grad_act_head - (grad_bias_head + norm_head * grad_gain_head) / stat_head[2])
    )
    grad_w_hidden = jnp.dot(pooled.T, grad_pre_head, precision=PRECISE)
    grad_pooled = jnp.dot(grad_pre_head, head_matrix.T, precision=PRECISE)
    per_pixel = grad_pooled / crop_count[:, None]
    scale_rows = lax.all_gather(per_pixel, "rows", axis=0, tiled=True)
    kept, stats = block_forward(features, pixel_mask, block_weights, block_params, stats)
    (
        flat_in,
        weight_col,
        columns,
        norm_one,
        act_one,
        norm_two,
        act_two,
        hidden_two,
        norm_three,
        summed,
        output,
    ) = kept
    stat_one, stat_two, stat_three = stats
    grad_output = (
        scale_rows[:, None, :] * weight_col.reshape(local_crops, height * breadth, 1)
    ).reshape(-1, channels)
    grad_summed = gelu_back(summed, grad_output)
    grad_pre_three, grad_gain_three, grad_bias_three = norm_back(
        grad_summed, norm_three, weight_col, gain_three, stat_three[1], stat_three[2]
    )
    grad_pre_three = grad_pre_three.astype(jnp.bfloat16)
    grad_w_expand = jnp.dot(hidden_two.T, grad_pre_three, preferred_element_type=jnp.float32)
    grad_hidden_two = jnp.dot(grad_pre_three, full_expand.T, preferred_element_type=jnp.float32)
    grad_act_two = gelu_back(act_two, grad_hidden_two * weight_col)
    grad_pre_two, grad_gain_two, grad_bias_two = norm_back(
        grad_act_two, norm_two, weight_col, gain_two, stat_two[1], stat_two[2]
    )
    grad_pre_two = grad_pre_two.astype(jnp.bfloat16)
    grad_w_spatial = jnp.dot(columns.T, grad_pre_two, preferred_element_type=jnp.float32)
    narrow = grad_pre_two.shape[1]
    grad_grid = grad_pre_two.reshape(local_crops, height, breadth, narrow)
    grad_extended = with_halo(grad_grid, (("rows", 1),), 1)
    spatial_back = (
        full_spatial.reshape(9, -1, narrow)[::-1].transpose(0, 2, 1).reshape(9 * narrow, -1)
    )
    grad_hidden_one = jnp.dot(
        tap_columns(grad_extended, height, breadth),
        spatial_back,
        preferred_element_type=jnp.float32,
    )
    grad_act_one = gelu_back(act_one, grad_hidden_one * weight_col)
    grad_pre_one, grad_gain_one, grad_bias_one = norm_back(
        grad_act_one, norm_one, weight_col, gain_one, stat_one[1], stat_one[2]
    )
    grad_pre_one = grad_pre_one.astype(jnp.bfloat16)
    grad_w_reduce = jnp.dot(flat_in.T, grad_pre_one, preferred_element_type=jnp.float32)
    grad_features = (
        (
            (jnp.dot(grad_pre_one, full_reduce.T, preferred_element_type=jnp.float32) + grad_summed)
            * weight_col
        )
        .astype(jnp.bfloat16)
        .reshape(features.shape)
    )
    sum_reduce, sum_spatial, sum_expand, sum_hidden, sum_embed = (
        lax.psum_scatter(grad_w_reduce, "crops", scatter_dimension=0, tiled=True),
        lax.psum_scatter(grad_w_spatial, "crops", scatter_dimension=0, tiled=True),
        lax.psum_scatter(grad_w_expand, "crops", scatter_dimension=0, tiled=True),
        lax.psum_scatter(grad_w_hidden, "crops", scatter_dimension=0, tiled=True),
        lax.psum_scatter(grad_w_embed, "crops", scatter_dimension=0, tiled=True),
    )
    out_reduce, out_spatial, out_expand, out_hidden, out_embed = lax.psum(
        (sum_reduce, sum_spatial, sum_expand, sum_hidden, sum_embed), "rows"
    )
    return (
        swav_loss,
        grad_features,
        out_reduce,
        out_spatial,
        out_expand,
        out_hidden,
        out_embed,
        grad_prototypes,
        grad_gain_one,
        grad_bias_one,
        grad_gain_two,
        grad_bias_two,
        grad_gain_three,
        grad_bias_three,
        grad_gain_head,
        grad_bias_head,
    )


def solution(mesh):
    in_specs = (
        P("crops", "rows", None, None),
        P("crops", "rows", None),
        P("crops"),
        P(("crops", "rows"), None),
        P("crops", None),
        P("crops", None),
        P("crops", None),
        P("crops", None),
        P("crops", None),
        P(),
        P(),
        P(),
        P(),
        P(),
        P(),
        P(),
        P(),
        P(),
    )
    out_specs = (
        P(),
        P("crops", "rows", None, None),
        P("crops", None),
        P("crops", None),
        P("crops", None),
        P("crops", None),
        P("crops", None),
        P(),
        P(),
        P(),
        P(),
        P(),
        P(),
        P(),
        P(),
        P(),
    )
    return jax.shard_map(shards, mesh=mesh, in_specs=in_specs, out_specs=out_specs, check_vma=False)
```

profile of v0, /device:TPU:1, one launch (start us, length us, event | category | flops | bytes accessed | tf_op | source)
XLA Modules:
  0.0 1605.5 jit_solution(18232524275703027354)
XLA Ops:
  18.8 41.7 %all-gather.7.cloned.1.call-done = bf16[2048,512]{1,0:T(8,128)(2,1)} async-done(((bf16[256,512]{1,0:T(8,128)(2,1)}), bf16[2048,512]{1,0:T(8,128)(2,1)}) %all-gather.7.cloned.1.call-update) | async-done | bytes 2097168 | tf_op jit(solution)/shard_map/all_gather | solution.py:127
  68.2 41.9 %all-reduce.12 = (f32[512]{0:T(512)S(1)}, f32[]{:T(128)}, f32[512]{0:T(512)S(1)}) all-reduce(f32[512]{0:T(512)S(1)} %get-tuple-element.23, f32[]{:T(128)} %convert_reduce_fusion, f32[512]{0:T(512)S(1)} %get-tuple-element.22), channel_id=1, replica_groups=mesh['crops'=8,'rows'=4] {'crops','rows'}, use_global_device_ids=true, to_apply=%region_5.0 | all-reduce | flops 1025 | bytes 8200 | tf_op jit(solution)/shard_map/psum | solution.py:33
  135.2 28.6 %all_gather.25 = bf16[2048,128]{1,0:T(8,128)(2,1)} all-gather(bf16[256,128]{1,0:T(8,128)(2,1)S(1)} %copy-done.27), channel_id=1, replica_groups=mesh['crops'=8,'rows'=4] {'crops'}, dimensions={0}, use_global_device_ids=true | all-gather | bytes 589824 | tf_op jit(solution)/shard_map/all_gather | solution.py:131
  185.4 11.7 multiply_reduce_fusion.6
  197.1 45.9 %all-reduce.11 = (f32[512]{0:T(512)S(1)}, f32[512]{0:T(512)S(1)}) all-reduce(f32[512]{0:T(512)S(1)} %get-tuple-element.21, f32[512]{0:T(512)S(1)} %get-tuple-element.20), channel_id=1, replica_groups=mesh['crops'=8,'rows'=4] {'crops','rows'}, use_global_device_ids=true, to_apply=%region_9.10 | all-reduce | flops 1024 | bytes 8192 | tf_op jit(solution)/shard_map/psum | solution.py:33
  253.1 45.0 %all-reduce.10 = (f32[2048]{0:T(1024)S(1)}, f32[2048]{0:T(1024)S(1)}) all-reduce(f32[2048]{0:T(1024)S(1)} %get-tuple-element.17, f32[2048]{0:T(1024)S(1)} %get-tuple-element.16), channel_id=1, replica_groups=mesh['crops'=8,'rows'=4] {'crops','rows'}, use_global_device_ids=true, to_apply=%region_11.12 | all-reduce | flops 4096 | bytes 32768 | tf_op jit(solution)/shard_map/psum | solution.py:33
  300.1 13.3 multiply_multiply_fusion.2
  346.8 42.2 %all-reduce.9 = (f32[2048]{0:T(1024)S(1)}, f32[]{:T(128)}, f32[2048]{0:T(1024)S(1)}) all-reduce(f32[2048]{0:T(1024)S(1)} %get-tuple-element.37, f32[]{:T(128)} %constant.39.clone.1, f32[2048]{0:T(1024)S(1)} %get-tuple-element.36), channel_id=1, replica_groups=mesh['crops'=8,'rows'=4] {'crops','rows'}, use_global_device_ids=true, to_apply=%region_22.23 | all-reduce | flops 4097 | bytes 32776 | tf_op jit(solution)/shard_map/psum | solution.py:33
  394.8 40.7 %psum.212 = f32[3000]{0:T(1024)} all-reduce(f32[3000]{0:T(1024)} %add.273), channel_id=1, replica_groups=mesh['crops'=8,'rows'=4] {'crops','rows'}, use_global_device_ids=true, to_apply=%region_27.28 | all-reduce | flops 3000 | bytes 24000 | tf_op jit(solution)/shard_map/psum | solution.py:165
  438.8 41.3 %psum.213 = f32[3000]{0:T(1024)} all-reduce(f32[3000]{0:T(1024)} %add.274), channel_id=1, replica_groups=mesh['crops'=8,'rows'=4] {'crops','rows'}, use_global_device_ids=true, to_apply=%region_32.33 | all-reduce | flops 3000 | bytes 24000 | tf_op jit(solution)/shard_map/psum | solution.py:165
  485.2 40.0 %psum.214 = f32[3000]{0:T(1024)S(1)} all-reduce(f32[3000]{0:T(1024)S(1)} %add.275), channel_id=1, replica_groups=mesh['crops'=8,'rows'=4] {'crops','rows'}, use_global_device_ids=true, to_apply=%region_37.38 | all-reduce | flops 3000 | bytes 24000 | tf_op jit(solution)/shard_map/psum | solution.py:165
  527.0 13.3 all-gather
  548.2 37.0 %all-reduce.8 = (f32[2048]{0:T(1024)S(1)}, f32[2048]{0:T(1024)S(1)}) all-reduce(f32[2048]{0:T(1024)S(1)} %get-tuple-element.35, f32[2048]{0:T(1024)S(1)} %get-tuple-element.34), channel_id=1, replica_groups=mesh['crops'=8,'rows'=4] {'crops','rows'}, use_global_device_ids=true, to_apply=%region_48.49 | all-reduce | flops 4096 | bytes 32768 | tf_op jit(solution)/shard_map/psum | solution.py:194
  605.9 15.1 fusion.82
  621.0 38.6 %all-reduce.7 = (f32[2048]{0:T(1024)S(1)}, f32[2048]{0:T(1024)S(1)}) all-reduce(f32[2048]{0:T(1024)S(1)} %get-tuple-element.19, f32[2048]{0:T(1024)S(1)} %get-tuple-element.18), channel_id=1, replica_groups=mesh['crops'=8,'rows'=4] {'crops','rows'}, use_global_device_ids=true, to_apply=%region_52.53 | all-reduce | flops 4096 | bytes 32768 | tf_op jit(solution)/shard_map/psum | solution.py:42
  676.0 39.6 %all-reduce.6 = (f32[512]{0:T(512)S(1)}, f32[512]{0:T(512)S(1)}) all-reduce(f32[512]{0:T(512)S(1)} %get-tuple-element.27, f32[512]{0:T(512)S(1)} %get-tuple-element.26), channel_id=1, replica_groups=mesh['crops'=8,'rows'=4] {'crops','rows'}, use_global_device_ids=true, to_apply=%region_56.57 | all-reduce | flops 1024 | bytes 8192 | tf_op jit(solution)/shard_map/psum | solution.py:42
  769.1 39.8 %all-reduce.5 = (f32[]{:T(128)}, f32[512]{0:T(512)S(1)}, f32[512]{0:T(512)S(1)}) all-reduce(f32[]{:T(128)S(6)} %div.220, f32[512]{0:T(512)S(1)} %get-tuple-element.25, f32[512]{0:T(512)S(1)} %get-tuple-element.24), channel_id=1, replica_groups=mesh['crops'=8,'rows'=4] {'crops','rows'}, use_global_device_ids=true, to_apply=%region_42.43 | all-reduce | flops 1025 | bytes 8200 | tf_op jit(solution)/shard_map/psum | solution.py:194
  821.2 13.3 fusion.98
  835.5 16.8 %fusion.58 = f32[2048,2048]{1,0:T(8,128)} fusion(f32[36,2048]{1,0:T(8,128)S(1)} %copy-done.9, u32[]{:S(6)} %subtract, f32[20]{0:T(128)S(1)} %copy-done.43, f32[20,2048]{1,0:T(8,128)S(1)} %get-tuple-element.112, f32[20,2048]{1,0:T(8,128)S(1)} %get-tuple-element.104, f32[]{:T(128)} %get-tuple-element.48, f32[2048]{0:T(1024)S(1)} %get-tuple-element.129, ...), kind=kOutput, calls=%fused_computation.144 | convolution fusion | flops 1006960640 | bytes 17408520 | tf_op jit(solution)/shard_map/dot_general | solution.py:208
  857.0 52.3 %reduce-scatter.8.cloned.1.call-done = f32[256,512]{1,0:T(8,128)} async-done(((f32[2048,512]{1,0:T(8,128)}), f32[256,512]{1,0:T(8,128)}) %reduce-scatter.8.cloned.1.call-update) | async-done | bytes 524304 | tf_op jit(solution)/shard_map/reduce_scatter | solution.py:269
  909.3 167.1 %reduce-scatter.10.cloned.1.call-done = f32[576,512]{1,0:T(8,128)} async-done(((f32[4608,512]{1,0:T(8,128)}), f32[576,512]{1,0:T(8,128)}) %reduce-scatter.10.cloned.1.call-update) | async-done | bytes 1179664 | tf_op jit(solution)/shard_map/reduce_scatter | solution.py:270
  1076.4 285.4 %reduce-scatter.14.cloned.1.call-done = f32[256,2048]{1,0:T(8,128)} async-done(((f32[2048,2048]{1,0:T(8,128)}), f32[256,2048]{1,0:T(8,128)}) %reduce-scatter.14.cloned.1.call-update) | async-done | bytes 2097168 | tf_op jit(solution)/shard_map/reduce_scatter | solution.py:272
  1369.7 127.9 %all-reduce.17.cloned.1.call-done = f32[128,3000]{0,1:T(8,128)} async-done(((f32[128,3000]{0,1:T(8,128)}), f32[128,3000]{0,1:T(8,128)}) %all-reduce.17.cloned.1.call-update) | async-done | bytes 1536016 | tf_op jit(solution)/shard_map/psum | solution.py:194
  1497.6 92.9 %all-reduce.19.cloned.1.call-done = (f32[256,512]{1,0:T(8,128)}, f32[576,512]{1,0:T(8,128)}, f32[64,2048]{1,0:T(8,128)}, f32[256,2048]{1,0:T(8,128)}, f32[256,128]{1,0:T(8,128)}) async-done(((f32[256,512]{1,0:T(8,128)}, f32[576,512]{1,0:T(8,128)}, f32[64,2048]{1,0:T(8,128)}, f32[256,2048]{1,0:T(8,128)}, f32[256,128]{1,0:T(8,128)}), (f32[256,512]{1,0:T(8,128)}, f32[576,512]{1,0:T(8,128)}, ...) | async-done | bytes 4456464 | tf_op jit(solution)/shard_map/psum | solution.py:275
  (316 shorter events, 256.6 us)
Async XLA Ops:
  7.2 156.7 %copy-start = (f32[128,3000]{0,1:T(8,128)S(1)}, f32[128,3000]{0,1:T(8,128)}, u32[]{:S(2)}) copy-start(f32[128,3000]{0,1:T(8,128)} %param.27) | copy-start | bytes 4608004
  7.2 53.3 %all-gather.7.cloned.1.call-start = ((), (), s32[]{:S(2)}) async-start(), calls=%async_computation.5 | async-start | bytes 2359296 | tf_op jit(solution)/shard_map/all_gather | solution.py:127
  7.9 177.5 %all-gather.9.cloned.1.call-start = ((), (), s32[]{:S(2)}) async-start(), calls=%async_computation.6 | async-start | bytes 5308416 | tf_op jit(solution)/shard_map/all_gather | solution.py:128
  8.7 235.6 %all-gather.11.cloned.1.call-start = ((), (), s32[]{:S(2)}) async-start(), calls=%async_computation.7 | async-start | bytes 2359296 | tf_op jit(solution)/shard_map/all_gather | solution.py:129
  9.4 331.5 %all-gather.13.cloned.1.call-start = ((), (), s32[]{:S(2)}) async-start(), calls=%async_computation.8 | async-start | bytes 9437184 | tf_op jit(solution)/shard_map/all_gather | solution.py:130
  10.0 846.9 %reduce-scatter.16.cloned.1.call-start = ((), (), s32[]{:S(2)}) async-start(), calls=%async_computation.13 | async-start | bytes 1179648 | tf_op jit(solution)/shard_map/reduce_scatter | solution.py:273
  111.4 66.9 %copy-start.29 = (f32[512]{0:T(512)}, f32[512]{0:T(512)S(1)}, u32[]{:S(2)}) copy-start(f32[512]{0:T(512)S(1)} %get-tuple-element.63) | copy-start | bytes 6148
  111.4 66.9 %copy-start.31 = (f32[512]{0:T(512)}, f32[512]{0:T(512)S(1)}, u32[]{:S(2)}) copy-start(f32[512]{0:T(512)S(1)} %get-tuple-element.98) | copy-start | bytes 6148
  116.6 49.5 %collective-permute-start = (bf16[80,1,8,512]{3,2,1,0:T(8,128)(2,1)}, bf16[80,1,8,512]{3,2,1,0:T(8,128)(2,1)}, u32[]{:S(2)}, u32[]{:S(2)}) collective-permute-start(bf16[80,1,8,512]{3,2,1,0:T(8,128)(2,1)} %get-tuple-element.89), channel_id=1, source_target_pairs={{0,1},{1,2},{2,3},{4,5},{5,6},{6,7},{8,9},{9,10},{10,11},{12,13},{... | collective-permute-start | bytes 1966088 | tf_op jit(solution)/shard_map/ppermute | solution.py:21
  121.0 45.1 %collective-permute-start.1 = (bf16[80,1,8,512]{3,2,1,0:T(8,128)(2,1)}, bf16[80,1,8,512]{3,2,1,0:T(8,128)(2,1)}, u32[]{:S(2)}, u32[]{:S(2)}) collective-permute-start(bf16[80,1,8,512]{3,2,1,0:T(8,128)(2,1)} %get-tuple-element.90), channel_id=1, source_target_pairs={{1,0},{2,1},{3,2},{5,4},{6,5},{7,6},{9,8},{10,9},{11,10},{13,12},{... | collective-permute-start | bytes 1966088 | tf_op jit(solution)/shard_map/ppermute | solution.py:23
  134.6 206.3 %copy-start.41 = (f32[20]{0:T(128)}, f32[20]{0:T(128)S(1)}, u32[]{:S(2)}) copy-start(f32[20]{0:T(128)S(1)} %dynamic-slice.3) | copy-start | bytes 244
  185.4 58.9 %copy-start.80 = (f32[512]{0:T(512)S(1)}, f32[512]{0:T(512)}, u32[]{:S(2)}) copy-start(f32[512]{0:T(512)} %param.31) | copy-start | bytes 6148
  332.3 6.3 collective-permute-start.4
  585.1 249.5 %copy-start.37 = (f32[2048]{0:T(1024)}, f32[2048]{0:T(1024)S(1)}, u32[]{:S(2)}) copy-start(f32[2048]{0:T(1024)S(1)} %get-tuple-element.129) | copy-start | bytes 24580
  585.1 249.5 %copy-start.38 = (f32[2048]{0:T(1024)}, f32[2048]{0:T(1024)S(1)}, u32[]{:S(2)}) copy-start(f32[2048]{0:T(1024)S(1)} %get-tuple-element.130) | copy-start | bytes 24580
  605.7 251.3 %reduce-scatter.12.cloned.1.call-start = ((), (), s32[]{:S(2)}) async-start(), calls=%async_computation.11 | async-start | bytes 4718592 | tf_op jit(solution)/shard_map/reduce_scatter | solution.py:271
  724.6 184.7 %reduce-scatter.8.cloned.1.call-start = ((), (), s32[]{:S(2)}) async-start(), calls=%async_computation.9 | async-start | bytes 4718592 | tf_op jit(solution)/shard_map/reduce_scatter | solution.py:269
  730.6 17.3 %collective-permute-start.2 = (bf16[80,1,8,512]{3,2,1,0:T(8,128)(2,1)}, bf16[80,1,8,512]{3,2,1,0:T(8,128)(2,1)S(1)}, u32[]{:S(2)}, u32[]{:S(2)}) collective-permute-start(bf16[80,1,8,512]{3,2,1,0:T(8,128)(2,1)} %get-tuple-element.85), channel_id=1, source_target_pairs={{0,1},{1,2},{2,3},{4,5},{5,6},{6,7},{8,9},{9,10},{10,11},{12,13},{... | collective-permute-start | bytes 1966088 | tf_op jit(solution)/shard_map/ppermute | solution.py:21
  736.0 12.5 collective-permute-start.3
  821.1 255.3 %reduce-scatter.10.cloned.1.call-start = ((), (), s32[]{:S(2)}) async-start(), calls=%async_computation.10 | async-start | bytes 10616832 | tf_op jit(solution)/shard_map/reduce_scatter | solution.py:270
  834.5 527.3 %reduce-scatter.14.cloned.1.call-start = ((), (), s32[]{:S(2)}) async-start(), calls=%async_computation.12 | async-start | bytes 18874368 | tf_op jit(solution)/shard_map/reduce_scatter | solution.py:272
  852.4 645.2 %all-reduce.17.cloned.1.call-start = ((), (), s32[]{:S(2)}) async-start(), calls=%async_computation.14 | async-start | bytes 3072000 | tf_op jit(solution)/shard_map/psum | solution.py:194
  856.8 505.0 %copy-start.12 = (bf16[1280,512]{1,0:T(8,128)(2,1)S(1)}, bf16[1280,512]{1,0:T(8,128)(2,1)}, u32[]{:S(2)}) copy-start(bf16[1280,512]{1,0:T(8,128)(2,1)} %copy-done.11) | copy-start | bytes 3932164
  856.9 733.7 %all-reduce.19.cloned.1.call-start = ((), (), s32[]{:S(2)}) async-start(), calls=%async_computation.15 | async-start | bytes 8912896 | tf_op jit(solution)/shard_map/psum | solution.py:275
  (78 other events, 1072.7 us)
Sparse Core Ops, SparseCore 0:
  10.2 50.2 all-gather.6
  62.7 81.1 all-gather.8
  146.0 48.2 all-gather.10
  196.3 126.2 all-gather.12
  605.8 60.7 reduce-scatter.15
  724.7 89.0 reduce-scatter.11
  821.2 88.0 reduce-scatter.7
  913.3 163.0 reduce-scatter.9
  1080.7 281.0 reduce-scatter.13
  1367.6 130.0 all-reduce.16
  1500.3 90.1 all-reduce.18
where the time goes:
time: 1610 us
  waiting for transfers between devices  772 us (48%)
  blocking collectives  526 us (33%)
  matrix products  128 us (8%)
  other arithmetic  95 us (6%)
  local copies, waits for them, and re-layouts  48 us (3%)
  starting transfers between devices  19.2 us (1%)
  between operations  17.1 us (1%)
    reduce_scatter x1, waiting for transfers between devices, shards(): lax.psum_scatter(grad_w_hidden, 'crops', scatter_dimension=0, tiled=True)  285 us
    psum x4, blocking collectives, moments(): lax.psum((first_sum, second_sum, jnp.sum(weights)), ('crops', 'rows'))  175 us
    reduce_scatter x1, waiting for transfers between devices, shards(): lax.psum_scatter(grad_w_spatial, 'crops', scatter_dimension=0, tiled=True)  167 us
    psum x1, waiting for transfers between devices, shards(): lax.psum((jnp.sum(grad_act_head * norm_head, axis=0), jnp.sum(grad_act_he...  128 us
    psum x3, blocking collectives, shards(): lax.psum(jnp.sum(plan_mass, axis=0) + jnp.sum(queue_mass, axis=0), ('crop...  122 us
    psum x1, waiting for transfers between devices, shards(): lax.psum((sum_reduce, sum_spatial, sum_expand, sum_hidden, sum_embed), 'r...  92.9 us
    psum x2, blocking collectives, norm_back(): lax.psum((jnp.sum(upstream * normed, axis=0), jnp.sum(upstream, axis=0)),...  78.2 us
    psum x2, blocking collectives, shards(): lax.psum((jnp.sum(grad_act_head * norm_head, axis=0), jnp.sum(grad_act_he...  76.8 us
  transfers between devices with their start and end apart: 16, of which 8 were waited for; matrix products, arithmetic and copies ran while one was open for 14% of the time, Pallas kernels for 0%

commit v1 on v0

v1 whole, which is shorter than its diff:
```python
import functools
import math

import jax
import jax.numpy as jnp
from jax import lax
from jax.experimental import pallas as pl
from jax.experimental.pallas import tpu as pltpu
from jax.sharding import PartitionSpec as P

EPS_NORM = 1e-05
EPS_UNIT = 1e-06
SHARPNESS = 0.05
SOFTMAX_TEMPER = 0.1
PRECISE = lax.Precision.HIGHEST
BOTH = ("crops", "rows")
GELU_SCALE = 0.7978845608028654
GELU_CUBE = 0.044715
F32 = jnp.float32
BF16 = jnp.bfloat16


def bits_of(axis):
    return [1 << k for k in range(lax.axis_size(axis).bit_length() - 1)]


def xor_permute(values, crop_xor, row_xor):
    crop_total, row_total = lax.axis_size("crops"), lax.axis_size("rows")
    pairs = [
        (c * row_total + r, (c ^ crop_xor) * row_total + (r ^ row_xor))
        for c in range(crop_total)
        for r in range(row_total)
    ]
    return lax.ppermute(values, BOTH, pairs)


def all_bits():
    return [(0, b) for b in bits_of("rows")] + [(b, 0) for b in bits_of("crops")]


def total_wide(values):
    steps = all_bits()
    groups = [steps[:1]] + [steps[k : k + 2] for k in range(1, len(steps), 2)]
    for group in groups:
        if len(group) == 1:
            values = values + xor_permute(values, *group[0])
        else:
            (a, b), (c, d) = group
            near = xor_permute(values, a, b)
            far = xor_permute(values, c, d)
            both = xor_permute(values, a ^ c, b ^ d)
            values = (values + near) + (far + both)
    return values


def total_carrying(values, rows_extra):
    width, own = values.shape[1], rows_extra.reshape(1, -1)
    slots = {0: own}
    steps = all_bits()
    groups = [steps[:1]] + [steps[k : k + 2] for k in range(1, len(steps), 2)]

    def send(step, current):
        if step[0]:
            return xor_permute(current, *step), {}
        keys = sorted(slots)
        got = xor_permute(jnp.concatenate([current] + [slots[k] for k in keys], axis=1), *step)
        parts = jnp.split(got[:, width:], len(keys), axis=1)
        return got[:, :width], {k ^ step[1]: part for k, part in zip(keys, parts)}

    for group in groups:
        if len(group) == 1:
            other, more = send(group[0], values)
            values = values + other
            slots.update(more)
        else:
            (a, b), (c, d) = group
            near, near_slots = send((a, b), values)
            far, far_slots = send((c, d), values)
            both, both_slots = send((a ^ c, b ^ d), values)
            values = (values + near) + (far + both)
            for more in (near_slots, far_slots, both_slots):
                slots.update(more)
    stacked = jnp.concatenate([slots[k] for k in sorted(slots)], axis=0)
    return values, stacked.reshape(-1, rows_extra.shape[1])


def after(values, *earlier):
    return lax.optimization_barrier((values,) + earlier)[0]


def total_narrow(values):
    count = lax.axis_size("crops") * lax.axis_size("rows")
    copies = jnp.broadcast_to(values[None], (count,) + values.shape)
    return jnp.sum(lax.all_to_all(copies, BOTH, 0, 0, tiled=True), axis=0)


def my_bit(step):
    crop_xor, row_xor = step
    if crop_xor:
        return (lax.axis_index("crops") // crop_xor) % 2
    return (lax.axis_index("rows") // row_xor) % 2


def halve(values, dim, step, narrow):
    bit = my_bit(step)
    kept = lax.dynamic_index_in_dim(values, bit, dim, keepdims=False)
    sent = lax.dynamic_index_in_dim(values, 1 - bit, dim, keepdims=False)
    if narrow:
        sent = sent.astype(BF16)
    return kept.astype(F32) + xor_permute(sent, *step).astype(F32)


def double(values, step):
    other = xor_permute(values, *step)
    low = my_bit(step) == 0
    return jnp.stack([jnp.where(low, values, other), jnp.where(low, other, values)])


def swap_sum(values, dims, bits):
    crop_total, row_total = lax.axis_size("crops"), lax.axis_size("rows")
    crop_mask, row_mask = sum(b for b, _ in bits), sum(b for _, b in bits)
    groups = {}
    for c in range(crop_total):
        for r in range(row_total):
            groups.setdefault((c & ~crop_mask, r & ~row_mask), []).append(c * row_total + r)
    front = [k for k, step in enumerate(dims) if step in bits]
    rest = [k for k in range(values.ndim) if k not in front]
    values = values.transpose(front + rest)
    values = values.reshape((2 ** len(bits),) + values.shape[len(bits) :]).astype(BF16)
    values = lax.all_to_all(
        values, BOTH, 0, 0, axis_index_groups=list(groups.values()), tiled=True
    )
    return jnp.sum(values.astype(F32), axis=0), [step for step in dims if step not in bits]


def gather_rows(values):
    row_bits = [(0, b) for b in bits_of("rows")]
    count = len(row_bits)
    rows, cols = values.shape
    for step in reversed(row_bits):
        values = double(values, step)
    values = values.transpose(tuple(range(count - 1, -1, -1)) + (count, count + 1))
    return values.reshape(-1, cols)


def reduce_stages(values):
    row_bits = [(0, b) for b in reversed(bits_of("rows"))]
    crop_bits = [(b, 0) for b in reversed(bits_of("crops"))]
    dims = crop_bits + row_bits
    rows, cols = values.shape
    values = values.reshape((2,) * len(dims) + (rows >> len(dims), cols))
    values = halve(values, len(dims) - 1, dims[-1], True)
    yield values
    values, dims = swap_sum(values, dims[:-1], row_bits[:-1] + crop_bits[-1:])
    yield values
    values, dims = swap_sum(values, dims, list(dims))
    yield values
    yield gather_rows(values.astype(BF16)).astype(F32)


def row_quarter(weight):
    size = weight.shape[0] // lax.axis_size("rows")
    return lax.dynamic_slice_in_dim(weight, lax.axis_index("rows") * size, size)


def gather_first(weight):
    crop_total = lax.axis_size("crops")
    size, cols = weight.shape[0] // 2, weight.shape[1]
    bit = lax.axis_index("rows") % 2
    mine = lax.dynamic_slice_in_dim(weight, bit * size, size)
    mine = lax.all_to_all(
        jnp.broadcast_to(mine[None], (crop_total, size, cols)), "crops", 0, 0, tiled=True
    )
    other = xor_permute(mine, 0, 1)
    low = bit == 0
    both = jnp.stack([jnp.where(low, mine, other), jnp.where(low, other, mine)], axis=1)
    return both.reshape(2 * crop_total * size, cols)


def gather_pair(first, second):
    quarter_one, quarter_two = row_quarter(first), row_quarter(second)
    cols = first.shape[1]
    blocks = second.shape[1] // cols
    size, short = quarter_one.shape[0], quarter_two.shape[0]
    flat_two = quarter_two.reshape(short, blocks, cols).transpose(1, 0, 2).reshape(-1, cols)
    whole = lax.all_gather(jnp.concatenate([quarter_one, flat_two], axis=0), BOTH, axis=0, tiled=False)
    count = whole.shape[0]
    second_blocks = whole[:, size:].reshape(count, blocks, short, cols).transpose(1, 0, 2, 3)
    if size % 16:
        whole, size = whole[:, :size].reshape(1, -1, cols), count * size
    return (whole, size), second_blocks.reshape(blocks, -1, cols)


def gather_products(left, right):
    mean = jnp.mean(left, axis=0, keepdims=True)
    total = jnp.sum(right, axis=0, keepdims=True)
    mean_high, total_high = lax.reduce_precision(mean, 8, 7), lax.reduce_precision(total, 8, 7)
    mean_low, total_low = mean - mean_high, total - total_high
    left = jnp.concatenate([left - mean, mean_high, mean_high, mean_low, mean_low], axis=0)
    right = jnp.concatenate([right, total_high, total_low, total_high, total_low], axis=0)
    return (
        lax.all_gather(left.astype(BF16), BOTH, axis=0, tiled=True),
        lax.all_gather(right.astype(BF16), BOTH, axis=0, tiled=True),
    )


def spread_of(sums, count):
    mean = sums[0] / count
    return mean, lax.rsqrt(sums[1] / count - mean * mean + EPS_NORM)


def gelu_both(x, mask=None):
    square = x * x
    half = 0.5 * jnp.tanh(x * (GELU_SCALE + GELU_SCALE * GELU_CUBE * square)) + 0.5
    inner = x * (2.0 * GELU_SCALE + 6.0 * GELU_SCALE * GELU_CUBE * square)
    kept = half if mask is None else half * mask
    return x * kept, kept * (1.0 + (1.0 - half) * inner)


def split_parts(x, parts):
    pieces = []
    for _ in range(parts - 1):
        piece = lax.reduce_precision(x, 8, 7)
        pieces.append(piece.astype(BF16))
        x = x - piece
    pieces.append(x.astype(BF16))
    return jnp.concatenate(pieces, axis=0)


def split_dot(x, matrix, dim, parts):
    count = x.shape[0]
    out = lax.dot_general(
        split_parts(x, parts), matrix, (((1,), (dim,)), ((), ())), preferred_element_type=F32
    )
    total = out[(parts - 1) * count :]
    for k in range(parts - 2, -1, -1):
        total = total + out[k * count : (k + 1) * count]
    return total


TN = (((0,), (0,)), ((), ()))
NT = (((1,), (1,)), ((), ()))
TILE = 16
UNROLL = 16


def kernel_call(body, grid, ins, outs, scratch, args, flops, transcendentals=0):
    moved = sum(a.size * a.dtype.itemsize for a in args) + sum(
        math.prod(s.shape) * s.dtype.itemsize for s, _ in outs
    )
    return pl.pallas_call(
        body,
        grid=(grid,),
        in_specs=ins,
        out_specs=[spec for _, spec in outs],
        out_shape=[shape for shape, _ in outs],
        scratch_shapes=scratch,
        compiler_params=pltpu.CompilerParams(vmem_limit_bytes=52 * 2**20),
        cost_estimate=pl.CostEstimate(
            flops=flops, bytes_accessed=moved, transcendentals=transcendentals
        ),
    )(*args)


def whole_block(array):
    zeros = (0,) * array.ndim
    return pl.BlockSpec(array.shape, lambda k: zeros)


def spatial_block(weight):
    array, size = weight
    return pl.BlockSpec((array.shape[0], size, array.shape[2]), lambda k: (0, 0, 0))


def sum_block(width):
    return jax.ShapeDtypeStruct((8, width), F32), pl.BlockSpec((8, width), lambda k: (0, 0))


def tall(row):
    return jnp.broadcast_to(row.reshape(1, -1), (TILE, row.size))


def fold(values):
    return values[:8] + values[8:]


def loop(count, step, start):
    return lax.fori_loop(0, count, step, start, unroll=math.gcd(count, UNROLL))


def clear_first(*refs):
    @pl.when(pl.program_id(0) == 0)
    def _():
        for ref in refs:
            ref[...] = jnp.zeros_like(ref)


def planes_of(height, width, rows):
    return pl.BlockSpec((height, rows, width), lambda k: (0, k, 0))


def gather_tile(ref, index, height):
    if height == 1:
        return ref[0, pl.ds(pl.multiple_of(index * TILE, TILE), TILE), :]
    return jnp.concatenate(
        [ref[i, pl.ds(pl.multiple_of(index * 8, 8), 8), :] for i in range(height)], axis=0
    )


def store_tile(ref, index, values, height):
    if height == 1:
        ref[0, pl.ds(pl.multiple_of(index * TILE, TILE), TILE), :] = values
    else:
        for i in range(height):
            ref[i, pl.ds(pl.multiple_of(index * 8, 8), 8), :] = values[8 * i : 8 * i + 8]


def tile_rows(index):
    return pl.ds(pl.multiple_of(index * TILE, TILE), TILE)


def first_body(height, x_ref, m_ref, c_ref, hidden_ref, slope_ref, sum_ref):
    clear_first(sum_ref)
    pairs = x_ref.shape[0] // 2
    width = x_ref.shape[3]
    for i in range(height):

        def step(k, carry):
            x = x_ref[pl.ds(pl.multiple_of(2 * k, 2), 2), i].reshape(TILE, width)
            m = m_ref[i, tile_rows(k), :]
            value, slope = gelu_both(c_ref[:TILE] * x + c_ref[TILE:], m)
            hidden = value.astype(BF16)
            hidden_ref[i, tile_rows(k), :] = hidden
            slope_ref[i, tile_rows(k), :] = slope
            return carry + fold(hidden.astype(F32))

        sum_ref[...] += loop(pairs, step, jnp.zeros(sum_ref.shape, F32))


def first_hidden(pre_one, mask_planes, scale, shift):
    crops, height, breadth, width = pre_one.shape
    tile = 16
    consts = jnp.concatenate([tall(scale), tall(shift)], axis=0)
    planes = planes_of(height, width, tile * 8)
    hidden, slope, sums = kernel_call(
        functools.partial(first_body, height),
        crops // tile,
        [
            pl.BlockSpec((tile, height, 8, width), lambda k: (k, 0, 0, 0)),
            planes_of(height, 1, tile * 8),
            whole_block(consts),
        ],
        [
            (jax.ShapeDtypeStruct((height, crops * 8, width), BF16), planes),
            (jax.ShapeDtypeStruct((height, crops * 8, width), F32), planes),
            sum_block(width),
        ],
        [],
        (pre_one, mask_planes, consts),
        40 * pre_one.size,
        pre_one.size,
    )
    return hidden, slope, jnp.sum(sums, axis=0)


def shifted(values, back):
    wide = values.astype(F32).reshape(2, 8, values.shape[1])
    place = lax.broadcasted_iota(jnp.int32, wide.shape, 1)
    before = jnp.where(place == 0, 0.0, pltpu.roll(wide, 1, 1)).reshape(values.shape).astype(BF16)
    after = jnp.where(place == 7, 0.0, pltpu.roll(wide, 7, 1)).reshape(values.shape).astype(BF16)
    return (after, before) if back else (before, after)


def fill_taps(read, out_ref, back):
    width = out_ref.shape[1] // 3

    def step(k, carry):
        values = read(k)
        low, high = shifted(values, back)
        out_ref[tile_rows(k), :width] = low
        out_ref[tile_rows(k), width : 2 * width] = values
        out_ref[tile_rows(k), 2 * width :] = high
        return carry

    loop(out_ref.shape[0] // TILE, step, 0)


def tap_dot(taps, w_ref, tap_row, back):
    width = taps.shape[1] // 3
    w_ref = w_ref.reshape(w_ref.shape[0] * w_ref.shape[1], w_ref.shape[2])
    if not back:
        return jnp.dot(
            taps, w_ref[3 * width * tap_row : 3 * width * (tap_row + 1), :], preferred_element_type=F32
        )
    total = None
    for b in range(3):
        at = (3 * tap_row + b) * width
        part = lax.dot_general(
            taps[:, b * width : (b + 1) * width],
            w_ref[at : at + width, :],
            NT,
            preferred_element_type=F32,
        )
        total = part if total is None else total + part
    return total


def local_body(height, back, x_ref, w_ref, out_ref, taps_ref):
    for p in range(height):
        fill_taps(lambda k, p=p: x_ref[p, tile_rows(k), :], taps_ref.at[p], back)
    for i in range(height):
        total = None
        for p in range(height):
            tap_row = i - p + 1 if back else p - i + 1
            if 0 <= tap_row <= 2:
                part = tap_dot(taps_ref[p], w_ref, tap_row, back)
                total = part if total is None else total + part
        out_ref[i] = total


def conv_local(planes, weight, back):
    height, rows, width = planes.shape
    parts = 2 if rows % 32 == 0 else 1
    block = planes_of(height, width, rows // parts)
    (out,) = kernel_call(
        functools.partial(local_body, height, back),
        parts,
        [block, spatial_block(weight)],
        [(jax.ShapeDtypeStruct(planes.shape, F32), block)],
        [pltpu.VMEM((height, rows // parts, 3 * width), BF16)],
        (planes, weight[0]),
        2 * rows * (3 * height - 2) * 3 * width * width,
    )
    return out


def add_halo(height, back, part_ref, above_ref, below_ref, w_ref, taps_ref):
    fill_taps(lambda k: above_ref[tile_rows(k), :], taps_ref.at[0], back)
    fill_taps(lambda k: below_ref[tile_rows(k), :], taps_ref.at[1], back)
    upper = tap_dot(taps_ref[0], w_ref, 2 if back else 0, back)
    lower = tap_dot(taps_ref[1], w_ref, 0 if back else 2, back)
    if height == 1:
        return [part_ref[0] + (upper + lower)]
    middle = [part_ref[i] for i in range(1, height - 1)]
    return [part_ref[0] + upper] + middle + [part_ref[height - 1] + lower]


def halo_body(height, part_ref, above_ref, below_ref, w_ref, m_ref, out_ref, sum_ref, square_ref, taps_ref):
    clear_first(sum_ref, square_ref)
    rows = add_halo(height, False, part_ref, above_ref, below_ref, w_ref, taps_ref)
    for i in range(height):
        out_ref[i] = rows[i]
    for i in range(height):

        def step(k, carry):
            x = out_ref[i, tile_rows(k), :]
            first = x * m_ref[i, tile_rows(k), :]
            return carry[0] + fold(first), carry[1] + fold(first * x)

        zero = jnp.zeros(sum_ref.shape, F32)
        first, second = loop(out_ref.shape[1] // TILE, step, (zero, zero))
        sum_ref[...] += first
        square_ref[...] += second


def conv_halo(part, above, below, weight, mask_planes):
    height, rows, width = part.shape
    parts = 2 if rows % 32 == 0 else 1
    size = rows // parts
    block = planes_of(height, width, size)
    edge = pl.BlockSpec((size, width), lambda k: (k, 0))
    out, first, second = kernel_call(
        functools.partial(halo_body, height),
        parts,
        [block, edge, edge, spatial_block(weight), planes_of(height, 1, size)],
        [(jax.ShapeDtypeStruct(part.shape, F32), block), sum_block(width), sum_block(width)],
        [pltpu.VMEM((2, size, 3 * width), BF16)],
        (part, above, below, weight[0], mask_planes),
        2 * rows * 2 * 3 * width * width,
    )
    return out, jnp.sum(first, axis=0), jnp.sum(second, axis=0)


def halo_back_body(
    height, part_ref, above_ref, below_ref, w_ref, slope_ref, x_ref, out_ref, sum_ref, dot_ref, taps_ref
):
    clear_first(sum_ref, dot_ref)
    rows = add_halo(height, True, part_ref, above_ref, below_ref, w_ref, taps_ref)
    for i in range(height):
        out_ref[i] = rows[i]
    width = out_ref.shape[2]
    for i in range(height):

        def step(k, carry):
            g = out_ref[i, tile_rows(k), :] * slope_ref[i, tile_rows(k), :]
            out_ref[i, tile_rows(k), :] = g
            x = x_ref[pl.ds(pl.multiple_of(2 * k, 2), 2), i].reshape(TILE, width)
            return carry[0] + fold(g), carry[1] + fold(g * x)

        zero = jnp.zeros(sum_ref.shape, F32)
        first, second = loop(out_ref.shape[1] // TILE, step, (zero, zero))
        sum_ref[...] += first
        dot_ref[...] += second


def conv_back_halo(part, above, below, weight, slope, pre_one):
    height, rows, width = part.shape
    parts = 2 if rows % 32 == 0 else 1
    size = rows // parts
    block = planes_of(height, width, size)
    edge = pl.BlockSpec((size, width), lambda k: (k, 0))
    out, first, second = kernel_call(
        functools.partial(halo_back_body, height),
        parts,
        [
            block,
            edge,
            edge,
            spatial_block(weight),
            block,
            pl.BlockSpec((size // 8, height, 8, width), lambda k: (k, 0, 0, 0)),
        ],
        [(jax.ShapeDtypeStruct(part.shape, F32), block), sum_block(width), sum_block(width)],
        [pltpu.VMEM((2, size, 3 * width), BF16)],
        (part, above, below, weight[0], slope, pre_one),
        2 * rows * 2 * 3 * width * width,
    )
    return out, jnp.sum(first, axis=0), jnp.sum(second, axis=0)


def spatial_grad_body(height, x_ref, above_ref, below_ref, g_ref, mean_ref, total_ref, out_ref, taps_ref):
    rows = g_ref.shape[1]
    reads = [lambda k: above_ref[tile_rows(k), :]]
    reads += [lambda k, p=p: x_ref[p, tile_rows(k), :] for p in range(height)]
    reads += [lambda k: below_ref[tile_rows(k), :]]
    for b in range(3):

        @pl.when(pl.program_id(0) == b)
        def _(b=b):
            for p in range(height + 2):

                def step(k, carry, p=p):
                    values = reads[p](k)
                    if b != 1:
                        values = shifted(values, False)[b // 2]
                    taps_ref[p, tile_rows(k), :] = values
                    return carry

                loop(rows // TILE, step, 0)

    for a in range(3):
        total = None
        for i in range(height):
            part = lax.dot_general(taps_ref[i + a], g_ref[i], TN, preferred_element_type=F32)
            total = part if total is None else total + part
        out_ref[a, 0] = (total - mean_ref[...] * total_ref[...]).astype(BF16)


def spatial_grad(hidden, above, below, grads, hidden_mean, grad_total):
    height, rows, width = hidden.shape
    mean, total = hidden_mean.reshape(width, 1), grad_total.reshape(1, width)
    (out,) = kernel_call(
        functools.partial(spatial_grad_body, height),
        3,
        [whole_block(a) for a in (hidden, above, below, grads, mean, total)],
        [
            (
                jax.ShapeDtypeStruct((3, 3, width, width), BF16),
                pl.BlockSpec((3, 1, width, width), lambda k: (0, k, 0, 0)),
            )
        ],
        [pltpu.VMEM((height + 2, rows, width), BF16)],
        (hidden, above, below, grads, mean, total),
        2 * 9 * height * rows * width * width,
    )
    return out.reshape(9 * width, width)


def second_body(height, x_ref, m_ref, c_ref, w_ref, hidden_ref, slope_ref, sum_ref, square_ref, mean_ref, y_ref):
    clear_first(sum_ref, square_ref, mean_ref)
    tiles = hidden_ref.shape[0] // TILE

    def step(k, carry):
        x = gather_tile(x_ref, k, height)
        m = m_ref[tile_rows(k), :]
        value, slope = gelu_both(c_ref[:TILE] * x + c_ref[TILE:], m)
        hidden = value.astype(BF16)
        hidden_ref[tile_rows(k), :] = hidden
        store_tile(slope_ref, k, slope, height)
        return carry + fold(hidden.astype(F32))

    mean_ref[...] += loop(tiles, step, jnp.zeros(mean_ref.shape, F32))
    half = w_ref.shape[2]
    for part in range(w_ref.shape[0]):
        cols = slice(part * half, (part + 1) * half)
        y_ref[:, cols] = jnp.dot(hidden_ref[...], w_ref[part], preferred_element_type=F32)

        def add(k, carry):
            y = y_ref[tile_rows(k), cols]
            return carry[0] + fold(y), carry[1] + fold(y * y)

        zero = jnp.zeros((8, half), F32)
        first, second = loop(tiles, add, (zero, zero))
        sum_ref[:, cols] += first
        square_ref[:, cols] += second


def second_hidden(pre_two, mask_flat, scale, shift, weight):
    height, rows, width = pre_two.shape
    channels = weight.shape[0] * weight.shape[2]
    crops = rows // 8
    tile = 16
    flat = tile * height * 8
    consts = jnp.concatenate([tall(scale), tall(shift)], axis=0)
    hidden, slope, first, second, mean = kernel_call(
        functools.partial(second_body, height),
        crops // tile,
        [
            planes_of(height, width, tile * 8),
            pl.BlockSpec((flat, 1), lambda k: (k, 0)),
            whole_block(consts),
            whole_block(weight),
        ],
        [
            (jax.ShapeDtypeStruct((height * rows, width), BF16), pl.BlockSpec((flat, width), lambda k: (k, 0))),
            (jax.ShapeDtypeStruct(pre_two.shape, F32), planes_of(height, width, tile * 8)),
            sum_block(channels),
            sum_block(channels),
            sum_block(width),
        ],
        [pltpu.VMEM((flat, channels), F32)],
        (pre_two, mask_flat, consts, weight),
        2 * height * rows * width * channels,
        pre_two.size,
    )
    return hidden, slope, jnp.sum(first, axis=0), jnp.sum(second, axis=0), jnp.sum(mean, axis=0)


def third_body(height, h_ref, w_ref, f_ref, m_ref, c_ref, slope_ref, pool_ref, first_ref, second_ref, y_ref):
    crops = pool_ref.shape[0]
    pixels = height * 8
    step_rows = max(pixels, TILE)
    per_step = step_rows // pixels
    chunk = w_ref.shape[2]
    for part in range(w_ref.shape[0]):
        cols = slice(part * chunk, (part + 1) * chunk)
        y_ref[:, cols] = jnp.dot(h_ref[...], w_ref[part], preferred_element_type=F32)

        def step(k, carry):
            at = pl.ds(pl.multiple_of(k * step_rows, TILE), step_rows)
            y = y_ref[at, cols]
            m = m_ref[at, :]
            s = y.reshape(-1, TILE, chunk) * c_ref[:TILE, cols] + c_ref[TILE:, cols]
            s = s.reshape(step_rows, chunk) + f_ref[at, cols].astype(F32)
            value, slope = gelu_both(s, m)
            slope_ref[at, cols] = slope.astype(BF16)
            for j in range(per_step):
                rows = slice(j * pixels, (j + 1) * pixels)
                crop = pl.ds(k * per_step + j, 1)
                pool_ref[crop, cols] = jnp.sum(value[rows], axis=0, keepdims=True)
                first_ref[crop, cols] = jnp.sum(slope[rows], axis=0, keepdims=True)
                second_ref[crop, cols] = jnp.sum(slope[rows] * y[rows], axis=0, keepdims=True)
            return carry

        loop(crops // per_step, step, 0)


def third_output(hidden, weight, features, mask_flat, scale, shift, height):
    total, width = hidden.shape
    channels = weight.shape[0] * weight.shape[2]
    tile = 16
    flat = tile * height * 8
    crops = total // (height * 8)
    consts = jnp.concatenate([tall(scale), tall(shift)], axis=0)
    rows_of = lambda n: pl.BlockSpec((flat, n), lambda k: (k, 0))
    crop_rows = (jax.ShapeDtypeStruct((crops, channels), F32), pl.BlockSpec((tile, channels), lambda k: (k, 0)))
    return kernel_call(
        functools.partial(third_body, height),
        crops // tile,
        [rows_of(width), whole_block(weight), rows_of(channels), rows_of(1), whole_block(consts)],
        [(jax.ShapeDtypeStruct((total, channels), BF16), rows_of(channels)), crop_rows, crop_rows, crop_rows],
        [pltpu.VMEM((flat, channels), F32)],
        (hidden, weight, features, mask_flat, consts),
        2 * total * width * channels + 40 * total * channels,
        total * channels,
    )


def third_back_body(
    height,
    h_ref,
    w_ref,
    d_ref,
    m_ref,
    s_ref,
    c_ref,
    slope_ref,
    x_ref,
    mean_ref,
    centred_ref,
    total_ref,
    out_ref,
    sum_ref,
    dot_ref,
    y_ref,
    g_ref,
    back_ref,
    grad_ref,
):
    clear_first(grad_ref, total_ref, sum_ref, dot_ref)
    crops = s_ref.shape[0]
    pixels = height * 8
    step_rows = max(pixels, TILE)
    per_step = step_rows // pixels
    chunk = w_ref.shape[2]
    for part in range(w_ref.shape[0]):
        cols = slice(part * chunk, (part + 1) * chunk)
        y_ref[:, cols] = jnp.dot(h_ref[...], w_ref[part], preferred_element_type=F32)

        def step(k, carry):
            at = pl.ds(pl.multiple_of(k * step_rows, TILE), step_rows)
            scales = [
                jnp.broadcast_to(s_ref[pl.ds(k * per_step + j, 1), cols], (pixels, chunk))
                for j in range(per_step)
            ]
            scale = scales[0] if per_step == 1 else jnp.concatenate(scales, axis=0)
            line = y_ref[at, cols].reshape(-1, TILE, chunk) * c_ref[TILE:, cols] + c_ref[:TILE, cols]
            g = d_ref[at, cols].astype(F32) * scale + m_ref[at, :] * line.reshape(step_rows, chunk)
            g = g.astype(BF16)
            g_ref[at, cols] = g
            g = g.astype(F32)
            return carry + jnp.sum(g.reshape(-1, 8, chunk), axis=0)

        total_ref[:, cols] += loop(crops // per_step, step, jnp.zeros((8, chunk), F32))
    grad_ref[...] += lax.dot_general(h_ref[...], g_ref[...], TN, preferred_element_type=F32)
    back = None
    for part in range(w_ref.shape[0]):
        cols = slice(part * chunk, (part + 1) * chunk)
        term = lax.dot_general(g_ref[:, cols], w_ref[part], NT, preferred_element_type=F32)
        back = term if back is None else back + term
    back_ref[...] = back

    def finish(k, carry):
        g = back_ref[tile_rows(k), :] * gather_tile(slope_ref, k, height)
        store_tile(out_ref, k, g, height)
        return carry[0] + fold(g), carry[1] + fold(g * gather_tile(x_ref, k, height))

    zero = jnp.zeros(sum_ref.shape, F32)
    first, second = loop(h_ref.shape[0] // TILE, finish, (zero, zero))
    sum_ref[...] += first
    dot_ref[...] += second

    @pl.when(pl.program_id(0) == pl.num_programs(0) - 1)
    def _():
        total = jnp.sum(total_ref[...], axis=0, keepdims=True)

        def centre(k, carry):
            at = tile_rows(k)
            centred_ref[at, :] = (grad_ref[at, :] - mean_ref[at, :] * total).astype(BF16)
            return carry

        lax.fori_loop(0, grad_ref.shape[0] // TILE, centre, 0, unroll=4)


def third_back(
    hidden, weight, slope_three, mask_flat, scale_rows, beta, gamma, slope_two, pre_two, hidden_mean
):
    height, rows, width = pre_two.shape
    total = height * rows
    channels = weight.shape[0] * weight.shape[2]
    mean = hidden_mean.reshape(width, 1)
    tile = 16
    flat = tile * height * 8
    crops = rows // 8
    consts = jnp.concatenate([tall(beta), tall(gamma)], axis=0)
    rows_of = lambda n: pl.BlockSpec((flat, n), lambda k: (k, 0))
    planes = planes_of(height, width, tile * 8)
    grad, sums, out, first, second = kernel_call(
        functools.partial(third_back_body, height),
        crops // tile,
        [
            rows_of(width),
            whole_block(weight),
            rows_of(channels),
            rows_of(1),
            pl.BlockSpec((tile, channels), lambda k: (k, 0)),
            whole_block(consts),
            planes,
            planes,
            whole_block(mean),
        ],
        [
            (jax.ShapeDtypeStruct((width, channels), BF16), pl.BlockSpec((width, channels), lambda k: (0, 0))),
            sum_block(channels),
            (jax.ShapeDtypeStruct(pre_two.shape, F32), planes),
            sum_block(width),
            sum_block(width),
        ],
        [
            pltpu.VMEM((flat, channels), F32),
            pltpu.VMEM((flat, channels), BF16),
            pltpu.VMEM((flat, width), F32),
            pltpu.VMEM((width, channels), F32),
        ],
        (hidden, weight, slope_three, mask_flat, scale_rows, consts, slope_two, pre_two, mean),
        6 * total * width * channels,
    )
    return grad, jnp.sum(sums, axis=0), out, jnp.sum(first, axis=0), jnp.sum(second, axis=0)


def second_back_body(height, g_ref, x_ref, m_ref, c_ref, out_ref, sum_ref):
    clear_first(sum_ref)
    for i in range(height):

        def step(k, carry):
            at = tile_rows(k)
            line = c_ref[TILE : 2 * TILE] + c_ref[2 * TILE :] * x_ref[i, at, :]
            g = (c_ref[:TILE] * g_ref[i, at, :] + m_ref[i, at, :] * line).astype(BF16)
            out_ref[i, at, :] = g
            return carry + fold(g.astype(F32))

        sum_ref[...] += loop(g_ref.shape[1] // TILE, step, jnp.zeros(sum_ref.shape, F32))


def second_back(grads, pre_two, mask_planes, alpha, beta, gamma):
    height, rows, width = pre_two.shape
    size = 128
    consts = jnp.concatenate([tall(alpha), tall(beta), tall(gamma)], axis=0)
    block = planes_of(height, width, size)
    out, sums = kernel_call(
        functools.partial(second_back_body, height),
        rows // size,
        [block, block, planes_of(height, 1, size), whole_block(consts)],
        [(jax.ShapeDtypeStruct(pre_two.shape, BF16), block), sum_block(width)],
        [],
        (grads, pre_two, mask_planes, consts),
        10 * pre_two.size,
    )
    return out, jnp.sum(sums, axis=0)


def first_back_body(height, g_ref, x_ref, m_ref, c_ref, out_ref):
    width = out_ref.shape[1]
    per_step = max(1, 2 // height)

    def step(k, carry):
        g = gather_tile(g_ref, k, height)
        x = x_ref[pl.ds(k * per_step, per_step)].reshape(-1, width)
        line = c_ref[TILE : 2 * TILE] + c_ref[2 * TILE :] * x
        out_ref[tile_rows(k), :] = (c_ref[:TILE] * g + m_ref[tile_rows(k), :] * line).astype(BF16)
        return carry

    loop(out_ref.shape[0] // TILE, step, 0)


def first_back(grads, pre_one, mask_flat, alpha, beta, gamma):
    crops, height, breadth, width = pre_one.shape
    tile = 16
    flat = tile * height * 8
    consts = jnp.concatenate([tall(alpha), tall(beta), tall(gamma)], axis=0)
    (out,) = kernel_call(
        functools.partial(first_back_body, height),
        crops // tile,
        [
            planes_of(height, width, tile * 8),
            pl.BlockSpec((tile, height, 8, width), lambda k: (k, 0, 0, 0)),
            pl.BlockSpec((flat, 1), lambda k: (k, 0)),
            whole_block(consts),
        ],
        [
            (
                jax.ShapeDtypeStruct((crops * height * 8, width), BF16),
                pl.BlockSpec((flat, width), lambda k: (k, 0)),
            )
        ],
        [],
        (grads, pre_one, mask_flat, consts),
        10 * pre_one.size,
    )
    return out


def last_body(height, g_ref, w_ref, d_ref, s_ref, out_ref, y_ref):
    y_ref[...] = lax.dot_general(g_ref[...], w_ref[...], NT, preferred_element_type=F32)
    pixels = height * 8
    step_rows = max(pixels, TILE)
    per_step = step_rows // pixels
    chunk = 1024
    for part in range(y_ref.shape[1] // chunk):
        cols = slice(part * chunk, (part + 1) * chunk)

        def step(k, carry):
            at = pl.ds(pl.multiple_of(k * step_rows, TILE), step_rows)
            scales = [
                jnp.broadcast_to(s_ref[pl.ds(k * per_step + j, 1), cols], (pixels, chunk))
                for j in range(per_step)
            ]
            scale = scales[0] if per_step == 1 else jnp.concatenate(scales, axis=0)
            out_ref[at, cols] = (y_ref[at, cols] + d_ref[at, cols].astype(F32) * scale).astype(BF16)
            return carry

        loop(s_ref.shape[0] // per_step, step, 0)


def last_grads(grads, weight, slope_three, scale_rows, height):
    total, width = grads.shape
    channels = weight.shape[0]
    tile = 16
    flat = tile * height * 8
    crops = total // (height * 8)
    rows_of = lambda n: pl.BlockSpec((flat, n), lambda k: (k, 0))
    (out,) = kernel_call(
        functools.partial(last_body, height),
        crops // tile,
        [
            rows_of(width),
            whole_block(weight),
            rows_of(channels),
            pl.BlockSpec((tile, channels), lambda k: (k, 0)),
        ],
        [(jax.ShapeDtypeStruct((total, channels), BF16), rows_of(channels))],
        [pltpu.VMEM((flat, channels), F32)],
        (grads, weight, slope_three, scale_rows),
        2 * total * width * channels,
    )
    return out


def edge_rows(planes):
    ends = lax.axis_size("rows") - 1
    above = lax.ppermute(planes[-1], "rows", [(i, i + 1) for i in range(ends)])
    below = lax.ppermute(planes[0], "rows", [(i + 1, i) for i in range(ends)])
    return above, below


def back_consts(gain, mean, spread, count, grad_sum, grad_dot):
    grad_gain = spread * (grad_dot - mean * grad_sum)
    alpha = gain * spread
    gamma = -alpha * spread * grad_gain / count
    beta = -alpha * grad_sum / count - gamma * mean
    return alpha, beta, gamma, grad_gain


def shards(
    features,
    pixel_mask,
    partners,
    queued,
    w_reduce,
    w_spatial,
    w_expand,
    w_hidden,
    w_embed,
    prototypes,
    gain_one,
    bias_one,
    gain_two,
    bias_two,
    gain_three,
    bias_three,
    gain_head,
    bias_head,
):
    local_crops, height, breadth, channels = features.shape
    pixels = height * breadth
    narrow = w_reduce.shape[1]
    row_count = lax.axis_size("rows")
    share = local_crops // row_count
    total_crops = local_crops * lax.axis_size("crops")
    full_reduce = gather_first(w_reduce)
    full_spatial, full_expand = gather_pair(w_spatial, w_expand)
    head_whole = lax.all_gather(
        jnp.concatenate([row_quarter(w_hidden), row_quarter(w_embed)], axis=1), BOTH, axis=0, tiled=True
    )
    hidden_cols = w_hidden.shape[1]
    full_hidden, full_embed = head_whole[:, :hidden_cols], head_whole[:, hidden_cols:]

    flat_in = features.reshape(-1, channels)
    weight_col = pixel_mask.reshape(-1, 1).astype(F32)
    mask_planes = (
        pixel_mask.transpose(1, 0, 2).reshape(height, local_crops * breadth, 1).astype(F32)
    )

    pre_one = jnp.dot(flat_in, full_reduce, preferred_element_type=F32)
    masked_one = pre_one * weight_col
    sums_one = total_narrow(
        jnp.stack(
            [
                jnp.sum(masked_one, axis=0),
                jnp.sum(masked_one * pre_one, axis=0),
                jnp.full((narrow,), jnp.sum(weight_col)),
            ]
        )
    )
    valid_count = sums_one[2, :1]
    mean_one, spread_one = spread_of(sums_one, valid_count)
    pre_one = pre_one.reshape(local_crops, height, breadth, narrow)
    scale_one = gain_one * spread_one
    hidden_one, slope_one, hidden_sum_one = first_hidden(
        pre_one, mask_planes, scale_one, bias_one - mean_one * scale_one
    )
    above_one, below_one = edge_rows(hidden_one)
    part_two = conv_local(hidden_one, full_spatial, False)
    pre_two, sum_two, square_two = conv_halo(part_two, above_one, below_one, full_spatial, mask_planes)
    sums_two = total_narrow(jnp.stack([sum_two, square_two, hidden_sum_one]))
    mean_two, spread_two = spread_of(sums_two, valid_count)
    hidden_mean_one = sums_two[2] / valid_count
    scale_two = gain_two * spread_two
    hidden_two, slope_two, sum_three, square_three, hidden_sum_two = second_hidden(
        pre_two, weight_col, scale_two, bias_two - mean_two * scale_two, full_expand
    )
    sums_three = total_wide(jnp.concatenate([sum_three, square_three, hidden_sum_two])[None])[0]
    hidden_mean_two = sums_three[2 * channels :] / valid_count
    mean_three, spread_three = spread_of(sums_three[: 2 * channels].reshape(2, -1), valid_count)
    scale_three = gain_three * spread_three
    slope_three, crop_sums, slope_sums, slope_dots = third_output(
        hidden_two, full_expand, flat_in, weight_col, scale_three, bias_three - mean_three * scale_three, height
    )
    crop_valid = jnp.sum(pixel_mask.reshape(local_crops, -1), axis=1).astype(F32)

    row_bits = [(0, b) for b in bits_of("rows")]
    pooled = jnp.concatenate(
        [crop_sums, jnp.broadcast_to(crop_valid[:, None], (local_crops, 128))], axis=1
    )
    pooled = pooled.reshape((2,) * len(row_bits) + (share, channels + 128))
    for k, step in enumerate(row_bits):
        pooled = halve(pooled, len(row_bits) - 1 - k, step, False)
    crop_count = pooled[:, channels : channels + 1]
    pooled = pooled[:, :channels] / crop_count

    pre_head = split_dot(pooled, full_hidden, 0, 3)
    sums_head = total_wide(jnp.stack([jnp.sum(pre_head, axis=0), jnp.sum(pre_head * pre_head, axis=0)]))
    mean_head, spread_head = spread_of(sums_head, F32(total_crops))
    norm_head = (pre_head - mean_head) * spread_head
    hidden_head, slope_head = gelu_both(gain_head * norm_head + bias_head)
    embedding = split_dot(hidden_head, full_embed, 0, 3)
    inverse = lax.rsqrt(jnp.sum(embedding * embedding, axis=1, keepdims=True) + EPS_UNIT)
    unit_embed = embedding * inverse

    partner_rows = (
        lax.dynamic_slice_in_dim(partners, lax.axis_index("rows") * share, share)
        - lax.axis_index("crops") * local_crops
    )
    partner_at = (partner_rows // share ^ lax.axis_index("rows")) * share + partner_rows % share
    queue_unit = queued * lax.rsqrt(jnp.sum(queued * queued, axis=1, keepdims=True) + EPS_UNIT)
    row_total = total_crops + queued.shape[0] * lax.axis_size("crops") * row_count
    proto_total = prototypes.shape[1]
    scores = jnp.dot(unit_embed, prototypes, precision=PRECISE)
    queue_scores = jnp.dot(queue_unit, prototypes, precision=PRECISE)
    plan_mass = jnp.exp(scores / SHARPNESS)
    queue_mass = jnp.exp(queue_scores / SHARPNESS)
    for iteration in range(3):
        column = jnp.sum(plan_mass, axis=0, keepdims=True) + jnp.sum(queue_mass, axis=0, keepdims=True)
        if iteration == 0:
            column, everyone = total_carrying(column, unit_embed)
            partner_embed = jnp.take(everyone, partner_at, axis=0)
            partner_scores = jnp.dot(partner_embed, prototypes, precision=PRECISE)
            partner_mass = jnp.exp(partner_scores / SHARPNESS)
        else:
            column = total_wide(column)
        scale = 1.0 / (proto_total * column)
        partner_mass = partner_mass * scale
        partner_mass = partner_mass / (row_total * jnp.sum(partner_mass, axis=1, keepdims=True))
        if iteration < 2:
            plan_mass = plan_mass * scale
            queue_mass = queue_mass * scale
            plan_mass = plan_mass / (row_total * jnp.sum(plan_mass, axis=1, keepdims=True))
            queue_mass = queue_mass / (row_total * jnp.sum(queue_mass, axis=1, keepdims=True))
    target = row_total * partner_mass
    log_probability = jax.nn.log_softmax(scores / SOFTMAX_TEMPER, axis=1)
    loss_part = -jnp.sum(target * log_probability) / total_crops
    grad_scores = (
        jnp.exp(log_probability) * jnp.sum(target, axis=1, keepdims=True) - target
    ) / (SOFTMAX_TEMPER * total_crops)
    grad_unit = jnp.dot(grad_scores, prototypes.T, precision=PRECISE)
    grad_embedding = inverse * (
        grad_unit - unit_embed * jnp.sum(unit_embed * grad_unit, axis=1, keepdims=True)
    )
    grad_hidden_head = split_dot(grad_embedding, full_embed, 1, 3)
    grad_act_head = grad_hidden_head * slope_head
    sums_back = total_wide(
        jnp.stack(
            [
                jnp.sum(grad_act_head * norm_head, axis=0),
                jnp.sum(grad_act_head, axis=0),
                jnp.full((channels,), loss_part),
            ]
        )
    )
    grad_gain_head, grad_bias_head, swav_loss = sums_back[0], sums_back[1], sums_back[2, 0]
    grad_pre_head = (
        gain_head
        * spread_head
        * (grad_act_head - (grad_bias_head + norm_head * grad_gain_head) / total_crops)
    )
    grad_pooled = split_dot(grad_pre_head, full_hidden, 1, 2)
    per_pixel = grad_pooled / crop_count
    scale_rows = lax.all_gather(per_pixel, "rows", axis=0, tiled=True)

    crop_index = lax.axis_index("crops")
    forward_all, backward_all = gather_products(
        jnp.concatenate([pooled, hidden_head, unit_embed], axis=1),
        jnp.concatenate([grad_pre_head, grad_embedding, grad_scores], axis=1),
    )
    shard_hidden, shard_embed = w_hidden.shape[0], w_embed.shape[0]
    score_at = hidden_cols + w_embed.shape[1]
    pooled_part = lax.dynamic_slice_in_dim(forward_all, crop_index * shard_hidden, shard_hidden, 1)
    hidden_part = lax.dynamic_slice_in_dim(
        forward_all, channels + crop_index * shard_embed, shard_embed, 1
    )
    out_hidden = jnp.dot(pooled_part.T, backward_all[:, :hidden_cols], preferred_element_type=F32)
    out_embed = jnp.dot(hidden_part.T, backward_all[:, hidden_cols:score_at], preferred_element_type=F32)
    grad_prototypes = jnp.dot(
        forward_all[:, channels + hidden_cols :].T, backward_all[:, score_at:], preferred_element_type=F32
    )

    sums_three_back = jnp.concatenate(
        [jnp.sum(scale_rows * slope_sums, axis=0), jnp.sum(scale_rows * slope_dots, axis=0)]
    )
    sums_three_back = total_wide(after(sums_three_back, forward_all)[None])[0]
    grad_bias_three = sums_three_back[:channels]
    alpha, beta, gamma, grad_gain_three = back_consts(
        gain_three, mean_three, spread_three, valid_count, grad_bias_three, sums_three_back[channels:]
    )
    grad_w_expand, total_three, grad_act_two, sum_back, dot_back = third_back(
        hidden_two,
        full_expand,
        slope_three,
        weight_col,
        scale_rows * alpha,
        beta,
        gamma,
        slope_two,
        pre_two,
        hidden_mean_two,
    )
    expand_stages = reduce_stages(grad_w_expand)
    sums_two_back = total_narrow(jnp.stack([sum_back, dot_back]))
    grad_bias_two = sums_two_back[0]
    alpha, beta, gamma, grad_gain_two = back_consts(
        gain_two, mean_two, spread_two, valid_count, grad_bias_two, sums_two_back[1]
    )
    alpha = after(alpha, next(expand_stages))
    grad_pre_two, total_two = second_back(grad_act_two, pre_two, mask_planes, alpha, beta, gamma)
    above_two, below_two = edge_rows(grad_pre_two)
    part_one = conv_local(grad_pre_two, full_spatial, True)
    grad_w_spatial = spatial_grad(
        hidden_one,
        above_one,
        below_one,
        grad_pre_two,
        hidden_mean_one,
        after(total_two, next(expand_stages), part_one),
    )
    spatial_stages = reduce_stages(grad_w_spatial)
    grad_act_one, sum_back, dot_back = conv_back_halo(
        part_one, after(above_two, next(expand_stages)), below_two, full_spatial, slope_one, pre_one
    )
    next(spatial_stages)
    sums_one_back = total_narrow(jnp.stack([sum_back, dot_back]))
    grad_bias_one = sums_one_back[0]
    alpha, beta, gamma, grad_gain_one = back_consts(
        gain_one, mean_one, spread_one, valid_count, grad_bias_one, sums_one_back[1]
    )
    out_expand = next(expand_stages)
    grad_pre_one = first_back(grad_act_one, pre_one, weight_col, alpha, beta, gamma)
    grad_w_reduce = lax.dot_general(
        flat_in, after(grad_pre_one, next(spatial_stages)), TN, preferred_element_type=F32
    ).astype(BF16)
    *_, out_reduce = reduce_stages(grad_w_reduce)
    *_, out_spatial = spatial_stages
    grad_features = last_grads(
        grad_pre_one, full_reduce, slope_three, scale_rows, height
    ).reshape(features.shape)

    totals = total_wide(jnp.concatenate([total_three, total_two])[None])[0]
    tap_means = jnp.tile(hidden_mean_one, 9)
    shard_expand, shard_spatial = w_expand.shape[0], w_spatial.shape[0]
    means = lax.dynamic_slice_in_dim(hidden_mean_two, crop_index * shard_expand, shard_expand)
    out_expand = out_expand + means[:, None] * totals[:channels]
    means = lax.dynamic_slice_in_dim(tap_means, crop_index * shard_spatial, shard_spatial)
    out_spatial = out_spatial + means[:, None] * totals[channels:]
    return (
        swav_loss,
        grad_features,
        out_reduce,
        out_spatial,
        out_expand,
        out_hidden,
        out_embed,
        grad_prototypes,
        grad_gain_one,
        grad_bias_one,
        grad_gain_two,
        grad_bias_two,
        grad_gain_three,
        grad_bias_three,
        grad_gain_head,
        grad_bias_head,
    )


def solution(mesh):
    split = P("crops", None)
    map_spec = P("crops", "rows", None, None)
    in_specs = (
        (map_spec, P("crops", "rows", None), P("crops"), P(BOTH, None)) + (split,) * 5 + (P(),) * 9
    )
    out_specs = (P(), map_spec) + (split,) * 5 + (P(),) * 9
    return jax.shard_map(shards, mesh=mesh, in_specs=in_specs, out_specs=out_specs, check_vma=False)
```

time: 1610 us -> 593 us (0.37)
  waiting for transfers between devices: 772 us -> 123 us
  blocking collectives: 526 us -> 50.2 us
  Pallas kernels: 0 us -> 114 us
  starting transfers between devices: 19.2 us -> 132 us
  matrix products: 128 us -> 48 us
  other arithmetic: 95 us -> 43.4 us
    reduce_scatter x5 -> x0, waiting for transfers between devices: 505 us -> none  [the longest x1 285 us: shards(): lax.psum_scatter(grad_w_hidden, 'crops', scatter_dimension=0, tiled=True)]
    psum x11 -> x0, blocking collectives: 452 us -> none  [the longest x4 175 us: moments(): lax.psum((first_sum, second_sum, jnp.sum(weights)), ('crops', 'rows'))]
    psum x2 -> x0, waiting for transfers between devices: 221 us -> none  [the longest x1 128 us: shards(): lax.psum((jnp.sum(grad_act_head * norm_head, axis=0), jnp.sum(grad_act_he...]
    pallas_call x0 -> x12, Pallas kernels: none -> 114 us  [kernel_call(): pl.pallas_call(body, grid=(grid,), in_specs=ins, out_specs=[spec for _, s...]
    dot_general x18 -> x12, matrix products: 127 us -> 47 us  [the longest x4 13.8 us: split_dot(): lax.dot_general(split_parts(x, parts), matrix, (((1,), (dim,)), ((), ()))...]
    ppermute x4 -> x72, starting transfers between devices: 13.7 us -> 92 us  [the longest x68 80.1 us: xor_permute(): return lax.ppermute(values, BOTH, pairs)]
    all_to_all x0 -> x10, waiting for transfers between devices: none -> 70.7 us  [the longest x6 35.4 us: swap_sum(): lax.all_to_all(values, BOTH, 0, 0, axis_index_groups=list(groups.values()...]
    ppermute x4 -> x72, waiting for transfers between devices: 0.71 us -> 52 us  [the longest x68 44.5 us: xor_permute(): return lax.ppermute(values, BOTH, pairs)]
  transfers between devices with their start and end apart: 16 -> 86, of which waited for: 8 -> 53; matrix products, arithmetic and copies ran while one was open for 14% -> 22% of each run, Pallas kernels for 0% -> 20%
where the time goes in v1:
time: 593 us; the launch traced here: 583 us
  starting transfers between devices  132 us (22%)
  waiting for transfers between devices  123 us (21%)
  Pallas kernels  114 us (19%)
  local copies, waits for them, and re-layouts  55.5 us (9%)
  blocking collectives  50.2 us (8%)
  matrix products  48 us (8%)
  other arithmetic  43.4 us (7%)
  between operations  16.8 us (3%)
    pallas_call x12, Pallas kernels, kernel_call(): pl.pallas_call(body, grid=(grid,), in_specs=ins, out_specs=[spec for _, s...  114 us
    ppermute x68, starting transfers between devices, xor_permute(): return lax.ppermute(values, BOTH, pairs)  80.1 us
    ppermute x68, waiting for transfers between devices, xor_permute(): return lax.ppermute(values, BOTH, pairs)  44.5 us
    all_to_all x1, blocking collectives, gather_first(): lax.all_to_all(jnp.broadcast_to(mine[None], (crop_total, size, cols)), 'c...  38.5 us
    all_to_all x6, waiting for transfers between devices, swap_sum(): lax.all_to_all(values, BOTH, 0, 0, axis_index_groups=list(groups.values()...  35.4 us
    all_to_all x4, waiting for transfers between devices, total_narrow(): return jnp.sum(lax.all_to_all(copies, BOTH, 0, 0, tiled=True), axis=0)  35.3 us
    all_to_all x6, starting transfers between devices, swap_sum(): lax.all_to_all(values, BOTH, 0, 0, axis_index_groups=list(groups.values()...  22 us
    all_to_all x4, starting transfers between devices, total_narrow(): return jnp.sum(lax.all_to_all(copies, BOTH, 0, 0, tiled=True), axis=0)  17.6 us
  transfers between devices with their start and end apart: 86, of which 53 were waited for; matrix products, arithmetic and copies ran while one was open for 22% of the time, Pallas kernels for 20%

profile of v1, /device:TPU:1, one launch (start us, length us, event | category | flops | bytes accessed | tf_op | source)
XLA Modules:
  0.0 582.8 jit_solution(14393236866583650368)
XLA Ops:
  12.6 38.5 %all_to_all.55 = bf16[8,128,512]{2,1,0:T(8,128)(2,1)S(1)} all-to-all(bf16[8,128,512]{2,1,0:T(8,128)(2,1)S(1)} %broadcast_in_dim.58), channel_id=1, replica_groups=mesh['crops'=8,'rows'=4] {'crops'}, dimensions={0} | all-to-all | bytes 2097152 | tf_op jit(solution)/shard_map/all_to_all | solution.py:171
  59.4 7.8 %multiply_reduce_fusion = (f32[512]{0:T(512)S(1)}, f32[512]{0:T(512)S(1)}, f32[1280,512]{0,1:T(8,128)}) fusion(f32[1280]{0:T(1024)S(1)} %convert_element_type.177, bf16[2048,512]{1,0:T(8,128)(2,1)S(1)} %bitcast.182, bf16[1280,2048]{1,0:T(8,128)(2,1)} %bitcast.281), kind=kOutput, calls=%fused_computation.11 | convolution fusion | flops 2686974976 | bytes 9970688 | tf_op jit(solution)/shard_map/dot_general | solution.py:984
  76.2 11.0 %all-to-all-done.1 = f32[32,3,512]{2,1,0:T(4,128)S(1)} async-done(((f32[32,3,512]{2,1,0:T(4,128)}), f32[32,3,512]{2,1,0:T(4,128)S(1)}, u32[]{:S(2)}, u32[]{:S(2)}) %all-to-all-start.1) | async-done | bytes 196640 | tf_op jit(solution)/shard_map/all_to_all | solution.py:94
  89.7 5.9 %shard_map.297 = (bf16[2,640,512]{2,1,0:T(8,128)(2,1)}, f32[2,640,512]{2,1,0:T(8,128)}, f32[8,512]{1,0:T(8,128)S(1)}) custom-call(f32[80,2,8,512]{3,2,1,0:T(8,128)} %bitcast.173, f32[2,640,1]{2,1,0:T(8,128)S(1)} %convert_element_type.238.m_ref, f32[32,512]{1,0:T(8,128)S(1)} %pad_maximum_fusion.13.c_ref), custom_call_target="tpu_custom_call" | custom-call | flops 26214400 | bytes 6640640 | tf_op jit(solution)/shard_map/pallas_call | solution.py:251
  103.7 8.8 %shard_map.298.part_ref = f32[2,640,512]{2,1,0:T(8,128)} custom-call(bf16[2,640,512]{2,1,0:T(8,128)(2,1)S(1)} %copy-done.5, bf16[32,208,512]{2,1,0:T(8,128)(2,1)} %bitcast.176), custom_call_target="tpu_custom_call" | custom-call | flops 4026531840 | bytes 10747904 | tf_op jit(solution)/shard_map/pallas_call | solution.py:251
  116.3 8.9 %shard_map.299 = (f32[2,640,512]{2,1,0:T(8,128)}, f32[8,512]{1,0:T(8,128)S(1)}, f32[8,512]{1,0:T(8,128)S(1)}) custom-call(f32[2,640,512]{2,1,0:T(8,128)} %shard_map.298.part_ref, bf16[640,512]{1,0:T(8,128)(2,1)} %collective-permute-done.1.above_ref, bf16[640,512]{1,0:T(8,128)(2,1)} %collective-permute-done.2.below_ref, bf16[32,208,512]{2,1,0:T(8,128)(2,1)} %bitcast.177, ...), custom_call_target="tpu_custom_call" | custom-call | flops 2013265920 | bytes 13407232 | tf_op jit(solution)/shard_map/pallas_call | solution.py:251
  134.2 10.6 %all-to-all-done.2 = f32[32,3,512]{2,1,0:T(4,128)S(1)} async-done(((f32[32,3,512]{2,1,0:T(4,128)}), f32[32,3,512]{2,1,0:T(4,128)S(1)}, u32[]{:S(2)}, u32[]{:S(2)}) %all-to-all-start.2) | async-done | bytes 196640 | tf_op jit(solution)/shard_map/all_to_all | solution.py:94
  146.6 8.6 %shard_map.300 = (bf16[1280,512]{1,0:T(8,128)(2,1)}, f32[2,640,512]{2,1,0:T(8,128)}, f32[8,2048]{1,0:T(8,128)S(1)}, f32[8,2048]{1,0:T(8,128)S(1)}, f32[8,512]{1,0:T(8,128)S(1)}) custom-call(f32[2,640,512]{2,1,0:T(8,128)} %get-tuple-element.47.x_ref, f32[1280,1]{1,0:T(8,128)S(1)} %convert_element_type.239.m_ref, f32[32,512]{1,0:T(8,128)S(1)} %pad_maximum_fusion.14.c_ref, ...), custom_call_target="tpu_custom_call" | custom-call | flops 2684354560 | bytes 8868864 | tf_op jit(solution)/shard_map/pallas_call | solution.py:251
  170.8 16.9 %shard_map.301 = (bf16[1280,2048]{1,0:T(8,128)(2,1)}, f32[80,2048]{1,0:T(8,128)S(1)}, f32[80,2048]{1,0:T(8,128)S(1)}, f32[80,2048]{1,0:T(8,128)}) custom-call(bf16[1280,512]{1,0:T(8,128)(2,1)} %get-tuple-element.51.h_ref, bf16[4,512,512]{2,1,0:T(8,128)(2,1)} %bitcast.196, bf16[1280,2048]{1,0:T(8,128)(2,1)} %bitcast.282, f32[1280,1]{1,0:T(8,128)} %copy-done.3, ...), custom_call_target="tpu_custom_call" | custom-call | flops 2789212160 | bytes 16126976 | tf_op jit(solution)/shard_map/pallas_call | solution.py:251
  196.6 5.8 %collective-permute-done.11 = f32[20,2176]{1,0:T(8,128)S(1)} collective-permute-done((f32[20,2176]{1,0:T(8,128)S(1)}, f32[20,2176]{1,0:T(8,128)S(1)}, u32[]{:S(2)}, u32[]{:S(2)}) %collective-permute-start.11) | collective-permute-done | bytes 174112 | tf_op jit(solution)/shard_map/ppermute | solution.py:34
  306.9 6.2 %fusion = f32[40,2048]{1,0:T(8,128)S(1)} fusion(bf16[2048,2176]{1,0:T(8,128)(2,1)} %all-gather.7.cloned.1.call-done, bf16[20,2048]{1,0:T(8,128)(2,1)S(1)} %fusion.39, bf16[20,2048]{1,0:T(8,128)(2,1)S(1)} %get-tuple-element.101), kind=kOutput, calls=%fused_computation.1 | convolution fusion | flops 335872000 | bytes 8880128 | tf_op jit(solution)/shard_map/dot_general | solution.py:232
  313.3 11.8 %all-gather.1 = f32[4,20,2048]{2,1,0:T(8,128)S(1)} all-gather(f32[1,20,2048]{2,1,0:T(8,128)S(1)} %fusion.43), channel_id=1, replica_groups=mesh['crops'=8,'rows'=4] {'rows'}, dimensions={0}, use_global_device_ids=true | all-gather | bytes 819200 | tf_op jit(solution)/shard_map/all_gather | solution.py:1098
  338.9 15.5 %shard_map.302 = (bf16[512,2048]{1,0:T(8,128)(2,1)}, f32[8,2048]{1,0:T(8,128)S(1)}, f32[2,640,512]{2,1,0:T(8,128)}, f32[8,512]{1,0:T(8,128)S(1)}, f32[8,512]{1,0:T(8,128)S(1)}) custom-call(bf16[1280,512]{1,0:T(8,128)(2,1)} %get-tuple-element.51.h_ref, bf16[4,512,512]{2,1,0:T(8,128)(2,1)} %bitcast.197, bf16[1280,2048]{1,0:T(8,128)(2,1)} %get-tuple-element.56.d_ref, ...), custom_call_target="tpu_custom_call" | custom-call | flops 8053063680 | bytes 19635200 | tf_op jit(solution)/shard_map/pallas_call | solution.py:251
  363.0 10.2 %all-to-all-done.3 = f32[32,2,512]{2,1,0:T(2,128)S(1)} async-done(((f32[32,2,512]{2,1,0:T(2,128)}), f32[32,2,512]{2,1,0:T(2,128)S(1)}, u32[]{:S(2)}, u32[]{:S(2)}) %all-to-all-start.3) | async-done | bytes 131104 | tf_op jit(solution)/shard_map/all_to_all | solution.py:94
  381.1 5.3 shard_map.303
  387.7 8.9 %shard_map.304.part_ref = f32[2,640,512]{2,1,0:T(8,128)} custom-call(bf16[2,640,512]{2,1,0:T(8,128)(2,1)S(1)} %copy-done.6, bf16[32,208,512]{2,1,0:T(8,128)(2,1)} %bitcast.179), custom_call_target="tpu_custom_call" | custom-call | flops 4026531840 | bytes 10747904 | tf_op jit(solution)/shard_map/pallas_call | solution.py:251
  397.5 13.1 %shard_map.308 = bf16[3,3,512,512]{3,2,1,0:T(8,128)(2,1)} custom-call(bf16[2,640,512]{2,1,0:T(8,128)(2,1)} %get-tuple-element.46.x_ref, bf16[640,512]{1,0:T(8,128)(2,1)} %collective-permute-done.1.above_ref, bf16[640,512]{1,0:T(8,128)(2,1)} %collective-permute-done.2.below_ref, bf16[2,640,512]{2,1,0:T(8,128)(2,1)} %get-tuple-element.66.x_ref.g_ref, ...), custom_call_target="tpu_custom_call" | custom-call | flops 6039797760 | bytes 8654848 | tf_op jit(solution)/shard_map/pallas_call | solution.py:251
  442.5 8.4 %shard_map.305 = (f32[2,640,512]{2,1,0:T(8,128)}, f32[8,512]{1,0:T(8,128)S(1)}, f32[8,512]{1,0:T(8,128)S(1)}) custom-call(f32[2,640,512]{2,1,0:T(8,128)} %shard_map.304.part_ref, bf16[640,512]{1,0:T(8,128)(2,1)S(1)} %collective-permute-done.55.above_ref, bf16[640,512]{1,0:T(8,128)(2,1)S(1)} %collective-permute-done.56.below_ref, ...), custom_call_target="tpu_custom_call" | custom-call | flops 2013265920 | bytes 18644992 | tf_op jit(solution)/shard_map/pallas_call | solution.py:251
  451.7 5.7 all-to-all-start.6
  477.3 20.6 %all-to-all-done.7 = bf16[4,2,2,144,512]{4,3,2,1,0:T(8,128)(2,1)} async-done(((bf16[4,2,2,144,512]{4,3,2,1,0:T(8,128)(2,1)}), bf16[4,2,2,144,512]{4,3,2,1,0:T(8,128)(2,1)}, u32[]{:S(2)}, u32[]{:S(2)}) %all-to-all-start.7) | async-done | bytes 2359328 | tf_op jit(solution)/shard_map/all_to_all | solution.py:130
  500.8 6.6 %fusion.12 = bf16[2048,512]{0,1:T(8,128)(2,1)} fusion(bf16[1280,512]{1,0:T(8,128)(2,1)S(1)} %copy-done.2, bf16[1280,2048]{1,0:T(8,128)(2,1)} %bitcast.283), kind=kOutput, calls=%fused_computation.21 | convolution fusion | flops 2685403136 | bytes 8650752 | tf_op jit(solution)/shard_map/dot_general | solution.py:1167
  519.3 8.4 %shard_map.307 = bf16[1280,2048]{1,0:T(8,128)(2,1)} custom-call(bf16[1280,512]{1,0:T(8,128)(2,1)S(1)} %copy-done.2, bf16[2048,512]{1,0:T(8,128)(2,1)} %bitcast.183, bf16[1280,2048]{1,0:T(8,128)(2,1)} %get-tuple-element.56.d_ref, f32[80,2048]{1,0:T(8,128)S(1)} %reshape.399.s_ref), custom_call_target="tpu_custom_call" | custom-call | flops 2684354560 | bytes 14548992 | tf_op jit(solution)/shard_map/pallas_call | solution.py:251
  527.6 6.6 %all-to-all-done.10 = bf16[4,144,512]{2,1,0:T(8,128)(2,1)S(1)} async-done(((bf16[4,144,512]{2,1,0:T(8,128)(2,1)}), bf16[4,144,512]{2,1,0:T(8,128)(2,1)S(1)}, u32[]{:S(2)}, u32[]{:S(2)}) %all-to-all-start.10) | async-done | bytes 589856 | tf_op jit(solution)/shard_map/all_to_all | solution.py:130
  542.1 5.5 fusion.4
  (554 shorter events, 310.3 us)
Async XLA Ops:
  7.2 96.5 %all-gather.13.cloned.1.call-start = ((), (), s32[]{:S(2)}) async-start(), calls=%async_computation.14 | async-start | bytes 7028736 | tf_op jit(solution)/shard_map/all_gather | solution.py:186
  10.0 193.2 %all-gather.7.cloned.1.call-start = ((), (), s32[]{:S(2)}) async-start(), calls=%async_computation.11 | async-start | bytes 9191424 | tf_op jit(solution)/shard_map/all_gather | solution.py:972
  68.0 19.3 %all-to-all-start.1 = ((f32[32,3,512]{2,1,0:T(4,128)}), f32[32,3,512]{2,1,0:T(4,128)S(1)}, u32[]{:S(2)}, u32[]{:S(2)}) async-start(f32[32,3,512]{2,1,0:T(4,128)} %broadcast_in_dim.59), calls=%async_computation.1 | async-start | bytes 524288 | tf_op jit(solution)/shard_map/all_to_all | solution.py:94
  98.1 14.4 %collective-permute-start.1 = (bf16[640,512]{1,0:T(8,128)(2,1)}, bf16[640,512]{1,0:T(8,128)(2,1)}, u32[]{:S(2)}, u32[]{:S(2)}) collective-permute-start(bf16[640,512]{1,0:T(8,128)(2,1)} %get-tuple-element.130), channel_id=1, source_target_pairs={{0,1},{1,2},{2,3},{4,5},{5,6},{6,7},{8,9},{9,10},{10,11},{12,13},{... | collective-permute-start | bytes 1966088 | tf_op jit(solution)/shard_map/ppermute | solution.py:931
  101.7 14.5 %collective-permute-start.2 = (bf16[640,512]{1,0:T(8,128)(2,1)}, bf16[640,512]{1,0:T(8,128)(2,1)}, u32[]{:S(2)}, u32[]{:S(2)}) collective-permute-start(bf16[640,512]{1,0:T(8,128)(2,1)} %get-tuple-element.129), channel_id=1, source_target_pairs={{1,0},{2,1},{3,2},{5,4},{6,5},{7,6},{9,8},{10,9},{11,10},{13,12},{... | collective-permute-start | bytes 1966088 | tf_op jit(solution)/shard_map/ppermute | solution.py:932
  126.0 18.8 %all-to-all-start.2 = ((f32[32,3,512]{2,1,0:T(4,128)}), f32[32,3,512]{2,1,0:T(4,128)S(1)}, u32[]{:S(2)}, u32[]{:S(2)}) async-start(f32[32,3,512]{2,1,0:T(4,128)} %broadcast_in_dim.64), calls=%async_computation.2 | async-start | bytes 524288 | tf_op jit(solution)/shard_map/all_to_all | solution.py:94
  130.3 196.3 %all-gather.9.cloned.1.call-start = ((), (), s32[]{:S(2)}) async-start(), calls=%async_computation.12 | async-start | bytes 6690816 | tf_op jit(solution)/shard_map/all_gather | solution.py:202
  239.9 302.2 %all-gather.11.cloned.1.call-start = ((), (), s32[]{:S(2)}) async-start(), calls=%async_computation.13 | async-start | bytes 8312832 | tf_op jit(solution)/shard_map/all_gather | solution.py:203
  355.7 17.6 %collective-permute-start.54 = (bf16[2,2,2,2,16,2048]{5,4,3,2,1,0:T(8,128)(2,1)S(1)}, bf16[2,2,2,2,16,2048]{5,4,3,2,1,0:T(8,128)(2,1)}, u32[]{:S(2)}, u32[]{:S(2)}) collective-permute-start(bf16[2,2,2,2,16,2048]{5,4,3,2,1,0:T(8,128)(2,1)S(1)} %dynamic-slice_bitcast_fusion.2), channel_id=1, source_target_pairs={{0,1},{1,0},{2,3},{3,2},{4,5},{5,4},{6,7},{7,6},{8,9},{9,8},{10,11... | collective-permute-start | bytes 3145736 | tf_op jit(solution)/shard_map/ppermute | solution.py:34
  359.5 13.7 %all-to-all-start.3 = ((f32[32,2,512]{2,1,0:T(2,128)}), f32[32,2,512]{2,1,0:T(2,128)S(1)}, u32[]{:S(2)}, u32[]{:S(2)}) async-start(f32[32,2,512]{2,1,0:T(2,128)} %broadcast_in_dim.78), calls=%async_computation.3 | async-start | bytes 262144 | tf_op jit(solution)/shard_map/all_to_all | solution.py:94
  376.3 20.3 %all-to-all-start.4 = ((bf16[4,2,2,16,2048]{4,3,2,1,0:T(8,128)(2,1)}), bf16[4,2,2,16,2048]{4,3,2,1,0:T(8,128)(2,1)S(1)}, u32[]{:S(2)}, u32[]{:S(2)}) async-start(bf16[4,2,2,16,2048]{4,3,2,1,0:T(8,128)(2,1)} %bitcast.190), calls=%async_computation.4 | async-start | bytes 2097152 | tf_op jit(solution)/shard_map/all_to_all | solution.py:130
  413.9 43.5 %collective-permute-start.57 = (bf16[2,2,2,2,144,512]{5,4,3,2,1,0:T(8,128)(2,1)}, bf16[2,2,2,2,144,512]{5,4,3,2,1,0:T(8,128)(2,1)}, u32[]{:S(2)}, u32[]{:S(2)}) collective-permute-start(bf16[2,2,2,2,144,512]{5,4,3,2,1,0:T(8,128)(2,1)} %dynamic-slice_bitcast_fusion), channel_id=1, source_target_pairs={{0,1},{1,0},{2,3},{3,2},{4,5},{5,4},{6,7},{7,6},{8,9},{9,8},{10,11... | collective-permute-start | bytes 7077896 | tf_op jit(solution)/shard_map/ppermute | solution.py:34
  422.5 16.1 %collective-permute-start.55 = (bf16[640,512]{1,0:T(8,128)(2,1)}, bf16[640,512]{1,0:T(8,128)(2,1)S(1)}, u32[]{:S(2)}, u32[]{:S(2)}) collective-permute-start(bf16[640,512]{1,0:T(8,128)(2,1)} %get-tuple-element.128), channel_id=1, source_target_pairs={{0,1},{1,2},{2,3},{4,5},{5,6},{6,7},{8,9},{9,10},{10,11},{12,13},{... | collective-permute-start | bytes 1966088 | tf_op jit(solution)/shard_map/ppermute | solution.py:931
  432.4 37.9 %collective-permute-start.68 = (f32[1,2560]{1,0:T(1,128)S(1)}, f32[1,2560]{1,0:T(1,128)S(1)}, u32[]{:S(2)}, u32[]{:S(2)}) collective-permute-start(f32[1,2560]{1,0:T(1,128)S(1)} %add_add_fusion.11), channel_id=1, source_target_pairs={{0,16},{1,17},{2,18},{3,19},{4,20},{5,21},{6,22},{7,23},{8,24},{9,... | collective-permute-start | bytes 30728 | tf_op jit(solution)/shard_map/ppermute | solution.py:34
  434.7 35.5 %collective-permute-start.69 = (f32[1,2560]{1,0:T(1,128)S(1)}, f32[1,2560]{1,0:T(1,128)S(1)}, u32[]{:S(2)}, u32[]{:S(2)}) collective-permute-start(f32[1,2560]{1,0:T(1,128)S(1)} %add_add_fusion.11), channel_id=1, source_target_pairs={{0,24},{1,25},{2,26},{3,27},{4,28},{5,29},{6,30},{7,31},{8,16},{9,... | collective-permute-start | bytes 30728 | tf_op jit(solution)/shard_map/ppermute | solution.py:34
  438.6 31.7 %collective-permute-start.67 = (f32[1,2560]{1,0:T(1,128)S(1)}, f32[1,2560]{1,0:T(1,128)S(1)}, u32[]{:S(2)}, u32[]{:S(2)}) collective-permute-start(f32[1,2560]{1,0:T(1,128)S(1)} %add_add_fusion.11), channel_id=1, source_target_pairs={{0,8},{1,9},{2,10},{3,11},{4,12},{5,13},{6,14},{7,15},{8,0},{9,1},... | collective-permute-start | bytes 30728 | tf_op jit(solution)/shard_map/ppermute | solution.py:34
  442.5 27.8 %collective-permute-start.70 = (bf16[16,2048]{1,0:T(8,128)(2,1)S(1)}, bf16[16,2048]{1,0:T(8,128)(2,1)S(1)}, u32[]{:S(2)}, u32[]{:S(2)}) collective-permute-start(bf16[16,2048]{1,0:T(8,128)(2,1)S(1)} %convert_reduce_fusion.2), channel_id=1, source_target_pairs={{0,2},{1,3},{2,0},{3,1},{4,6},{5,7},{6,4},{7,5},{8,10},{9,11},{10,... | collective-permute-start | bytes 196616 | tf_op jit(solution)/shard_map/ppermute | solution.py:34
  451.7 13.9 %all-to-all-start.6 = ((f32[32,2,512]{2,1,0:T(2,128)}), f32[32,2,512]{2,1,0:T(2,128)S(1)}, u32[]{:S(2)}, u32[]{:S(2)}) async-start(f32[32,2,512]{2,1,0:T(2,128)} %broadcast_in_dim.81), calls=%async_computation.6 | async-start | bytes 262144 | tf_op jit(solution)/shard_map/all_to_all | solution.py:94
  465.6 32.2 %all-to-all-start.7 = ((bf16[4,2,2,144,512]{4,3,2,1,0:T(8,128)(2,1)}), bf16[4,2,2,144,512]{4,3,2,1,0:T(8,128)(2,1)}, u32[]{:S(2)}, u32[]{:S(2)}) async-start(bf16[4,2,2,144,512]{4,3,2,1,0:T(8,128)(2,1)} %bitcast.181), calls=%async_computation.7 | async-start | bytes 4718592 | tf_op jit(solution)/shard_map/all_to_all | solution.py:130
  470.4 44.4 %collective-permute-start.71 = (bf16[2,16,2048]{2,1,0:T(8,128)(2,1)S(1)}, bf16[2,16,2048]{2,1,0:T(8,128)(2,1)S(1)}, u32[]{:S(2)}, u32[]{:S(2)}) collective-permute-start(bf16[2,16,2048]{2,1,0:T(8,128)(2,1)S(1)} %pad_maximum_fusion.10), channel_id=1, source_target_pairs={{0,1},{1,0},{2,3},{3,2},{4,5},{5,4},{6,7},{7,6},{8,9},{9,8},{10,11... | collective-permute-start | bytes 393224 | tf_op jit(solution)/shard_map/ppermute | solution.py:34
  513.6 22.0 %collective-permute-start.58 = (bf16[2,2,2,2,64,512]{5,4,3,2,1,0:T(8,128)(2,1)}, bf16[2,2,2,2,64,512]{5,4,3,2,1,0:T(8,128)(2,1)}, u32[]{:S(2)}, u32[]{:S(2)}) collective-permute-start(bf16[2,2,2,2,64,512]{5,4,3,2,1,0:T(8,128)(2,1)} %dynamic-slice_bitcast_fusion.1), channel_id=1, source_target_pairs={{0,1},{1,0},{2,3},{3,2},{4,5},{5,4},{6,7},{7,6},{8,9},{9,8},{10,11... | collective-permute-start | bytes 3145736 | tf_op jit(solution)/shard_map/ppermute | solution.py:34
  514.8 19.5 %all-to-all-start.10 = ((bf16[4,144,512]{2,1,0:T(8,128)(2,1)}), bf16[4,144,512]{2,1,0:T(8,128)(2,1)S(1)}, u32[]{:S(2)}, u32[]{:S(2)}) async-start(bf16[4,144,512]{2,1,0:T(8,128)(2,1)} %bitcast.89), calls=%async_computation.10 | async-start | bytes 1179648 | tf_op jit(solution)/shard_map/all_to_all | solution.py:130
  538.5 16.6 %all-to-all-start.8 = ((bf16[4,2,2,64,512]{4,3,2,1,0:T(8,128)(2,1)}), bf16[4,2,2,64,512]{4,3,2,1,0:T(8,128)(2,1)S(1)}, u32[]{:S(2)}, u32[]{:S(2)}) async-start(bf16[4,2,2,64,512]{4,3,2,1,0:T(8,128)(2,1)} %copy.170), calls=%async_computation.8 | async-start | bytes 2097152 | tf_op jit(solution)/shard_map/all_to_all | solution.py:130
  547.7 13.8 %collective-permute-start.62 = (bf16[2,144,512]{2,1,0:T(8,128)(2,1)S(1)}, bf16[2,144,512]{2,1,0:T(8,128)(2,1)S(1)}, u32[]{:S(2)}, u32[]{:S(2)}) collective-permute-start(bf16[2,144,512]{2,1,0:T(8,128)(2,1)S(1)} %pad_maximum_fusion.4), channel_id=1, source_target_pairs={{0,1},{1,0},{2,3},{3,2},{4,5},{5,4},{6,7},{7,6},{8,9},{9,8},{10,11... | collective-permute-start | bytes 884744 | tf_op jit(solution)/shard_map/ppermute | solution.py:34
  (136 other events, 1099.6 us)
Sparse Core Ops, SparseCore 0:
  11.4 82.0 all-gather.12
  97.0 84.1 all-gather.6
  240.0 72.6 all-gather.8
  316.1 76.0 all-gather.10

commit v2 on v1

--- a/solution.py
+++ b/solution.py
@@ -1,4 +1,5 @@
 import functools
+import itertools
 import math
 
 import jax
@@ -84,10 +85,6 @@
     return values, stacked.reshape(-1, rows_extra.shape[1])
 
 
-def after(values, *earlier):
-    return lax.optimization_barrier((values,) + earlier)[0]
-
-
 def total_narrow(values):
     count = lax.axis_size("crops") * lax.axis_size("rows")
     copies = jnp.broadcast_to(values[None], (count,) + values.shape)
@@ -114,23 +111,6 @@
     other = xor_permute(values, *step)
     low = my_bit(step) == 0
     return jnp.stack([jnp.where(low, values, other), jnp.where(low, other, values)])
-
-
-def swap_sum(values, dims, bits):
-    crop_total, row_total = lax.axis_size("crops"), lax.axis_size("rows")
-    crop_mask, row_mask = sum(b for b, _ in bits), sum(b for _, b in bits)
-    groups = {}
-    for c in range(crop_total):
-        for r in range(row_total):
-            groups.setdefault((c & ~crop_mask, r & ~row_mask), []).append(c * row_total + r)
-    front = [k for k, step in enumerate(dims) if step in bits]
-    rest = [k for k in range(values.ndim) if k not in front]
-    values = values.transpose(front + rest)
-    values = values.reshape((2 ** len(bits),) + values.shape[len(bits) :]).astype(BF16)
-    values = lax.all_to_all(
-        values, BOTH, 0, 0, axis_index_groups=list(groups.values()), tiled=True
-    )
-    return jnp.sum(values.astype(F32), axis=0), [step for step in dims if step not in bits]
 
 
 def gather_rows(values):
@@ -141,21 +121,6 @@
         values = double(values, step)
     values = values.transpose(tuple(range(count - 1, -1, -1)) + (count, count + 1))
     return values.reshape(-1, cols)
-
-
-def reduce_stages(values):
-    row_bits = [(0, b) for b in reversed(bits_of("rows"))]
-    crop_bits = [(b, 0) for b in reversed(bits_of("crops"))]
-    dims = crop_bits + row_bits
-    rows, cols = values.shape
-    values = values.reshape((2,) * len(dims) + (rows >> len(dims), cols))
-    values = halve(values, len(dims) - 1, dims[-1], True)
-    yield values
-    values, dims = swap_sum(values, dims[:-1], row_bits[:-1] + crop_bits[-1:])
-    yield values
-    values, dims = swap_sum(values, dims, list(dims))
-    yield values
-    yield gather_rows(values.astype(BF16)).astype(F32)
 
 
 def row_quarter(weight):
@@ -191,19 +156,6 @@
     return (whole, size), second_blocks.reshape(blocks, -1, cols)
 
 
-def gather_products(left, right):
-    mean = jnp.mean(left, axis=0, keepdims=True)
-    total = jnp.sum(right, axis=0, keepdims=True)
-    mean_high, total_high = lax.reduce_precision(mean, 8, 7), lax.reduce_precision(total, 8, 7)
-    mean_low, total_low = mean - mean_high, total - total_high
-    left = jnp.concatenate([left - mean, mean_high, mean_high, mean_low, mean_low], axis=0)
-    right = jnp.concatenate([right, total_high, total_low, total_high, total_low], axis=0)
-    return (
-        lax.all_gather(left.astype(BF16), BOTH, axis=0, tiled=True),
-        lax.all_gather(right.astype(BF16), BOTH, axis=0, tiled=True),
-    )
-
-
 def spread_of(sums, count):
     mean = sums[0] / count
     return mean, lax.rsqrt(sums[1] / count - mean * mean + EPS_NORM)
@@ -244,14 +196,19 @@
 UNROLL = 16
 
 
-def kernel_call(body, grid, ins, outs, scratch, args, flops, transcendentals=0):
+def kernel_call(body, grid, ins, outs, scratch, args, flops, transcendentals=0, deps=()):
     moved = sum(a.size * a.dtype.itemsize for a in args) + sum(
         math.prod(s.shape) * s.dtype.itemsize for s, _ in outs
     )
+    count = len(ins)
+
+    def inner(*refs):
+        body(*refs[:count], *refs[count + len(deps) :])
+
     return pl.pallas_call(
-        body,
+        inner,
         grid=(grid,),
-        in_specs=ins,
+        in_specs=ins + [pl.BlockSpec(memory_space=pl.ANY)] * len(deps),
         out_specs=[spec for _, spec in outs],
         out_shape=[shape for shape, _ in outs],
         scratch_shapes=scratch,
@@ -259,7 +216,7 @@
         cost_estimate=pl.CostEstimate(
             flops=flops, bytes_accessed=moved, transcendentals=transcendentals
         ),
-    )(*args)
+    )(*args, *deps)
 
 
 def whole_block(array):
@@ -297,6 +254,14 @@
 
 def planes_of(height, width, rows):
     return pl.BlockSpec((height, rows, width), lambda k: (0, k, 0))
+
+
+def rows_block(rows, width):
+    return pl.BlockSpec((rows, width), lambda k: (k, 0))
+
+
+def plane_out(total, width, rows):
+    return jax.ShapeDtypeStruct((total, width), BF16), rows_block(rows, width)
 
 
 def gather_tile(ref, index, height):
@@ -319,7 +284,144 @@
     return pl.ds(pl.multiple_of(index * TILE, TILE), TILE)
 
 
-def first_body(height, x_ref, m_ref, c_ref, hidden_ref, slope_ref, sum_ref):
+def merge_body(counts, place_ref, *refs):
+    step = pl.program_id(0)
+    at, rows, totals = 0, 0, []
+    for count in counts:
+        total = refs[at][...].astype(F32)
+        for ref in refs[at + 1 : at + count]:
+            total = total + ref[...].astype(F32)
+        lead, _, inner, cols = total.shape
+        totals.append((rows, inner, total.astype(BF16).reshape(lead, inner, cols)))
+        at, rows = at + count, rows + inner
+    for k, out_ref in enumerate(refs[at:]):
+
+        @pl.when(step == k)
+        def _(out_ref=out_ref):
+            for first, inner, total in totals:
+                out_ref[:, first : first + inner, :] = total
+
+
+def merge_split(groups, place, deps):
+    lead, split, _, cols = groups[0][0].shape
+    counts = [len(parts) for parts in groups]
+    inner = sum(parts[0].shape[2] for parts in groups)
+    args = [part for parts in groups for part in parts]
+
+    def body(place_ref, *refs):
+        merge_body(counts, place_ref, *refs[: len(args)], *refs[len(args) + len(deps) :])
+
+    return pl.pallas_call(
+        body,
+        grid_spec=pltpu.PrefetchScalarGridSpec(
+            num_scalar_prefetch=1,
+            grid=(split,),
+            in_specs=[
+                pl.BlockSpec(
+                    (lead, 1, part.shape[2], cols), lambda k, at: (0, jnp.bitwise_xor(at[0], k), 0, 0)
+                )
+                for part in args
+            ]
+            + [pl.BlockSpec(memory_space=pl.ANY)] * len(deps),
+            out_specs=[pl.BlockSpec((lead, inner, cols), lambda k, at: (0, 0, 0))] * split,
+        ),
+        out_shape=[jax.ShapeDtypeStruct((lead, inner, cols), BF16)] * split,
+        compiler_params=pltpu.CompilerParams(vmem_limit_bytes=52 * 2**20),
+        cost_estimate=pl.CostEstimate(
+            flops=sum(a.size for a in args), bytes_accessed=3 * sum(a.size for a in args), transcendentals=0
+        ),
+    )(jnp.reshape(place, (1,)).astype(jnp.int32), *args, *deps)
+
+
+def reduce_steps():
+    row_bits = [(0, b) for b in reversed(bits_of("rows"))]
+    crop_bits = [(b, 0) for b in reversed(bits_of("crops"))]
+    return [row_bits[-1:], crop_bits[-1:] + row_bits[:-1], crop_bits[:-1]]
+
+
+def device_count():
+    return lax.axis_size("crops") * lax.axis_size("rows")
+
+
+def exchange(groups, bits, inner, deps=()):
+    split = 2 ** len(bits)
+    place = sum(my_bit(step) << k for k, step in enumerate(reversed(bits)))
+    groups = [[p.reshape(-1, split, n, p.shape[-1]) for p in parts] for parts, n in zip(groups, inner)]
+    pieces = merge_split(groups, place, deps)
+    parts = [pieces[0]]
+    for flips in range(1, split):
+        chosen = [step for k, step in enumerate(reversed(bits)) if flips >> k & 1]
+        parts.append(xor_permute(pieces[flips], sum(b for b, _ in chosen), sum(b for _, b in chosen)))
+    return parts
+
+
+def core_exchange(values, deps=()):
+    inner = values.shape[0] // device_count()
+    return exchange([[values]], reduce_steps()[0], [inner], deps)
+
+
+def near_exchange(groups, inner, deps=()):
+    return exchange(groups, reduce_steps()[1], inner, deps)
+
+
+def far_exchange(parts, deps=()):
+    return exchange([parts], reduce_steps()[2], [parts[0].shape[-2]], deps)
+
+
+def line_exchange(parts, inner):
+    _, near, far = reduce_steps()
+    return exchange([parts], far[-1:], [inner * 2 ** len(near)])
+
+
+def reduce_end(parts, deps=()):
+    (total,) = merge_split([[p[:, None] for p in parts]], jnp.int32(0), deps)
+    return gather_rows(total.reshape(total.shape[1:])).astype(F32)
+
+
+def pack_body(count, *refs):
+    *ins, out_ref, rows_ref = refs
+    at = 0
+    for k, ref in enumerate(ins):
+        share, width = ref.shape
+        cols = slice(at, at + width)
+        at += width
+        values = ref[...]
+        extra = jnp.sum(values, axis=0, keepdims=True)
+        if k < count:
+            extra = extra * (1.0 / share)
+            values = values - extra
+        high = extra.astype(BF16).astype(F32)
+        low = extra - high
+        rows_ref[:share, cols] = values
+        order = (high, high, low, low) if k < count else (high, low, high, low)
+        for j, row in enumerate(order):
+            rows_ref[share + j : share + j + 1, cols] = row
+    out_ref[...] = rows_ref[...].astype(BF16)
+
+
+def gather_products(left, right):
+    arrays = left + right
+    widths = [a.shape[1] for a in arrays]
+    rows = arrays[0].shape[0] + 4
+    (packed,) = kernel_call(
+        functools.partial(pack_body, len(left)),
+        1,
+        [whole_block(a) for a in arrays],
+        [
+            (
+                jax.ShapeDtypeStruct((rows, sum(widths)), BF16),
+                pl.BlockSpec((rows, sum(widths)), lambda k: (0, 0)),
+            )
+        ],
+        [pltpu.VMEM((rows, sum(widths)), F32)],
+        tuple(arrays),
+        6 * rows * sum(widths),
+    )
+    return lax.all_gather(packed, BOTH, axis=0, tiled=True)
+
+
+def first_body(height, x_ref, m_ref, c_ref, *refs):
+    hidden_refs, (slope_ref, sum_ref) = refs[:height], refs[height:]
     clear_first(sum_ref)
     pairs = x_ref.shape[0] // 2
     width = x_ref.shape[3]
@@ -330,19 +432,19 @@
             m = m_ref[i, tile_rows(k), :]
             value, slope = gelu_both(c_ref[:TILE] * x + c_ref[TILE:], m)
             hidden = value.astype(BF16)
-            hidden_ref[i, tile_rows(k), :] = hidden
+            hidden_refs[i][tile_rows(k), :] = hidden
             slope_ref[i, tile_rows(k), :] = slope
             return carry + fold(hidden.astype(F32))
 
         sum_ref[...] += loop(pairs, step, jnp.zeros(sum_ref.shape, F32))
 
 
-def first_hidden(pre_one, mask_planes, scale, shift):
+def first_hidden(pre_one, mask_planes, scale, shift, deps):
     crops, height, breadth, width = pre_one.shape
     tile = 16
     consts = jnp.concatenate([tall(scale), tall(shift)], axis=0)
     planes = planes_of(height, width, tile * 8)
-    hidden, slope, sums = kernel_call(
+    *hidden, slope, sums = kernel_call(
         functools.partial(first_body, height),
         crops // tile,
         [
@@ -351,7 +453,7 @@
             whole_block(consts),
         ],
         [
-            (jax.ShapeDtypeStruct((height, crops * 8, width), BF16), planes),
+            *[plane_out(crops * 8, width, tile * 8)] * height,
             (jax.ShapeDtypeStruct((height, crops * 8, width), F32), planes),
             sum_block(width),
         ],
@@ -359,6 +461,7 @@
         (pre_one, mask_planes, consts),
         40 * pre_one.size,
         pre_one.size,
+        deps,
     )
     return hidden, slope, jnp.sum(sums, axis=0)
 
@@ -405,9 +508,10 @@
     return total
 
 
-def local_body(height, back, x_ref, w_ref, out_ref, taps_ref):
+def local_body(height, back, *refs):
+    w_ref, out_ref, taps_ref = refs[height:]
     for p in range(height):
-        fill_taps(lambda k, p=p: x_ref[p, tile_rows(k), :], taps_ref.at[p], back)
+        fill_taps(lambda k, p=p: refs[p][tile_rows(k), :], taps_ref.at[p], back)
     for i in range(height):
         total = None
         for p in range(height):
@@ -419,16 +523,16 @@
 
 
 def conv_local(planes, weight, back):
-    height, rows, width = planes.shape
+    height = len(planes)
+    rows, width = planes[0].shape
     parts = 2 if rows % 32 == 0 else 1
-    block = planes_of(height, width, rows // parts)
     (out,) = kernel_call(
         functools.partial(local_body, height, back),
         parts,
-        [block, spatial_block(weight)],
-        [(jax.ShapeDtypeStruct(planes.shape, F32), block)],
+        [rows_block(rows // parts, width)] * height + [spatial_block(weight)],
+        [(jax.ShapeDtypeStruct((height, rows, width), F32), planes_of(height, width, rows // parts))],
         [pltpu.VMEM((height, rows // parts, 3 * width), BF16)],
-        (planes, weight[0]),
+        (*planes, weight[0]),
         2 * rows * (3 * height - 2) * 3 * width * width,
     )
     return out
@@ -503,7 +607,7 @@
         dot_ref[...] += second
 
 
-def conv_back_halo(part, above, below, weight, slope, pre_one):
+def conv_back_halo(part, above, below, weight, slope, pre_one, deps):
     height, rows, width = part.shape
     parts = 2 if rows % 32 == 0 else 1
     size = rows // parts
@@ -524,14 +628,17 @@
         [pltpu.VMEM((2, size, 3 * width), BF16)],
         (part, above, below, weight[0], slope, pre_one),
         2 * rows * 2 * 3 * width * width,
+        deps=deps,
     )
     return out, jnp.sum(first, axis=0), jnp.sum(second, axis=0)
 
 
-def spatial_grad_body(height, x_ref, above_ref, below_ref, g_ref, mean_ref, total_ref, out_ref, taps_ref):
-    rows = g_ref.shape[1]
+def spatial_grad_body(height, *refs):
+    x_refs, (above_ref, below_ref), g_refs = refs[:height], refs[height : height + 2], refs[height + 2 : -4]
+    mean_ref, total_ref, out_ref, taps_ref = refs[-4:]
+    rows = above_ref.shape[0]
     reads = [lambda k: above_ref[tile_rows(k), :]]
-    reads += [lambda k, p=p: x_ref[p, tile_rows(k), :] for p in range(height)]
+    reads += [lambda k, ref=ref: ref[tile_rows(k), :] for ref in x_refs]
     reads += [lambda k: below_ref[tile_rows(k), :]]
     for b in range(3):
 
@@ -551,18 +658,19 @@
     for a in range(3):
         total = None
         for i in range(height):
-            part = lax.dot_general(taps_ref[i + a], g_ref[i], TN, preferred_element_type=F32)
+            part = lax.dot_general(taps_ref[i + a], g_refs[i][...], TN, preferred_element_type=F32)
             total = part if total is None else total + part
         out_ref[a, 0] = (total - mean_ref[...] * total_ref[...]).astype(BF16)
 
 
-def spatial_grad(hidden, above, below, grads, hidden_mean, grad_total):
-    height, rows, width = hidden.shape
+def spatial_grad(hidden, above, below, grads, hidden_mean, grad_total, deps):
+    height = len(hidden)
+    rows, width = above.shape
     mean, total = hidden_mean.reshape(width, 1), grad_total.reshape(1, width)
     (out,) = kernel_call(
         functools.partial(spatial_grad_body, height),
         3,
-        [whole_block(a) for a in (hidden, above, below, grads, mean, total)],
+        [whole_block(a) for a in (*hidden, above, below, *grads, mean, total)],
         [
             (
                 jax.ShapeDtypeStruct((3, 3, width, width), BF16),
@@ -570,8 +678,9 @@
             )
         ],
         [pltpu.VMEM((height + 2, rows, width), BF16)],
-        (hidden, above, below, grads, mean, total),
+        (*hidden, above, below, *grads, mean, total),
         2 * 9 * height * rows * width * width,
+        deps=deps,
     )
     return out.reshape(9 * width, width)
 
@@ -636,8 +745,12 @@
     return hidden, slope, jnp.sum(first, axis=0), jnp.sum(second, axis=0), jnp.sum(mean, axis=0)
 
 
-def third_body(height, h_ref, w_ref, f_ref, m_ref, c_ref, slope_ref, pool_ref, first_ref, second_ref, y_ref):
-    crops = pool_ref.shape[0]
+def third_body(
+    height, share, h_ref, w_ref, f_ref, m_ref, c_ref, slope_ref, pool_ref, first_ref, second_ref, y_ref
+):
+    crops = first_ref.shape[0]
+    start = pl.program_id(0) * crops
+    padding = -share % 8
     pixels = height * 8
     step_rows = max(pixels, TILE)
     per_step = step_rows // pixels
@@ -657,7 +770,9 @@
             for j in range(per_step):
                 rows = slice(j * pixels, (j + 1) * pixels)
                 crop = pl.ds(k * per_step + j, 1)
-                pool_ref[crop, cols] = jnp.sum(value[rows], axis=0, keepdims=True)
+                pooled_at = start + k * per_step + j
+                pooled_at = pooled_at + pooled_at // share * padding
+                pool_ref[pl.ds(pooled_at, 1), cols] = jnp.sum(value[rows], axis=0, keepdims=True)
                 first_ref[crop, cols] = jnp.sum(slope[rows], axis=0, keepdims=True)
                 second_ref[crop, cols] = jnp.sum(slope[rows] * y[rows], axis=0, keepdims=True)
             return carry
@@ -665,7 +780,7 @@
         loop(crops // per_step, step, 0)
 
 
-def third_output(hidden, weight, features, mask_flat, scale, shift, height):
+def third_output(hidden, weight, features, mask_flat, scale, shift, height, share):
     total, width = hidden.shape
     channels = weight.shape[0] * weight.shape[2]
     tile = 16
@@ -673,12 +788,21 @@
     crops = total // (height * 8)
     consts = jnp.concatenate([tall(scale), tall(shift)], axis=0)
     rows_of = lambda n: pl.BlockSpec((flat, n), lambda k: (k, 0))
+    padded = crops // share * (share + -share % 8)
     crop_rows = (jax.ShapeDtypeStruct((crops, channels), F32), pl.BlockSpec((tile, channels), lambda k: (k, 0)))
     return kernel_call(
-        functools.partial(third_body, height),
+        functools.partial(third_body, height, share),
         crops // tile,
         [rows_of(width), whole_block(weight), rows_of(channels), rows_of(1), whole_block(consts)],
-        [(jax.ShapeDtypeStruct((total, channels), BF16), rows_of(channels)), crop_rows, crop_rows, crop_rows],
+        [
+            (jax.ShapeDtypeStruct((total, channels), BF16), rows_of(channels)),
+            (
+                jax.ShapeDtypeStruct((padded, channels), F32),
+                pl.BlockSpec((padded, channels), lambda k: (0, 0)),
+            ),
+            crop_rows,
+            crop_rows,
+        ],
         [pltpu.VMEM((flat, channels), F32)],
         (hidden, weight, features, mask_flat, consts),
         2 * total * width * channels + 40 * total * channels,
@@ -688,6 +812,7 @@
 
 def third_back_body(
     height,
+    inner,
     h_ref,
     w_ref,
     d_ref,
@@ -753,10 +878,15 @@
     @pl.when(pl.program_id(0) == pl.num_programs(0) - 1)
     def _():
         total = jnp.sum(total_ref[...], axis=0, keepdims=True)
+        width = centred_ref.shape[1]
+        blocks, tiles = grad_ref.shape[1] // width, inner // TILE
 
         def centre(k, carry):
             at = tile_rows(k)
-            centred_ref[at, :] = (grad_ref[at, :] - mean_ref[at, :] * total).astype(BF16)
+            centred = (grad_ref[at, :] - mean_ref[at, :] * total).astype(BF16)
+            for part in range(centred.shape[1] // width):
+                block = (k // tiles * blocks + part) * tiles + k % tiles
+                centred_ref[tile_rows(block), :] = centred[:, part * width : (part + 1) * width]
             return carry
 
         lax.fori_loop(0, grad_ref.shape[0] // TILE, centre, 0, unroll=4)
@@ -769,6 +899,7 @@
     total = height * rows
     channels = weight.shape[0] * weight.shape[2]
     mean = hidden_mean.reshape(width, 1)
+    inner = max(TILE, width // device_count())
     tile = 16
     flat = tile * height * 8
     crops = rows // 8
@@ -776,7 +907,7 @@
     rows_of = lambda n: pl.BlockSpec((flat, n), lambda k: (k, 0))
     planes = planes_of(height, width, tile * 8)
     grad, sums, out, first, second = kernel_call(
-        functools.partial(third_back_body, height),
+        functools.partial(third_back_body, height, inner),
         crops // tile,
         [
             rows_of(width),
@@ -790,7 +921,7 @@
             whole_block(mean),
         ],
         [
-            (jax.ShapeDtypeStruct((width, channels), BF16), pl.BlockSpec((width, channels), lambda k: (0, 0))),
+            (jax.ShapeDtypeStruct((channels, width), BF16), pl.BlockSpec((channels, width), lambda k: (0, 0))),
             sum_block(channels),
             (jax.ShapeDtypeStruct(pre_two.shape, F32), planes),
             sum_block(width),
@@ -808,7 +939,8 @@
     return grad, jnp.sum(sums, axis=0), out, jnp.sum(first, axis=0), jnp.sum(second, axis=0)
 
 
-def second_back_body(height, g_ref, x_ref, m_ref, c_ref, out_ref, sum_ref):
+def second_back_body(height, g_ref, x_ref, m_ref, c_ref, *refs):
+    out_refs, sum_ref = refs[:height], refs[height]
     clear_first(sum_ref)
     for i in range(height):
 
@@ -816,30 +948,32 @@
             at = tile_rows(k)
             line = c_ref[TILE : 2 * TILE] + c_ref[2 * TILE :] * x_ref[i, at, :]
             g = (c_ref[:TILE] * g_ref[i, at, :] + m_ref[i, at, :] * line).astype(BF16)
-            out_ref[i, at, :] = g
+            out_refs[i][at, :] = g
             return carry + fold(g.astype(F32))
 
         sum_ref[...] += loop(g_ref.shape[1] // TILE, step, jnp.zeros(sum_ref.shape, F32))
 
 
-def second_back(grads, pre_two, mask_planes, alpha, beta, gamma):
+def second_back(grads, pre_two, mask_planes, alpha, beta, gamma, deps):
     height, rows, width = pre_two.shape
     size = 128
     consts = jnp.concatenate([tall(alpha), tall(beta), tall(gamma)], axis=0)
     block = planes_of(height, width, size)
-    out, sums = kernel_call(
+    *out, sums = kernel_call(
         functools.partial(second_back_body, height),
         rows // size,
         [block, block, planes_of(height, 1, size), whole_block(consts)],
-        [(jax.ShapeDtypeStruct(pre_two.shape, BF16), block), sum_block(width)],
+        [plane_out(rows, width, size)] * height + [sum_block(width)],
         [],
         (grads, pre_two, mask_planes, consts),
         10 * pre_two.size,
+        deps=deps,
     )
     return out, jnp.sum(sums, axis=0)
 
 
-def first_back_body(height, g_ref, x_ref, m_ref, c_ref, out_ref):
+def first_back_body(height, g_ref, x_ref, m_ref, c_ref, f_ref, out_ref, grad_ref, total_ref):
+    clear_first(total_ref)
     width = out_ref.shape[1]
     per_step = max(1, 2 // height)
 
@@ -851,33 +985,43 @@
         return carry
 
     loop(out_ref.shape[0] // TILE, step, 0)
-
-
-def first_back(grads, pre_one, mask_flat, alpha, beta, gamma):
+    last = pl.program_id(0) == pl.num_programs(0) - 1
+    for at in range(0, f_ref.shape[1], width):
+        part = slice(at, at + width)
+        total_ref[part, :] += lax.dot_general(
+            f_ref[:, part], out_ref[...], TN, preferred_element_type=F32
+        )
+
+    @pl.when(last)
+    def _():
+        grad_ref[...] = total_ref[...].astype(BF16)
+
+
+def first_back(grads, pre_one, mask_flat, alpha, beta, gamma, features, deps):
     crops, height, breadth, width = pre_one.shape
-    tile = 16
+    channels = features.shape[1]
+    tile = crops // 2
     flat = tile * height * 8
     consts = jnp.concatenate([tall(alpha), tall(beta), tall(gamma)], axis=0)
-    (out,) = kernel_call(
+    return kernel_call(
         functools.partial(first_back_body, height),
         crops // tile,
         [
             planes_of(height, width, tile * 8),
             pl.BlockSpec((tile, height, 8, width), lambda k: (k, 0, 0, 0)),
-            pl.BlockSpec((flat, 1), lambda k: (k, 0)),
+            rows_block(flat, 1),
             whole_block(consts),
+            rows_block(flat, channels),
         ],
         [
-            (
-                jax.ShapeDtypeStruct((crops * height * 8, width), BF16),
-                pl.BlockSpec((flat, width), lambda k: (k, 0)),
-            )
+            plane_out(crops * height * 8, width, flat),
+            (jax.ShapeDtypeStruct((channels, width), BF16), pl.BlockSpec((channels, width), lambda k: (0, 0))),
         ],
-        [],
-        (grads, pre_one, mask_flat, consts),
-        10 * pre_one.size,
-    )
-    return out
+        [pltpu.VMEM((channels, width), F32)],
+        (grads, pre_one, mask_flat, consts, features),
+        2 * crops * height * 8 * width * channels,
+        deps=deps,
+    )
 
 
 def last_body(height, g_ref, w_ref, d_ref, s_ref, out_ref, y_ref):
@@ -902,7 +1046,7 @@
         loop(s_ref.shape[0] // per_step, step, 0)
 
 
-def last_grads(grads, weight, slope_three, scale_rows, height):
+def last_grads(grads, weight, slope_three, scale_rows, height, deps):
     total, width = grads.shape
     channels = weight.shape[0]
     tile = 16
@@ -922,6 +1066,7 @@
         [pltpu.VMEM((flat, channels), F32)],
         (grads, weight, slope_three, scale_rows),
         2 * total * width * channels,
+        deps=deps,
     )
     return out
 
@@ -975,12 +1120,22 @@
     hidden_cols = w_hidden.shape[1]
     full_hidden, full_embed = head_whole[:, :hidden_cols], head_whole[:, hidden_cols:]
 
+    row_bits = [(0, b) for b in bits_of("rows")]
+    crop_count = jnp.sum(pixel_mask.reshape(local_crops, -1), axis=1).astype(F32)
+    crop_count = jnp.broadcast_to(crop_count[:, None], (local_crops, 128))
+    crop_count = crop_count.reshape((2,) * len(row_bits) + (share, 128))
+    for k, step in enumerate(row_bits):
+        crop_count = halve(crop_count, len(row_bits) - 1 - k, step, False)
+    crop_count = crop_count[:, :1]
+
     flat_in = features.reshape(-1, channels)
     weight_col = pixel_mask.reshape(-1, 1).astype(F32)
     mask_planes = (
         pixel_mask.transpose(1, 0, 2).reshape(height, local_crops * breadth, 1).astype(F32)
     )
 
+    queue_unit = queued * lax.rsqrt(jnp.sum(queued * queued, axis=1, keepdims=True) + EPS_UNIT)
+    queue_scores = jnp.dot(queue_unit, prototypes, precision=PRECISE)
     pre_one = jnp.dot(flat_in, full_reduce, preferred_element_type=F32)
     masked_one = pre_one * weight_col
     sums_one = total_narrow(
@@ -997,7 +1152,7 @@
     pre_one = pre_one.reshape(local_crops, height, breadth, narrow)
     scale_one = gain_one * spread_one
     hidden_one, slope_one, hidden_sum_one = first_hidden(
-        pre_one, mask_planes, scale_one, bias_one - mean_one * scale_one
+        pre_one, mask_planes, scale_one, bias_one - mean_one * scale_one, (queue_scores,)
     )
     above_one, below_one = edge_rows(hidden_one)
     part_two = conv_local(hidden_one, full_spatial, False)
@@ -1014,19 +1169,12 @@
     mean_three, spread_three = spread_of(sums_three[: 2 * channels].reshape(2, -1), valid_count)
     scale_three = gain_three * spread_three
     slope_three, crop_sums, slope_sums, slope_dots = third_output(
-        hidden_two, full_expand, flat_in, weight_col, scale_three, bias_three - mean_three * scale_three, height
-    )
-    crop_valid = jnp.sum(pixel_mask.reshape(local_crops, -1), axis=1).astype(F32)
-
-    row_bits = [(0, b) for b in bits_of("rows")]
-    pooled = jnp.concatenate(
-        [crop_sums, jnp.broadcast_to(crop_valid[:, None], (local_crops, 128))], axis=1
-    )
-    pooled = pooled.reshape((2,) * len(row_bits) + (share, channels + 128))
+        hidden_two, full_expand, flat_in, weight_col, scale_three, bias_three - mean_three * scale_three, height, share
+    )
+    pooled = crop_sums.reshape((2,) * len(row_bits) + (-1, channels))
     for k, step in enumerate(row_bits):
         pooled = halve(pooled, len(row_bits) - 1 - k, step, False)
-    crop_count = pooled[:, channels : channels + 1]
-    pooled = pooled[:, :channels] / crop_count
+    pooled = pooled[:share] / crop_count
 
     pre_head = split_dot(pooled, full_hidden, 0, 3)
     sums_head = total_wide(jnp.stack([jnp.sum(pre_head, axis=0), jnp.sum(pre_head * pre_head, axis=0)]))
@@ -1042,11 +1190,9 @@
         - lax.axis_index("crops") * local_crops
     )
     partner_at = (partner_rows // share ^ lax.axis_index("rows")) * share + partner_rows % share
-    queue_unit = queued * lax.rsqrt(jnp.sum(queued * queued, axis=1, keepdims=True) + EPS_UNIT)
     row_total = total_crops + queued.shape[0] * lax.axis_size("crops") * row_count
     proto_total = prototypes.shape[1]
     scores = jnp.dot(unit_embed, prototypes, precision=PRECISE)
-    queue_scores = jnp.dot(queue_unit, prototypes, precision=PRECISE)
     plan_mass = jnp.exp(scores / SHARPNESS)
     queue_mass = jnp.exp(queue_scores / SHARPNESS)
     for iteration in range(3):
@@ -1098,26 +1244,30 @@
     scale_rows = lax.all_gather(per_pixel, "rows", axis=0, tiled=True)
 
     crop_index = lax.axis_index("crops")
-    forward_all, backward_all = gather_products(
-        jnp.concatenate([pooled, hidden_head, unit_embed], axis=1),
-        jnp.concatenate([grad_pre_head, grad_embedding, grad_scores], axis=1),
-    )
-    shard_hidden, shard_embed = w_hidden.shape[0], w_embed.shape[0]
-    score_at = hidden_cols + w_embed.shape[1]
-    pooled_part = lax.dynamic_slice_in_dim(forward_all, crop_index * shard_hidden, shard_hidden, 1)
-    hidden_part = lax.dynamic_slice_in_dim(
-        forward_all, channels + crop_index * shard_embed, shard_embed, 1
-    )
-    out_hidden = jnp.dot(pooled_part.T, backward_all[:, :hidden_cols], preferred_element_type=F32)
-    out_embed = jnp.dot(hidden_part.T, backward_all[:, hidden_cols:score_at], preferred_element_type=F32)
-    grad_prototypes = jnp.dot(
-        forward_all[:, channels + hidden_cols :].T, backward_all[:, score_at:], preferred_element_type=F32
-    )
+    proto_pad = -proto_total % 128
+    products = gather_products(
+        [pooled, hidden_head, unit_embed],
+        [grad_pre_head, grad_embedding, jnp.pad(grad_scores, ((0, 0), (0, proto_pad)))],
+    )
+    shard_hidden, shard_embed, width = w_hidden.shape[0], w_embed.shape[0], w_embed.shape[1]
+    right_at = channels + hidden_cols + width
+
+    def product_of(at, size, to, count):
+        return lax.dot_general(
+            lax.dynamic_slice_in_dim(products, at, size, 1),
+            lax.slice_in_dim(products, right_at + to, right_at + to + count, axis=1),
+            TN,
+            preferred_element_type=F32,
+        )
+
+    out_hidden = product_of(crop_index * shard_hidden, shard_hidden, 0, hidden_cols)
+    out_embed = product_of(channels + crop_index * shard_embed, shard_embed, hidden_cols, width)
+    grad_prototypes = product_of(channels + hidden_cols, width, hidden_cols + width, proto_total)
 
     sums_three_back = jnp.concatenate(
         [jnp.sum(scale_rows * slope_sums, axis=0), jnp.sum(scale_rows * slope_dots, axis=0)]
     )
-    sums_three_back = total_wide(after(sums_three_back, forward_all)[None])[0]
+    sums_three_back = total_wide(sums_three_back[None])[0]
     grad_bias_three = sums_three_back[:channels]
     alpha, beta, gamma, grad_gain_three = back_consts(
         gain_three, mean_three, spread_three, valid_count, grad_bias_three, sums_three_back[channels:]
@@ -1134,52 +1284,72 @@
         pre_two,
         hidden_mean_two,
     )
-    expand_stages = reduce_stages(grad_w_expand)
     sums_two_back = total_narrow(jnp.stack([sum_back, dot_back]))
     grad_bias_two = sums_two_back[0]
     alpha, beta, gamma, grad_gain_two = back_consts(
         gain_two, mean_two, spread_two, valid_count, grad_bias_two, sums_two_back[1]
     )
-    alpha = after(alpha, next(expand_stages))
-    grad_pre_two, total_two = second_back(grad_act_two, pre_two, mask_planes, alpha, beta, gamma)
+    grad_pre_two, total_two = second_back(
+        grad_act_two, pre_two, mask_planes, alpha, beta, gamma, ()
+    )
     above_two, below_two = edge_rows(grad_pre_two)
     part_one = conv_local(grad_pre_two, full_spatial, True)
+    grad_act_one, sum_back, dot_back = conv_back_halo(
+        part_one, above_two, below_two, full_spatial, slope_one, pre_one, ()
+    )
+    sums_one_back = total_narrow(
+        jnp.concatenate([sum_back, dot_back, total_two, total_three]).reshape(-1, narrow)
+    )
     grad_w_spatial = spatial_grad(
         hidden_one,
         above_one,
         below_one,
         grad_pre_two,
         hidden_mean_one,
-        after(total_two, next(expand_stages), part_one),
-    )
-    spatial_stages = reduce_stages(grad_w_spatial)
-    grad_act_one, sum_back, dot_back = conv_back_halo(
-        part_one, after(above_two, next(expand_stages)), below_two, full_spatial, slope_one, pre_one
-    )
-    next(spatial_stages)
-    sums_one_back = total_narrow(jnp.stack([sum_back, dot_back]))
+        total_two,
+        (grad_act_one,),
+    )
     grad_bias_one = sums_one_back[0]
     alpha, beta, gamma, grad_gain_one = back_consts(
         gain_one, mean_one, spread_one, valid_count, grad_bias_one, sums_one_back[1]
     )
-    out_expand = next(expand_stages)
-    grad_pre_one = first_back(grad_act_one, pre_one, weight_col, alpha, beta, gamma)
-    grad_w_reduce = lax.dot_general(
-        flat_in, after(grad_pre_one, next(spatial_stages)), TN, preferred_element_type=F32
-    ).astype(BF16)
-    *_, out_reduce = reduce_stages(grad_w_reduce)
-    *_, out_spatial = spatial_stages
+    spatial_core = core_exchange(grad_w_spatial, (alpha,))
+    blocks = channels // narrow
+    spatial_rows, *lane_rows = [
+        n // row_count for n in (w_spatial.shape[0], w_reduce.shape[0], blocks * w_expand.shape[0])
+    ]
+    grad_pre_one, grad_w_reduce = first_back(
+        grad_act_one, pre_one, weight_col, alpha, beta, gamma, flat_in, (spatial_core[0],)
+    )
+    near = near_exchange([spatial_core], [spatial_rows])
+    lines = [
+        line_exchange(core_exchange(g), n) for g, n in zip((grad_w_reduce, grad_w_expand), lane_rows)
+    ]
     grad_features = last_grads(
-        grad_pre_one, full_reduce, slope_three, scale_rows, height
-    ).reshape(features.shape)
-
-    totals = total_wide(jnp.concatenate([total_three, total_two])[None])[0]
+        grad_pre_one,
+        full_reduce,
+        slope_three,
+        scale_rows,
+        height,
+        (out_hidden, out_embed, grad_prototypes, near[0], *[parts[0] for parts in lines]),
+    )
+    far = far_exchange(near, (grad_features,))
+    lane = near_exchange(lines, lane_rows, (grad_features,))
+    lane = exchange([lane], reduce_steps()[2][:-1], [sum(lane_rows)])
+    out_spatial = reduce_end(far).reshape(w_spatial.shape)
+    sums = reduce_end(lane).reshape(row_count, -1, narrow)
+    out_reduce = sums[:, : lane_rows[0]].reshape(w_reduce.shape)
+    out_expand = sums[:, lane_rows[0] :].reshape(row_count, blocks, -1, narrow)
+    out_expand = out_expand.transpose(0, 2, 1, 3).reshape(w_expand.shape)
+    grad_features = grad_features.reshape(features.shape)
+
+    grad_totals = sums_one_back[2:].reshape(-1)
     tap_means = jnp.tile(hidden_mean_one, 9)
     shard_expand, shard_spatial = w_expand.shape[0], w_spatial.shape[0]
     means = lax.dynamic_slice_in_dim(hidden_mean_two, crop_index * shard_expand, shard_expand)
-    out_expand = out_expand + means[:, None] * totals[:channels]
+    out_expand = out_expand + means[:, None] * grad_totals[narrow:]
     means = lax.dynamic_slice_in_dim(tap_means, crop_index * shard_spatial, shard_spatial)
-    out_spatial = out_spatial + means[:, None] * totals[channels:]
+    out_spatial = out_spatial + means[:, None] * grad_totals[:narrow]
     return (
         swav_loss,
         grad_features,

time: 593 us -> 560 us (0.944)
  waiting for transfers between devices: 123 us -> 79.1 us
  Pallas kernels: 114 us -> 146 us
  local copies, waits for them, and re-layouts: 55.5 us -> 37.8 us
  blocking collectives: 50.2 us -> 66.3 us
  other arithmetic: 43.4 us -> 32.5 us
  matrix products: 48 us -> 41.7 us
    all_to_all x6 -> x0, waiting for transfers between devices: 35.4 us -> none  [swap_sum(): lax.all_to_all(values, BOTH, 0, 0, axis_index_groups=list(groups.values()...]
    pallas_call x12 -> x24, Pallas kernels: 114 us -> 146 us  [the longest x13 120 us: kernel_call(): pl.pallas_call(inner, grid=(grid,), in_specs=ins + [pl.BlockSpec(memory_s...]
    all_to_all x4 -> x3, waiting for transfers between devices: 35.3 us -> 6.93 us  [total_narrow(): return jnp.sum(lax.all_to_all(copies, BOTH, 0, 0, tiled=True), axis=0)]
    all_to_all x6 -> x0, starting transfers between devices: 22 us -> none  [swap_sum(): lax.all_to_all(values, BOTH, 0, 0, axis_index_groups=list(groups.values()...]
    ppermute x68 -> x73, starting transfers between devices: 80.1 us -> 98 us  [xor_permute(): return lax.ppermute(values, BOTH, pairs)]
    ppermute x68 -> x73, waiting for transfers between devices: 44.5 us -> 58.2 us  [xor_permute(): return lax.ppermute(values, BOTH, pairs)]
    all_to_all x0 -> x1, blocking collectives: none -> 13.4 us  [total_narrow(): return jnp.sum(lax.all_to_all(copies, BOTH, 0, 0, tiled=True), axis=0)]
    all_gather x2 -> x1, starting transfers between devices: 0.26 us -> 12.3 us  [gather_products(): return lax.all_gather(packed, BOTH, axis=0, tiled=True)]
  transfers between devices with their start and end apart: 86 -> 83, of which waited for: 53 -> 42; matrix products, arithmetic and copies ran while one was open for 22% -> 14% of each run, Pallas kernels for 20% -> 26%
where the time goes in v2:
time: 560 us; the launch traced here: 553 us
  Pallas kernels  146 us (26%)
  starting transfers between devices  134 us (24%)
  waiting for transfers between devices  79.1 us (14%)
  blocking collectives  66.3 us (12%)
  matrix products  41.7 us (7%)
  local copies, waits for them, and re-layouts  37.8 us (7%)
  other arithmetic  32.5 us (6%)
  between operations  16.3 us (3%)
    pallas_call x13, Pallas kernels, kernel_call(): pl.pallas_call(inner, grid=(grid,), in_specs=ins + [pl.BlockSpec(memory_s...  120 us
    ppermute x73, starting transfers between devices, xor_permute(): return lax.ppermute(values, BOTH, pairs)  98 us
    ppermute x73, waiting for transfers between devices, xor_permute(): return lax.ppermute(values, BOTH, pairs)  58.2 us
    all_to_all x1, blocking collectives, gather_first(): lax.all_to_all(jnp.broadcast_to(mine[None], (crop_total, size, cols)), 'c...  38.5 us
    pallas_call x11, Pallas kernels, merge_split(): pl.pallas_call(body, grid_spec=pltpu.PrefetchScalarGridSpec(num_scalar_pr...  25.2 us
    all_gather x1, blocking collectives, shards(): scale_rows = lax.all_gather(per_pixel, 'rows', axis=0, tiled=True)  14.4 us
    all_to_all x3, starting transfers between devices, total_narrow(): return jnp.sum(lax.all_to_all(copies, BOTH, 0, 0, tiled=True), axis=0)  13.6 us
    dot_general x4, matrix products, split_dot(): lax.dot_general(split_parts(x, parts), matrix, (((1,), (dim,)), ((), ()))...  13.6 us
  transfers between devices with their start and end apart: 83, of which 42 were waited for; matrix products, arithmetic and copies ran while one was open for 14% of the time, Pallas kernels for 26%

profile of v2, /device:TPU:1, one launch (start us, length us, event | category | flops | bytes accessed | tf_op | source)
XLA Modules:
  0.0 552.8 jit_solution(9997265066369065372)
XLA Ops:
  12.6 38.5 %all_to_all.25 = bf16[8,128,512]{2,1,0:T(8,128)(2,1)S(1)} all-to-all(bf16[8,128,512]{2,1,0:T(8,128)(2,1)S(1)} %broadcast_in_dim.68), channel_id=1, replica_groups=mesh['crops'=8,'rows'=4] {'crops'}, dimensions={0} | all-to-all | bytes 2097152 | tf_op jit(solution)/shard_map/all_to_all | solution.py:136
  59.5 7.9 %multiply_reduce_fusion = (f32[512]{0:T(512)S(1)}, f32[512]{0:T(512)S(1)}, f32[1280,512]{0,1:T(8,128)}) fusion(f32[1280]{0:T(1024)S(1)} %convert_element_type.79, bf16[2048,512]{1,0:T(8,128)(2,1)S(1)} %bitcast.200, bf16[1280,2048]{1,0:T(8,128)(2,1)} %bitcast.203), kind=kOutput, calls=%fused_computation.8 | convolution fusion | flops 2686974976 | bytes 9970688 | tf_op jit(solution)/shard_map/dot_general | solution.py:1139
  80.5 6.9 %all-to-all-done.1 = f32[32,3,512]{2,1,0:T(4,128)S(1)} async-done(((f32[32,3,512]{2,1,0:T(4,128)}), f32[32,3,512]{2,1,0:T(4,128)S(1)}, u32[]{:S(2)}, u32[]{:S(2)}) %all-to-all-start.1) | async-done | bytes 196640 | tf_op jit(solution)/shard_map/all_to_all | solution.py:91
  89.8 6.1 %shard_map.297 = (bf16[640,512]{1,0:T(8,128)(2,1)}, bf16[640,512]{1,0:T(8,128)(2,1)}, f32[2,640,512]{2,1,0:T(8,128)}, f32[8,512]{1,0:T(8,128)S(1)}) custom-call(f32[80,2,8,512]{3,2,1,0:T(8,128)} %bitcast.191, f32[2,640,1]{2,1,0:T(8,128)} %convert_element_type.104.refs_1_.refs_4_.refs_2_, f32[32,512]{1,0:T(8,128)S(1)} %pad_maximum_fusion.9.refs_2_, ...), custom_call_target="tpu_custom_call" | custom-call | flops 26214400 | bytes 6640640 | tf_op jit(solution)/shard_map/pallas_call | solution.py:208
  101.3 8.9 %shard_map.298.refs_0_ = f32[2,640,512]{2,1,0:T(8,128)} custom-call(bf16[640,512]{1,0:T(8,128)(2,1)} %get-tuple-element.69.refs_0_, bf16[640,512]{1,0:T(8,128)(2,1)} %get-tuple-element.70.refs_1_, bf16[32,208,512]{2,1,0:T(8,128)(2,1)} %bitcast.194), custom_call_target="tpu_custom_call" | custom-call | flops 4026531840 | bytes 10747904 | tf_op jit(solution)/shard_map/pallas_call | solution.py:208
  113.8 9.0 %shard_map.299 = (f32[2,640,512]{2,1,0:T(8,128)}, f32[8,512]{1,0:T(8,128)S(1)}, f32[8,512]{1,0:T(8,128)S(1)}) custom-call(f32[2,640,512]{2,1,0:T(8,128)} %shard_map.298.refs_0_, bf16[640,512]{1,0:T(8,128)(2,1)S(1)} %collective-permute-done.1.refs_1_.refs_2_, bf16[640,512]{1,0:T(8,128)(2,1)S(1)} %collective-permute-done.2.refs_2_.refs_3_, ...), custom_call_target="tpu_custom_call" | custom-call | flops 2013265920 | bytes 13407232 | tf_op jit(solution)/shard_map/pallas_call | solution.py:208
  127.9 12.3 %all-gather.8.cloned.1.call-start = ((), (), s32[]{:S(2)}) async-start(), calls=%async_computation.6 | async-start | bytes 15003648 | tf_op jit(solution)/shard_map/all_gather | solution.py:420
  148.0 8.8 %shard_map.300 = (bf16[1280,512]{1,0:T(8,128)(2,1)}, f32[2,640,512]{2,1,0:T(8,128)}, f32[8,2048]{1,0:T(8,128)S(1)}, f32[8,2048]{1,0:T(8,128)S(1)}, f32[8,512]{1,0:T(8,128)S(1)}) custom-call(f32[2,640,512]{2,1,0:T(8,128)} %get-tuple-element.71.refs_0_.refs_7_.refs_1_, f32[1280,1]{1,0:T(8,128)S(1)} %convert_element_type.105.refs_1_.refs_3_.refs_2_, ...), custom_call_target="tpu_custom_call" | custom-call | flops 2684354560 | bytes 8868864 | tf_op jit(solution)/shard_map/pallas_call | solution.py:208
  174.4 17.4 %shard_map.301 = (bf16[1280,2048]{1,0:T(8,128)(2,1)}, f32[96,2048]{1,0:T(8,128)}, f32[80,2048]{1,0:T(8,128)S(1)}, f32[80,2048]{1,0:T(8,128)S(1)}) custom-call(bf16[1280,512]{1,0:T(8,128)(2,1)} %get-tuple-element.75.refs_0_, bf16[4,512,512]{2,1,0:T(8,128)(2,1)} %bitcast.211, bf16[1280,2048]{1,0:T(8,128)(2,1)} %bitcast.204, f32[1280,1]{1,0:T(8,128)} %copy-done.3, ...), custom_call_target="tpu_custom_call" | custom-call | flops 2789212160 | bytes 16258048 | tf_op jit(solution)/shard_map/pallas_call | solution.py:208
  206.6 5.0 fusion.2
  310.8 6.0 %fusion = f32[40,2048]{1,0:T(8,128)S(1)} fusion(bf16[2048,2176]{1,0:T(8,128)(2,1)} %all-gather.6.cloned.1.call-done, bf16[20,2048]{1,0:T(8,128)(2,1)S(1)} %fusion.32, bf16[20,2048]{1,0:T(8,128)(2,1)S(1)} %get-tuple-element.147), kind=kOutput, calls=%fused_computation.1 | convolution fusion | flops 335872000 | bytes 8880128 | tf_op jit(solution)/shard_map/dot_general | solution.py:184
  316.9 14.4 %all-gather.1 = f32[4,20,2048]{2,1,0:T(8,128)S(1)} all-gather(f32[1,20,2048]{2,1,0:T(8,128)S(1)} %fusion.36), channel_id=1, replica_groups=mesh['crops'=8,'rows'=4] {'rows'}, dimensions={0}, use_global_device_ids=true | all-gather | bytes 819200 | tf_op jit(solution)/shard_map/all_gather | solution.py:1244
  349.3 15.0 %shard_map.302 = (bf16[2048,512]{1,0:T(8,128)(2,1)}, f32[8,2048]{1,0:T(8,128)S(1)}, f32[2,640,512]{2,1,0:T(8,128)}, f32[8,512]{1,0:T(8,128)S(1)}, f32[8,512]{1,0:T(8,128)S(1)}) custom-call(bf16[1280,512]{1,0:T(8,128)(2,1)} %get-tuple-element.75.refs_0_, bf16[4,512,512]{2,1,0:T(8,128)(2,1)} %bitcast.212, bf16[1280,2048]{1,0:T(8,128)(2,1)} %get-tuple-element.80.refs_2_, ...), custom_call_target="tpu_custom_call" | custom-call | flops 8053063680 | bytes 19635200 | tf_op jit(solution)/shard_map/pallas_call | solution.py:208
  364.4 13.4 %all_to_all.26 = f32[32,2,512]{2,1,0:T(2,128)S(1)} all-to-all(f32[32,2,512]{2,1,0:T(2,128)S(1)} %broadcast_in_dim.84), channel_id=1, replica_groups=mesh['crops'=8,'rows'=4] {'crops','rows'}, dimensions={0} | all-to-all | bytes 262144 | tf_op jit(solution)/shard_map/all_to_all | solution.py:91
  379.2 5.2 shard_map.303
  389.0 8.8 %shard_map.304.refs_0_ = f32[2,640,512]{2,1,0:T(8,128)} custom-call(bf16[640,512]{1,0:T(8,128)(2,1)S(1)} %get-tuple-element.87.refs_0_.refs_4_, bf16[640,512]{1,0:T(8,128)(2,1)} %get-tuple-element.88.refs_1_.refs_5_, bf16[32,208,512]{2,1,0:T(8,128)(2,1)} %bitcast.197), custom_call_target="tpu_custom_call" | custom-call | flops 4026531840 | bytes 10747904 | tf_op jit(solution)/shard_map/pallas_call | solution.py:208
  397.8 8.6 %collective-permute-done.56.refs_1_ = bf16[640,512]{1,0:T(8,128)(2,1)S(1)} collective-permute-done((bf16[640,512]{1,0:T(8,128)(2,1)}, bf16[640,512]{1,0:T(8,128)(2,1)S(1)}, u32[]{:S(2)}, u32[]{:S(2)}) %collective-permute-start.56) | collective-permute-done | bytes 655392 | tf_op jit(solution)/shard_map/ppermute | solution.py:1076
  408.0 8.4 %shard_map.305 = (f32[2,640,512]{2,1,0:T(8,128)}, f32[8,512]{1,0:T(8,128)S(1)}, f32[8,512]{1,0:T(8,128)S(1)}) custom-call(f32[2,640,512]{2,1,0:T(8,128)} %shard_map.304.refs_0_, bf16[640,512]{1,0:T(8,128)(2,1)S(1)} %collective-permute-done.56.refs_1_, bf16[640,512]{1,0:T(8,128)(2,1)S(1)} %collective-permute-done.57.refs_2_, bf16[32,208,512]{2,1,0:T(8,128)(2,1)} %bitcast.198, ...), custom_call_target="tpu_custom_call" | custom-call | flops 2013265920 | bytes 18644992 | tf_op jit(solution)/shard_map/pallas_call | solution.py:208
  422.3 13.4 %shard_map.306 = bf16[3,3,512,512]{3,2,1,0:T(8,128)(2,1)} custom-call(bf16[640,512]{1,0:T(8,128)(2,1)} %get-tuple-element.69.refs_0_, bf16[640,512]{1,0:T(8,128)(2,1)} %get-tuple-element.70.refs_1_, bf16[640,512]{1,0:T(8,128)(2,1)} %copy-done.8, bf16[640,512]{1,0:T(8,128)(2,1)} %copy-done.9, bf16[640,512]{1,0:T(8,128)(2,1)} %copy-done.11, ...), custom_call_target="tpu_custom_call" | custom-call | flops 6039797760 | bytes 8654848 | tf_op jit(solution)/shard_map/pallas_call | solution.py:208
  446.5 9.2 %shard_map.308 = (bf16[1280,512]{1,0:T(8,128)(2,1)}, bf16[2048,512]{1,0:T(8,128)(2,1)}) custom-call(f32[2,640,512]{2,1,0:T(8,128)} %get-tuple-element.90.refs_8_.refs_0_, f32[80,2,8,512]{3,2,1,0:T(8,128)} %bitcast.193, f32[1280,1]{1,0:T(8,128)S(1)} %copy-done.4, f32[48,512]{1,0:T(8,128)S(1)} %pad_maximum_fusion.8.refs_3_, bf16[1280,2048]{1,0:T(8,128)(2,1)} %bitcast.205, ...), custom_call_target="tpu_custom_call" | custom-call | flops 2684354560 | bytes 13997056 | tf_op jit(solution)/shard_map/pallas_call | solution.py:208
  475.2 5.5 fusion.4
  489.5 9.1 %shard_map.315.refs_4_ = bf16[1280,2048]{1,0:T(8,128)(2,1)} custom-call(bf16[1280,512]{1,0:T(8,128)(2,1)} %get-tuple-element.96.refs_0_, bf16[2048,512]{1,0:T(8,128)(2,1)} %bitcast.201, bf16[1280,2048]{1,0:T(8,128)(2,1)} %get-tuple-element.80.refs_2_, f32[80,2048]{1,0:T(8,128)} %reshape.463.refs_3_, f32[256,2048]{1,0:T(8,128)} %fusion.8.refs_4_, ...), custom_call_target="tpu_custom_call" | custom-call | flops 2684354560 | bytes 14548992 | tf_op jit(solution)/shard_map/pallas_call | solution.py:208
  515.9 7.5 %collective-permute-done.73 = bf16[1,144,512]{2,1,0:T(8,128)(2,1)S(1)} collective-permute-done((bf16[1,144,512]{2,1,0:T(8,128)(2,1)S(1)}, bf16[1,144,512]{2,1,0:T(8,128)(2,1)S(1)}, u32[]{:S(2)}, u32[]{:S(2)}) %collective-permute-start.73) | collective-permute-done | bytes 147488 | tf_op jit(solution)/shard_map/ppermute | solution.py:35
  531.8 5.4 collective-permute-start.76
  (534 shorter events, 285.8 us)
Async XLA Ops:
  7.2 94.1 %all-gather.10.cloned.1.call-start = ((), (), s32[]{:S(2)}) async-start(), calls=%async_computation.7 | async-start | bytes 7028736 | tf_op jit(solution)/shard_map/all_gather | solution.py:151
  10.0 196.6 %all-gather.6.cloned.1.call-start = ((), (), s32[]{:S(2)}) async-start(), calls=%async_computation.5 | async-start | bytes 9191424 | tf_op jit(solution)/shard_map/all_gather | solution.py:1117
  68.2 19.2 %all-to-all-start.1 = ((f32[32,3,512]{2,1,0:T(4,128)}), f32[32,3,512]{2,1,0:T(4,128)S(1)}, u32[]{:S(2)}, u32[]{:S(2)}) async-start(f32[32,3,512]{2,1,0:T(4,128)} %broadcast_in_dim.69), calls=%async_computation.1 | async-start | bytes 524288 | tf_op jit(solution)/shard_map/all_to_all | solution.py:91
  95.9 14.3 %collective-permute-start.1 = (bf16[640,512]{1,0:T(8,128)(2,1)}, bf16[640,512]{1,0:T(8,128)(2,1)S(1)}, u32[]{:S(2)}, u32[]{:S(2)}) collective-permute-start(bf16[640,512]{1,0:T(8,128)(2,1)} %get-tuple-element.70.refs_1_), channel_id=1, source_target_pairs={{0,1},{1,2},{2,3},{4,5},{5,6},{6,7},{8,9},{9,10},{10,11},{12,13},{... | collective-permute-start | bytes 1966088 | tf_op jit(solution)/shard_map/ppermute | solution.py:1076
  99.3 14.5 %collective-permute-start.2 = (bf16[640,512]{1,0:T(8,128)(2,1)}, bf16[640,512]{1,0:T(8,128)(2,1)S(1)}, u32[]{:S(2)}, u32[]{:S(2)}) collective-permute-start(bf16[640,512]{1,0:T(8,128)(2,1)} %get-tuple-element.69.refs_0_), channel_id=1, source_target_pairs={{1,0},{2,1},{3,2},{5,4},{6,5},{7,6},{9,8},{10,9},{11,10},{13,12},{... | collective-permute-start | bytes 1966088 | tf_op jit(solution)/shard_map/ppermute | solution.py:1077
  123.6 21.3 %all-to-all-start.2 = ((f32[32,3,512]{2,1,0:T(4,128)}), f32[32,3,512]{2,1,0:T(4,128)S(1)}, u32[]{:S(2)}, u32[]{:S(2)}) async-start(f32[32,3,512]{2,1,0:T(4,128)} %broadcast_in_dim.72), calls=%async_computation.2 | async-start | bytes 524288 | tf_op jit(solution)/shard_map/all_to_all | solution.py:91
  127.9 347.4 %all-gather.8.cloned.1.call-start = ((), (), s32[]{:S(2)}) async-start(), calls=%async_computation.6 | async-start | bytes 15003648 | tf_op jit(solution)/shard_map/all_gather | solution.py:420
  384.4 22.0 %collective-permute-start.56 = (bf16[640,512]{1,0:T(8,128)(2,1)}, bf16[640,512]{1,0:T(8,128)(2,1)S(1)}, u32[]{:S(2)}, u32[]{:S(2)}) collective-permute-start(bf16[640,512]{1,0:T(8,128)(2,1)} %get-tuple-element.88.refs_1_.refs_5_), channel_id=1, source_target_pairs={{0,1},{1,2},{2,3},{4,5},{5,6},{6,7},{8,9},{9,10},{10,11},{12,13},{... | collective-permute-start | bytes 1966088 | tf_op jit(solution)/shard_map/ppermute | solution.py:1076
  386.7 21.4 %collective-permute-start.57 = (bf16[640,512]{1,0:T(8,128)(2,1)S(1)}, bf16[640,512]{1,0:T(8,128)(2,1)S(1)}, u32[]{:S(2)}, u32[]{:S(2)}) collective-permute-start(bf16[640,512]{1,0:T(8,128)(2,1)S(1)} %get-tuple-element.87.refs_0_.refs_4_), channel_id=1, source_target_pairs={{1,0},{2,1},{3,2},{5,4},{6,5},{7,6},{9,8},{10,9},{11,10},{13,12},{... | collective-permute-start | bytes 1966088 | tf_op jit(solution)/shard_map/ppermute | solution.py:1077
  417.4 27.3 %all-to-all-start.4 = ((f32[32,7,512]{2,1,0:T(8,128)}), f32[32,7,512]{2,1,0:T(8,128)S(1)}, u32[]{:S(2)}, u32[]{:S(2)}) async-start(f32[32,7,512]{2,1,0:T(8,128)} %broadcast_in_dim.88), calls=%async_computation.4 | async-start | bytes 1048576 | tf_op jit(solution)/shard_map/all_to_all | solution.py:91
  440.4 27.7 %collective-permute-start.58 = (bf16[16,144,512]{2,1,0:T(8,128)(2,1)}, bf16[16,144,512]{2,1,0:T(8,128)(2,1)}, u32[]{:S(2)}, u32[]{:S(2)}) collective-permute-start(bf16[16,144,512]{2,1,0:T(8,128)(2,1)} %get-tuple-element.97), channel_id=1, source_target_pairs={{0,1},{1,0},{2,3},{3,2},{4,5},{5,4},{6,7},{7,6},{8,9},{9,8},{10,11... | collective-permute-start | bytes 7077896 | tf_op jit(solution)/shard_map/ppermute | solution.py:35
  444.3 15.2 %collective-permute-start.60 = (bf16[16,64,512]{2,1,0:T(8,128)(2,1)}, bf16[16,64,512]{2,1,0:T(8,128)(2,1)S(1)}, u32[]{:S(2)}, u32[]{:S(2)}) collective-permute-start(bf16[16,64,512]{2,1,0:T(8,128)(2,1)} %get-tuple-element.105), channel_id=1, source_target_pairs={{0,1},{1,0},{2,3},{3,2},{4,5},{5,4},{6,7},{7,6},{8,9},{9,8},{10,11... | collective-permute-start | bytes 3145736 | tf_op jit(solution)/shard_map/ppermute | solution.py:35
  463.0 42.5 %collective-permute-start.62 = (bf16[2,256,512]{2,1,0:T(8,128)(2,1)}, bf16[2,256,512]{2,1,0:T(8,128)(2,1)}, u32[]{:S(2)}, u32[]{:S(2)}) collective-permute-start(bf16[2,256,512]{2,1,0:T(8,128)(2,1)} %get-tuple-element.108), channel_id=1, source_target_pairs={{0,8},{1,9},{2,10},{3,11},{4,12},{5,13},{6,14},{7,15},{8,0},{9,1},... | collective-permute-start | bytes 1572872 | tf_op jit(solution)/shard_map/ppermute | solution.py:35
  468.0 37.6 %collective-permute-start.61 = (bf16[2,256,512]{2,1,0:T(8,128)(2,1)}, bf16[2,256,512]{2,1,0:T(8,128)(2,1)}, u32[]{:S(2)}, u32[]{:S(2)}) collective-permute-start(bf16[2,256,512]{2,1,0:T(8,128)(2,1)} %get-tuple-element.107), channel_id=1, source_target_pairs={{0,8},{1,9},{2,10},{3,11},{4,12},{5,13},{6,14},{7,15},{8,0},{9,1},... | collective-permute-start | bytes 1572872 | tf_op jit(solution)/shard_map/ppermute | solution.py:35
  472.5 26.1 %collective-permute-start.71 = (bf16[4,144,512]{2,1,0:T(8,128)(2,1)}, bf16[4,144,512]{2,1,0:T(8,128)(2,1)}, u32[]{:S(2)}, u32[]{:S(2)}) collective-permute-start(bf16[4,144,512]{2,1,0:T(8,128)(2,1)} %get-tuple-element.117), channel_id=1, source_target_pairs={{0,6},{1,7},{2,4},{3,5},{4,2},{5,3},{6,0},{7,1},{8,14},{9,15},{10,... | collective-permute-start | bytes 1769480 | tf_op jit(solution)/shard_map/ppermute | solution.py:35
  474.9 26.7 %collective-permute-start.69 = (bf16[4,144,512]{2,1,0:T(8,128)(2,1)S(1)}, bf16[4,144,512]{2,1,0:T(8,128)(2,1)S(1)}, u32[]{:S(2)}, u32[]{:S(2)}) collective-permute-start(bf16[4,144,512]{2,1,0:T(8,128)(2,1)S(1)} %get-tuple-element.115), channel_id=1, source_target_pairs={{0,2},{1,3},{2,0},{3,1},{4,6},{5,7},{6,4},{7,5},{8,10},{9,11},{10,... | collective-permute-start | bytes 1769480 | tf_op jit(solution)/shard_map/ppermute | solution.py:35
  475.2 26.5 %collective-permute-start.70 = (bf16[4,144,512]{2,1,0:T(8,128)(2,1)S(1)}, bf16[4,144,512]{2,1,0:T(8,128)(2,1)}, u32[]{:S(2)}, u32[]{:S(2)}) collective-permute-start(bf16[4,144,512]{2,1,0:T(8,128)(2,1)S(1)} %get-tuple-element.116), channel_id=1, source_target_pairs={{0,4},{1,5},{2,6},{3,7},{4,0},{5,1},{6,2},{7,3},{8,12},{9,13},{10,... | collective-permute-start | bytes 1769480 | tf_op jit(solution)/shard_map/ppermute | solution.py:35
  504.1 9.0 %collective-permute-start.72 = (bf16[1,144,512]{2,1,0:T(8,128)(2,1)S(1)}, bf16[1,144,512]{2,1,0:T(8,128)(2,1)S(1)}, u32[]{:S(2)}, u32[]{:S(2)}) collective-permute-start(bf16[1,144,512]{2,1,0:T(8,128)(2,1)S(1)} %get-tuple-element.119), channel_id=1, source_target_pairs={{0,8},{1,9},{2,10},{3,11},{4,12},{5,13},{6,14},{7,15},{8,0},{9,1},... | collective-permute-start | bytes 442376 | tf_op jit(solution)/shard_map/ppermute | solution.py:35
  508.3 16.5 %collective-permute-start.63 = (bf16[2,128,512]{2,1,0:T(8,128)(2,1)S(1)}, bf16[2,128,512]{2,1,0:T(8,128)(2,1)S(1)}, u32[]{:S(2)}, u32[]{:S(2)}) collective-permute-start(bf16[2,128,512]{2,1,0:T(8,128)(2,1)S(1)} %get-tuple-element.110), channel_id=1, source_target_pairs={{0,2},{1,3},{2,0},{3,1},{4,6},{5,7},{6,4},{7,5},{8,10},{9,11},{10,... | collective-permute-start | bytes 786440 | tf_op jit(solution)/shard_map/ppermute | solution.py:35
  509.5 15.3 %collective-permute-start.64 = (bf16[2,128,512]{2,1,0:T(8,128)(2,1)S(1)}, bf16[2,128,512]{2,1,0:T(8,128)(2,1)S(1)}, u32[]{:S(2)}, u32[]{:S(2)}) collective-permute-start(bf16[2,128,512]{2,1,0:T(8,128)(2,1)S(1)} %get-tuple-element.111), channel_id=1, source_target_pairs={{0,4},{1,5},{2,6},{3,7},{4,0},{5,1},{6,2},{7,3},{8,12},{9,13},{10,... | collective-permute-start | bytes 786440 | tf_op jit(solution)/shard_map/ppermute | solution.py:35
  509.6 15.2 %collective-permute-start.65 = (bf16[2,128,512]{2,1,0:T(8,128)(2,1)S(1)}, bf16[2,128,512]{2,1,0:T(8,128)(2,1)S(1)}, u32[]{:S(2)}, u32[]{:S(2)}) collective-permute-start(bf16[2,128,512]{2,1,0:T(8,128)(2,1)S(1)} %get-tuple-element.112), channel_id=1, source_target_pairs={{0,6},{1,7},{2,4},{3,5},{4,2},{5,3},{6,0},{7,1},{8,14},{9,15},{10,... | collective-permute-start | bytes 786440 | tf_op jit(solution)/shard_map/ppermute | solution.py:35
  511.0 12.4 %collective-permute-start.73 = (bf16[1,144,512]{2,1,0:T(8,128)(2,1)S(1)}, bf16[1,144,512]{2,1,0:T(8,128)(2,1)S(1)}, u32[]{:S(2)}, u32[]{:S(2)}) collective-permute-start(bf16[1,144,512]{2,1,0:T(8,128)(2,1)S(1)} %get-tuple-element.120), channel_id=1, source_target_pairs={{0,16},{1,17},{2,18},{3,19},{4,20},{5,21},{6,22},{7,23},{8,24},{9,... | collective-permute-start | bytes 442376 | tf_op jit(solution)/shard_map/ppermute | solution.py:35
  513.1 10.3 %collective-permute-start.74 = (bf16[1,144,512]{2,1,0:T(8,128)(2,1)S(1)}, bf16[1,144,512]{2,1,0:T(8,128)(2,1)S(1)}, u32[]{:S(2)}, u32[]{:S(2)}) collective-permute-start(bf16[1,144,512]{2,1,0:T(8,128)(2,1)S(1)} %get-tuple-element.121), channel_id=1, source_target_pairs={{0,24},{1,25},{2,26},{3,27},{4,28},{5,29},{6,30},{7,31},{8,16},{9,... | collective-permute-start | bytes 442376 | tf_op jit(solution)/shard_map/ppermute | solution.py:35
  531.8 9.9 %collective-permute-start.76 = (bf16[2,144,512]{2,1,0:T(8,128)(2,1)S(1)}, bf16[2,144,512]{2,1,0:T(8,128)(2,1)S(1)}, u32[]{:S(2)}, u32[]{:S(2)}) collective-permute-start(bf16[2,144,512]{2,1,0:T(8,128)(2,1)S(1)} %pad_maximum_fusion.1), channel_id=1, source_target_pairs={{0,1},{1,0},{2,3},{3,2},{4,5},{5,4},{6,7},{7,6},{8,9},{9,8},{10,11... | collective-permute-start | bytes 884744 | tf_op jit(solution)/shard_map/ppermute | solution.py:35
  (135 other events, 1064.8 us)
Sparse Core Ops, SparseCore 0:
  11.4 82.1 all-gather.9
  97.1 85.3 all-gather.5
  310.9 114.1 all-gather.7

commit v3 on v2

--- a/solution.py
+++ b/solution.py
@@ -378,33 +378,32 @@
     return gather_rows(total.reshape(total.shape[1:])).astype(F32)
 
 
-def pack_body(count, *refs):
+def pack_body(centred, *refs):
     *ins, out_ref, rows_ref = refs
     at = 0
-    for k, ref in enumerate(ins):
+    for ref in ins:
         share, width = ref.shape
         cols = slice(at, at + width)
         at += width
         values = ref[...]
         extra = jnp.sum(values, axis=0, keepdims=True)
-        if k < count:
+        if centred:
             extra = extra * (1.0 / share)
             values = values - extra
         high = extra.astype(BF16).astype(F32)
         low = extra - high
         rows_ref[:share, cols] = values
-        order = (high, high, low, low) if k < count else (high, low, high, low)
+        order = (high, high, low, low) if centred else (high, low, high, low)
         for j, row in enumerate(order):
             rows_ref[share + j : share + j + 1, cols] = row
     out_ref[...] = rows_ref[...].astype(BF16)
 
 
-def gather_products(left, right):
-    arrays = left + right
+def gather_products(arrays, centred, deps):
     widths = [a.shape[1] for a in arrays]
     rows = arrays[0].shape[0] + 4
     (packed,) = kernel_call(
-        functools.partial(pack_body, len(left)),
+        functools.partial(pack_body, centred),
         1,
         [whole_block(a) for a in arrays],
         [
@@ -416,6 +415,7 @@
         [pltpu.VMEM((rows, sum(widths)), F32)],
         tuple(arrays),
         6 * rows * sum(widths),
+        deps=deps,
     )
     return lax.all_gather(packed, BOTH, axis=0, tiled=True)
 
@@ -746,9 +746,10 @@
 
 
 def third_body(
-    height, share, h_ref, w_ref, f_ref, m_ref, c_ref, slope_ref, pool_ref, first_ref, second_ref, y_ref
+    height, share, h_ref, w_ref, f_ref, m_ref, c_ref, slope_ref, pool_ref, sums_ref, y_ref
 ):
-    crops = first_ref.shape[0]
+    crops = h_ref.shape[0] // (height * 8)
+    channels = y_ref.shape[1]
     start = pl.program_id(0) * crops
     padding = -share % 8
     pixels = height * 8
@@ -769,12 +770,13 @@
             slope_ref[at, cols] = slope.astype(BF16)
             for j in range(per_step):
                 rows = slice(j * pixels, (j + 1) * pixels)
-                crop = pl.ds(k * per_step + j, 1)
                 pooled_at = start + k * per_step + j
-                pooled_at = pooled_at + pooled_at // share * padding
-                pool_ref[pl.ds(pooled_at, 1), cols] = jnp.sum(value[rows], axis=0, keepdims=True)
-                first_ref[crop, cols] = jnp.sum(slope[rows], axis=0, keepdims=True)
-                second_ref[crop, cols] = jnp.sum(slope[rows] * y[rows], axis=0, keepdims=True)
+                at_crop = pl.ds(pooled_at + pooled_at // share * padding, 1)
+                pool_ref[at_crop, cols] = jnp.sum(value[rows], axis=0, keepdims=True)
+                sums_ref[at_crop, cols] = jnp.sum(slope[rows], axis=0, keepdims=True)
+                sums_ref[at_crop, slice(cols.start + channels, cols.stop + channels)] = jnp.sum(
+                    slope[rows] * y[rows], axis=0, keepdims=True
+                )
             return carry
 
         loop(crops // per_step, step, 0)
@@ -789,19 +791,15 @@
     consts = jnp.concatenate([tall(scale), tall(shift)], axis=0)
     rows_of = lambda n: pl.BlockSpec((flat, n), lambda k: (k, 0))
     padded = crops // share * (share + -share % 8)
-    crop_rows = (jax.ShapeDtypeStruct((crops, channels), F32), pl.BlockSpec((tile, channels), lambda k: (k, 0)))
+    kept = lambda n: (jax.ShapeDtypeStruct((padded, n), F32), pl.BlockSpec((padded, n), lambda k: (0, 0)))
     return kernel_call(
         functools.partial(third_body, height, share),
         crops // tile,
         [rows_of(width), whole_block(weight), rows_of(channels), rows_of(1), whole_block(consts)],
         [
             (jax.ShapeDtypeStruct((total, channels), BF16), rows_of(channels)),
-            (
-                jax.ShapeDtypeStruct((padded, channels), F32),
-                pl.BlockSpec((padded, channels), lambda k: (0, 0)),
-            ),
-            crop_rows,
-            crop_rows,
+            kept(channels),
+            kept(2 * channels),
         ],
         [pltpu.VMEM((flat, channels), F32)],
         (hidden, weight, features, mask_flat, consts),
@@ -1168,13 +1166,17 @@
     hidden_mean_two = sums_three[2 * channels :] / valid_count
     mean_three, spread_three = spread_of(sums_three[: 2 * channels].reshape(2, -1), valid_count)
     scale_three = gain_three * spread_three
-    slope_three, crop_sums, slope_sums, slope_dots = third_output(
+    slope_three, crop_sums, slope_sums = third_output(
         hidden_two, full_expand, flat_in, weight_col, scale_three, bias_three - mean_three * scale_three, height, share
     )
     pooled = crop_sums.reshape((2,) * len(row_bits) + (-1, channels))
     for k, step in enumerate(row_bits):
         pooled = halve(pooled, len(row_bits) - 1 - k, step, False)
     pooled = pooled[:share] / crop_count
+    slope_sums = slope_sums.reshape((2,) * len(row_bits) + (-1, 2 * channels))
+    for k, step in enumerate(row_bits):
+        slope_sums = halve(slope_sums, len(row_bits) - 1 - k, step, False)
+    slope_sums = slope_sums[:share]
 
     pre_head = split_dot(pooled, full_hidden, 0, 3)
     sums_head = total_wide(jnp.stack([jnp.sum(pre_head, axis=0), jnp.sum(pre_head * pre_head, axis=0)]))
@@ -1241,21 +1243,22 @@
     )
     grad_pooled = split_dot(grad_pre_head, full_hidden, 1, 2)
     per_pixel = grad_pooled / crop_count
-    scale_rows = lax.all_gather(per_pixel, "rows", axis=0, tiled=True)
+    scale_rows = gather_rows(per_pixel)
 
     crop_index = lax.axis_index("crops")
     proto_pad = -proto_total % 128
-    products = gather_products(
-        [pooled, hidden_head, unit_embed],
+    forward_all = gather_products([pooled, hidden_head, unit_embed], True, ())
+    backward_all = gather_products(
         [grad_pre_head, grad_embedding, jnp.pad(grad_scores, ((0, 0), (0, proto_pad)))],
+        False,
+        (slope_sums, forward_all),
     )
     shard_hidden, shard_embed, width = w_hidden.shape[0], w_embed.shape[0], w_embed.shape[1]
-    right_at = channels + hidden_cols + width
 
     def product_of(at, size, to, count):
         return lax.dot_general(
-            lax.dynamic_slice_in_dim(products, at, size, 1),
-            lax.slice_in_dim(products, right_at + to, right_at + to + count, axis=1),
+            lax.dynamic_slice_in_dim(forward_all, at, size, 1),
+            lax.slice_in_dim(backward_all, to, to + count, axis=1),
             TN,
             preferred_element_type=F32,
         )
@@ -1264,9 +1267,7 @@
     out_embed = product_of(channels + crop_index * shard_embed, shard_embed, hidden_cols, width)
     grad_prototypes = product_of(channels + hidden_cols, width, hidden_cols + width, proto_total)
 
-    sums_three_back = jnp.concatenate(
-        [jnp.sum(scale_rows * slope_sums, axis=0), jnp.sum(scale_rows * slope_dots, axis=0)]
-    )
+    sums_three_back = jnp.sum(jnp.concatenate([per_pixel, per_pixel], axis=1) * slope_sums, axis=0)
     sums_three_back = total_wide(sums_three_back[None])[0]
     grad_bias_three = sums_three_back[:channels]
     alpha, beta, gamma, grad_gain_three = back_consts(

time: 560 us -> 543 us (0.970)
  blocking collectives: 66.3 us -> 49.1 us
    all_gather x1 -> x0, blocking collectives: 14.4 us -> none  [shards(): scale_rows = lax.all_gather(per_pixel, 'rows', axis=0, tiled=True)]
    all_to_all x3, waiting for transfers between devices: 6.93 us -> 17 us  [total_narrow(): return jnp.sum(lax.all_to_all(copies, BOTH, 0, 0, tiled=True), axis=0)]
    ppermute x2, waiting for transfers between devices: 8.59 us -> 0.01 us  [edge_rows(): above = lax.ppermute(planes[-1], 'rows', [(i, i + 1) for i in range(ends)])]
    ppermute x73 -> x77, starting transfers between devices: 98 us -> 104 us  [xor_permute(): return lax.ppermute(values, BOTH, pairs)]
    pallas_call x13 -> x14, Pallas kernels: 120 us -> 120 us  [kernel_call(): pl.pallas_call(inner, grid=(grid,), in_specs=ins + [pl.BlockSpec(memory_s...]
    ppermute x73 -> x77, waiting for transfers between devices: 58.2 us -> 58.1 us  [xor_permute(): return lax.ppermute(values, BOTH, pairs)]
    all_gather x1 -> x2, starting transfers between devices: 12.3 us -> 12.3 us  [gather_products(): return lax.all_gather(packed, BOTH, axis=0, tiled=True)]
  transfers between devices with their start and end apart: 83 -> 88, of which waited for: 42 -> 41; matrix products, arithmetic and copies ran while one was open for 14% -> 15% of each run, Pallas kernels for 26% -> 27%
where the time goes in v3:
time: 543 us; the launch traced here: 534 us
  Pallas kernels  145 us (27%)
  starting transfers between devices  139 us (26%)
  waiting for transfers between devices  80.3 us (15%)
  blocking collectives  49.1 us (9%)
  matrix products  40.2 us (7%)
  local copies, waits for them, and re-layouts  35.4 us (7%)
  other arithmetic  27.6 us (5%)
  between operations  16.6 us (3%)
    pallas_call x14, Pallas kernels, kernel_call(): pl.pallas_call(inner, grid=(grid,), in_specs=ins + [pl.BlockSpec(memory_s...  120 us
    ppermute x77, starting transfers between devices, xor_permute(): return lax.ppermute(values, BOTH, pairs)  104 us
    ppermute x77, waiting for transfers between devices, xor_permute(): return lax.ppermute(values, BOTH, pairs)  58.1 us
    all_to_all x1, blocking collectives, gather_first(): lax.all_to_all(jnp.broadcast_to(mine[None], (crop_total, size, cols)), 'c...  38.5 us
    pallas_call x11, Pallas kernels, merge_split(): pl.pallas_call(body, grid_spec=pltpu.PrefetchScalarGridSpec(num_scalar_pr...  25.4 us
    all_to_all x3, waiting for transfers between devices, total_narrow(): return jnp.sum(lax.all_to_all(copies, BOTH, 0, 0, tiled=True), axis=0)  17 us
    all_to_all x3, starting transfers between devices, total_narrow(): return jnp.sum(lax.all_to_all(copies, BOTH, 0, 0, tiled=True), axis=0)  13.7 us
    dot_general x4, matrix products, split_dot(): lax.dot_general(split_parts(x, parts), matrix, (((1,), (dim,)), ((), ()))...  13.6 us
  transfers between devices with their start and end apart: 88, of which 41 were waited for; matrix products, arithmetic and copies ran while one was open for 15% of the time, Pallas kernels for 27%

profile of v3, /device:TPU:1, one launch (start us, length us, event | category | flops | bytes accessed | tf_op | source)
XLA Modules:
  0.0 533.8 jit_solution(2568284707450733778)
XLA Ops:
  12.6 38.5 %all_to_all.25 = bf16[8,128,512]{2,1,0:T(8,128)(2,1)S(1)} all-to-all(bf16[8,128,512]{2,1,0:T(8,128)(2,1)S(1)} %broadcast_in_dim.68), channel_id=1, replica_groups=mesh['crops'=8,'rows'=4] {'crops'}, dimensions={0} | all-to-all | bytes 2097152 | tf_op jit(solution)/shard_map/all_to_all | solution.py:136
  59.5 7.8 %multiply_reduce_fusion = (f32[512]{0:T(512)S(1)}, f32[512]{0:T(512)S(1)}, f32[1280,512]{0,1:T(8,128)}) fusion(f32[1280]{0:T(1024)S(1)} %convert_element_type.79, bf16[2048,512]{1,0:T(8,128)(2,1)S(1)} %bitcast.219, bf16[1280,2048]{1,0:T(8,128)(2,1)} %bitcast.222), kind=kOutput, calls=%fused_computation.8 | convolution fusion | flops 2686974976 | bytes 9970688 | tf_op jit(solution)/shard_map/dot_general | solution.py:1137
  80.5 6.9 %all-to-all-done.1 = f32[32,3,512]{2,1,0:T(4,128)S(1)} async-done(((f32[32,3,512]{2,1,0:T(4,128)}), f32[32,3,512]{2,1,0:T(4,128)S(1)}, u32[]{:S(2)}, u32[]{:S(2)}) %all-to-all-start.1) | async-done | bytes 196640 | tf_op jit(solution)/shard_map/all_to_all | solution.py:91
  89.9 6.1 %shard_map.297 = (bf16[640,512]{1,0:T(8,128)(2,1)}, bf16[640,512]{1,0:T(8,128)(2,1)}, f32[2,640,512]{2,1,0:T(8,128)}, f32[8,512]{1,0:T(8,128)S(1)}) custom-call(f32[80,2,8,512]{3,2,1,0:T(8,128)} %bitcast.210, f32[2,640,1]{2,1,0:T(8,128)} %convert_element_type.104.refs_1_.refs_4_.refs_2_, f32[32,512]{1,0:T(8,128)S(1)} %pad_maximum_fusion.10.refs_2_, ...), custom_call_target="tpu_custom_call" | custom-call | flops 26214400 | bytes 6640640 | tf_op jit(solution)/shard_map/pallas_call | solution.py:208
  101.4 8.9 %shard_map.298.refs_0_ = f32[2,640,512]{2,1,0:T(8,128)} custom-call(bf16[640,512]{1,0:T(8,128)(2,1)} %get-tuple-element.68.refs_0_, bf16[640,512]{1,0:T(8,128)(2,1)} %get-tuple-element.69.refs_1_, bf16[32,208,512]{2,1,0:T(8,128)(2,1)} %bitcast.213), custom_call_target="tpu_custom_call" | custom-call | flops 4026531840 | bytes 10747904 | tf_op jit(solution)/shard_map/pallas_call | solution.py:208
  113.9 8.9 %shard_map.299 = (f32[2,640,512]{2,1,0:T(8,128)}, f32[8,512]{1,0:T(8,128)S(1)}, f32[8,512]{1,0:T(8,128)S(1)}) custom-call(f32[2,640,512]{2,1,0:T(8,128)} %shard_map.298.refs_0_, bf16[640,512]{1,0:T(8,128)(2,1)S(1)} %collective-permute-done.1.refs_1_.refs_2_, bf16[640,512]{1,0:T(8,128)(2,1)S(1)} %collective-permute-done.2.refs_2_.refs_3_, ...), custom_call_target="tpu_custom_call" | custom-call | flops 2013265920 | bytes 13407232 | tf_op jit(solution)/shard_map/pallas_call | solution.py:208
  132.7 10.0 %all-to-all-done.2 = f32[32,3,512]{2,1,0:T(4,128)S(1)} async-done(((f32[32,3,512]{2,1,0:T(4,128)}), f32[32,3,512]{2,1,0:T(4,128)S(1)}, u32[]{:S(2)}, u32[]{:S(2)}) %all-to-all-start.2) | async-done | bytes 196640 | tf_op jit(solution)/shard_map/all_to_all | solution.py:91
  144.7 8.2 %shard_map.300 = (bf16[1280,512]{1,0:T(8,128)(2,1)}, f32[2,640,512]{2,1,0:T(8,128)}, f32[8,2048]{1,0:T(8,128)S(1)}, f32[8,2048]{1,0:T(8,128)S(1)}, f32[8,512]{1,0:T(8,128)S(1)}) custom-call(f32[2,640,512]{2,1,0:T(8,128)} %get-tuple-element.70.refs_0_.refs_7_.refs_1_, f32[1280,1]{1,0:T(8,128)S(1)} %convert_element_type.105.refs_1_.refs_3_.refs_2_, ...), custom_call_target="tpu_custom_call" | custom-call | flops 2684354560 | bytes 8868864 | tf_op jit(solution)/shard_map/pallas_call | solution.py:208
  169.2 17.0 %shard_map.301 = (bf16[1280,2048]{1,0:T(8,128)(2,1)}, f32[96,2048]{1,0:T(8,128)S(1)}, f32[96,4096]{1,0:T(8,128)}) custom-call(bf16[1280,512]{1,0:T(8,128)(2,1)} %get-tuple-element.74.refs_0_, bf16[4,512,512]{2,1,0:T(8,128)(2,1)} %bitcast.230, bf16[1280,2048]{1,0:T(8,128)(2,1)} %bitcast.223, f32[1280,1]{1,0:T(8,128)S(1)} %convert_element_type.105.refs_1_.refs_3_.refs_2_, ...), custom_call_target="tpu_custom_call" | custom-call | flops 2789212160 | bytes 16520192 | tf_op jit(solution)/shard_map/pallas_call | solution.py:208
  201.5 5.0 fusion.2
  233.5 12.0 %all-gather.10.cloned.1.call-start = ((), (), s32[]{:S(2)}) async-start(), calls=%async_computation.7 | async-start | bytes 8312832 | tf_op jit(solution)/shard_map/all_gather | solution.py:420
  311.0 6.0 %fusion = f32[40,2048]{1,0:T(8,128)S(1)} fusion(bf16[2048,2176]{1,0:T(8,128)(2,1)} %all-gather.6.cloned.1.call-done, bf16[20,2048]{1,0:T(8,128)(2,1)S(1)} %fusion.33, bf16[20,2048]{1,0:T(8,128)(2,1)S(1)} %get-tuple-element.145), kind=kOutput, calls=%fused_computation.1 | convolution fusion | flops 335872000 | bytes 8880128 | tf_op jit(solution)/shard_map/dot_general | solution.py:184
  342.7 15.2 %shard_map.302 = (bf16[2048,512]{1,0:T(8,128)(2,1)}, f32[8,2048]{1,0:T(8,128)S(1)}, f32[2,640,512]{2,1,0:T(8,128)}, f32[8,512]{1,0:T(8,128)S(1)}, f32[8,512]{1,0:T(8,128)S(1)}) custom-call(bf16[1280,512]{1,0:T(8,128)(2,1)} %get-tuple-element.74.refs_0_, bf16[4,512,512]{2,1,0:T(8,128)(2,1)} %bitcast.231, bf16[1280,2048]{1,0:T(8,128)(2,1)} %get-tuple-element.79.refs_2_, ...), custom_call_target="tpu_custom_call" | custom-call | flops 8053063680 | bytes 19635200 | tf_op jit(solution)/shard_map/pallas_call | solution.py:208
  358.0 10.6 %all_to_all.26 = f32[32,2,512]{2,1,0:T(2,128)S(1)} all-to-all(f32[32,2,512]{2,1,0:T(2,128)S(1)} %broadcast_in_dim.84), channel_id=1, replica_groups=mesh['crops'=8,'rows'=4] {'crops','rows'}, dimensions={0} | all-to-all | bytes 262144 | tf_op jit(solution)/shard_map/all_to_all | solution.py:91
  370.0 5.2 shard_map.303
  379.8 8.8 %shard_map.304.refs_0_ = f32[2,640,512]{2,1,0:T(8,128)} custom-call(bf16[640,512]{1,0:T(8,128)(2,1)S(1)} %get-tuple-element.85.refs_0_.refs_4_, bf16[640,512]{1,0:T(8,128)(2,1)} %get-tuple-element.86.refs_1_.refs_5_, bf16[32,208,512]{2,1,0:T(8,128)(2,1)} %bitcast.216), custom_call_target="tpu_custom_call" | custom-call | flops 4026531840 | bytes 10747904 | tf_op jit(solution)/shard_map/pallas_call | solution.py:208
  390.0 8.5 %shard_map.305 = (f32[2,640,512]{2,1,0:T(8,128)}, f32[8,512]{1,0:T(8,128)S(1)}, f32[8,512]{1,0:T(8,128)S(1)}) custom-call(f32[2,640,512]{2,1,0:T(8,128)} %shard_map.304.refs_0_, bf16[640,512]{1,0:T(8,128)(2,1)S(1)} %collective-permute-done.60.refs_1_, bf16[640,512]{1,0:T(8,128)(2,1)S(1)} %collective-permute-done.61.refs_2_, bf16[32,208,512]{2,1,0:T(8,128)(2,1)} %bitcast.217, ...), custom_call_target="tpu_custom_call" | custom-call | flops 2013265920 | bytes 18644992 | tf_op jit(solution)/shard_map/pallas_call | solution.py:208
  399.4 5.0 all-to-all-start.4
  404.4 13.2 %shard_map.306 = bf16[3,3,512,512]{3,2,1,0:T(8,128)(2,1)} custom-call(bf16[640,512]{1,0:T(8,128)(2,1)} %get-tuple-element.68.refs_0_, bf16[640,512]{1,0:T(8,128)(2,1)} %get-tuple-element.69.refs_1_, bf16[640,512]{1,0:T(8,128)(2,1)} %copy-done.6, bf16[640,512]{1,0:T(8,128)(2,1)} %copy-done.7, bf16[640,512]{1,0:T(8,128)(2,1)} %copy-done.9, ...), custom_call_target="tpu_custom_call" | custom-call | flops 6039797760 | bytes 8654848 | tf_op jit(solution)/shard_map/pallas_call | solution.py:208
  428.6 9.2 %shard_map.308 = (bf16[1280,512]{1,0:T(8,128)(2,1)}, bf16[2048,512]{1,0:T(8,128)(2,1)}) custom-call(f32[2,640,512]{2,1,0:T(8,128)} %get-tuple-element.88.refs_8_.refs_0_, f32[80,2,8,512]{3,2,1,0:T(8,128)} %bitcast.212, f32[1280,1]{1,0:T(8,128)S(1)} %convert_element_type.105.refs_1_.refs_3_.refs_2_, f32[48,512]{1,0:T(8,128)S(1)} %pad_maximum_fusion.9.refs_3_, ...), custom_call_target="tpu_custom_call" | custom-call | flops 2684354560 | bytes 13997056 | tf_op jit(solution)/shard_map/pallas_call | solution.py:208
  457.4 5.5 %fusion.4 = f32[128,3000]{0,1:T(8,128)} fusion(bf16[768,5248]{1,0:T(8,128)(2,1)} %all-gather.10.cloned.1.call-done, bf16[768,4224]{1,0:T(8,128)(2,1)} %all-gather.8.cloned.1.call-done.refs_4_), kind=kOutput, calls=%fused_computation.5 | convolution fusion | flops 589824000 | bytes 6451200 | tf_op jit(solution)/shard_map/dot_general | solution.py:1259
  471.6 9.1 %shard_map.316.refs_4_ = bf16[1280,2048]{1,0:T(8,128)(2,1)} custom-call(bf16[1280,512]{1,0:T(8,128)(2,1)} %get-tuple-element.94.refs_0_, bf16[2048,512]{1,0:T(8,128)(2,1)} %bitcast.220, bf16[1280,2048]{1,0:T(8,128)(2,1)} %get-tuple-element.79.refs_2_, f32[80,2048]{1,0:T(8,128)} %copy-done.13, f32[256,2048]{1,0:T(8,128)} %fusion.8.refs_4_, ...), custom_call_target="tpu_custom_call" | custom-call | flops 2684354560 | bytes 14548992 | tf_op jit(solution)/shard_map/pallas_call | solution.py:208
  502.9 7.0 %collective-permute-start.70 = (bf16[1,128,512]{2,1,0:T(8,128)(2,1)S(1)}, bf16[1,128,512]{2,1,0:T(8,128)(2,1)S(1)}, u32[]{:S(2)}, u32[]{:S(2)}) collective-permute-start(bf16[1,128,512]{2,1,0:T(8,128)(2,1)S(1)} %get-tuple-element.112), channel_id=1, source_target_pairs={{0,16},{1,17},{2,18},{3,19},{4,20},{5,21},{6,22},{7,23},{8,24},{9,... | collective-permute-start | bytes 393224 | tf_op jit(solution)/shard_map/ppermute | solution.py:35
  510.0 6.2 %collective-permute-done.70 = bf16[1,128,512]{2,1,0:T(8,128)(2,1)S(1)} collective-permute-done((bf16[1,128,512]{2,1,0:T(8,128)(2,1)S(1)}, bf16[1,128,512]{2,1,0:T(8,128)(2,1)S(1)}, u32[]{:S(2)}, u32[]{:S(2)}) %collective-permute-start.70) | collective-permute-done | bytes 131104 | tf_op jit(solution)/shard_map/ppermute | solution.py:35
  (539 shorter events, 278.3 us)
Async XLA Ops:
  7.2 94.1 %all-gather.12.cloned.1.call-start = ((), (), s32[]{:S(2)}) async-start(), calls=%async_computation.8 | async-start | bytes 7028736 | tf_op jit(solution)/shard_map/all_gather | solution.py:151
  10.0 191.5 %all-gather.6.cloned.1.call-start = ((), (), s32[]{:S(2)}) async-start(), calls=%async_computation.5 | async-start | bytes 9191424 | tf_op jit(solution)/shard_map/all_gather | solution.py:1115
  68.2 19.2 %all-to-all-start.1 = ((f32[32,3,512]{2,1,0:T(4,128)}), f32[32,3,512]{2,1,0:T(4,128)S(1)}, u32[]{:S(2)}, u32[]{:S(2)}) async-start(f32[32,3,512]{2,1,0:T(4,128)} %broadcast_in_dim.69), calls=%async_computation.1 | async-start | bytes 524288 | tf_op jit(solution)/shard_map/all_to_all | solution.py:91
  96.0 14.3 %collective-permute-start.1 = (bf16[640,512]{1,0:T(8,128)(2,1)}, bf16[640,512]{1,0:T(8,128)(2,1)S(1)}, u32[]{:S(2)}, u32[]{:S(2)}) collective-permute-start(bf16[640,512]{1,0:T(8,128)(2,1)} %get-tuple-element.69.refs_1_), channel_id=1, source_target_pairs={{0,1},{1,2},{2,3},{4,5},{5,6},{6,7},{8,9},{9,10},{10,11},{12,13},{... | collective-permute-start | bytes 1966088 | tf_op jit(solution)/shard_map/ppermute | solution.py:1074
  99.4 14.5 %collective-permute-start.2 = (bf16[640,512]{1,0:T(8,128)(2,1)}, bf16[640,512]{1,0:T(8,128)(2,1)S(1)}, u32[]{:S(2)}, u32[]{:S(2)}) collective-permute-start(bf16[640,512]{1,0:T(8,128)(2,1)} %get-tuple-element.68.refs_0_), channel_id=1, source_target_pairs={{1,0},{2,1},{3,2},{5,4},{6,5},{7,6},{9,8},{10,9},{11,10},{13,12},{... | collective-permute-start | bytes 1966088 | tf_op jit(solution)/shard_map/ppermute | solution.py:1075
  123.6 19.1 %all-to-all-start.2 = ((f32[32,3,512]{2,1,0:T(4,128)}), f32[32,3,512]{2,1,0:T(4,128)S(1)}, u32[]{:S(2)}, u32[]{:S(2)}) async-start(f32[32,3,512]{2,1,0:T(4,128)} %broadcast_in_dim.72), calls=%async_computation.2 | async-start | bytes 524288 | tf_op jit(solution)/shard_map/all_to_all | solution.py:91
  127.8 189.4 %all-gather.8.cloned.1.call-start = ((), (), s32[]{:S(2)}) async-start(), calls=%async_computation.6 | async-start | bytes 6690816 | tf_op jit(solution)/shard_map/all_gather | solution.py:420
  229.3 16.3 %collective-permute-start.23 = (f32[1,3000]{1,0:T(1,128)S(1)}, f32[1,3000]{1,0:T(1,128)S(1)}, u32[]{:S(2)}, u32[]{:S(2)}) collective-permute-start(f32[1,3000]{1,0:T(1,128)S(1)} %slice_add_fusion.8), channel_id=1, source_target_pairs={{0,4},{1,5},{2,6},{3,7},{4,0},{5,1},{6,2},{7,3},{8,12},{9,13},{10,... | collective-permute-start | bytes 36008 | tf_op jit(solution)/shard_map/ppermute | solution.py:35
  231.1 14.5 %collective-permute-start.24 = (f32[1,3000]{1,0:T(1,128)S(1)}, f32[1,3000]{1,0:T(1,128)S(1)}, u32[]{:S(2)}, u32[]{:S(2)}) collective-permute-start(f32[1,3000]{1,0:T(1,128)S(1)} %slice_add_fusion.8), channel_id=1, source_target_pairs={{0,6},{1,7},{2,4},{3,5},{4,2},{5,3},{6,0},{7,1},{8,14},{9,15},{10,... | collective-permute-start | bytes 36008 | tf_op jit(solution)/shard_map/ppermute | solution.py:35
  231.4 14.2 %collective-permute-start.22 = (f32[1,8120]{1,0:T(1,128)S(1)}, f32[1,8120]{1,0:T(1,128)S(1)}, u32[]{:S(2)}, u32[]{:S(2)}) collective-permute-start(f32[1,8120]{1,0:T(1,128)S(1)} %concatenate.63), channel_id=1, source_target_pairs={{0,2},{1,3},{2,0},{3,1},{4,6},{5,7},{6,4},{7,5},{8,10},{9,11},{10,... | collective-permute-start | bytes 97448 | tf_op jit(solution)/shard_map/ppermute | solution.py:35
  233.5 223.8 %all-gather.10.cloned.1.call-start = ((), (), s32[]{:S(2)}) async-start(), calls=%async_computation.7 | async-start | bytes 8312832 | tf_op jit(solution)/shard_map/all_gather | solution.py:420
  280.4 19.1 %collective-permute-start.51 = (f32[2,24,4096]{2,1,0:T(8,128)}, f32[2,24,4096]{2,1,0:T(8,128)}, u32[]{:S(2)}, u32[]{:S(2)}) collective-permute-start(f32[2,24,4096]{2,1,0:T(8,128)} %dynamic-slice_bitcast_fusion), channel_id=1, source_target_pairs={{0,1},{1,0},{2,3},{3,2},{4,5},{5,4},{6,7},{7,6},{8,9},{9,8},{10,11... | collective-permute-start | bytes 2359304 | tf_op jit(solution)/shard_map/ppermute | solution.py:35
  375.2 13.4 %collective-permute-start.60 = (bf16[640,512]{1,0:T(8,128)(2,1)}, bf16[640,512]{1,0:T(8,128)(2,1)S(1)}, u32[]{:S(2)}, u32[]{:S(2)}) collective-permute-start(bf16[640,512]{1,0:T(8,128)(2,1)} %get-tuple-element.86.refs_1_.refs_5_), channel_id=1, source_target_pairs={{0,1},{1,2},{2,3},{4,5},{5,6},{6,7},{8,9},{9,10},{10,11},{12,13},{... | collective-permute-start | bytes 1966088 | tf_op jit(solution)/shard_map/ppermute | solution.py:1074
  399.4 27.3 %all-to-all-start.4 = ((f32[32,7,512]{2,1,0:T(8,128)}), f32[32,7,512]{2,1,0:T(8,128)S(1)}, u32[]{:S(2)}, u32[]{:S(2)}) async-start(f32[32,7,512]{2,1,0:T(8,128)} %broadcast_in_dim.88), calls=%async_computation.4 | async-start | bytes 1048576 | tf_op jit(solution)/shard_map/all_to_all | solution.py:91
  422.5 27.8 %collective-permute-start.62 = (bf16[16,144,512]{2,1,0:T(8,128)(2,1)}, bf16[16,144,512]{2,1,0:T(8,128)(2,1)}, u32[]{:S(2)}, u32[]{:S(2)}) collective-permute-start(bf16[16,144,512]{2,1,0:T(8,128)(2,1)} %get-tuple-element.95), channel_id=1, source_target_pairs={{0,1},{1,0},{2,3},{3,2},{4,5},{5,4},{6,7},{7,6},{8,9},{9,8},{10,11... | collective-permute-start | bytes 7077896 | tf_op jit(solution)/shard_map/ppermute | solution.py:35
  426.3 15.2 %collective-permute-start.64 = (bf16[16,64,512]{2,1,0:T(8,128)(2,1)}, bf16[16,64,512]{2,1,0:T(8,128)(2,1)S(1)}, u32[]{:S(2)}, u32[]{:S(2)}) collective-permute-start(bf16[16,64,512]{2,1,0:T(8,128)(2,1)} %get-tuple-element.103), channel_id=1, source_target_pairs={{0,1},{1,0},{2,3},{3,2},{4,5},{5,4},{6,7},{7,6},{8,9},{9,8},{10,11... | collective-permute-start | bytes 3145736 | tf_op jit(solution)/shard_map/ppermute | solution.py:35
  445.1 41.3 %collective-permute-start.66 = (bf16[2,256,512]{2,1,0:T(8,128)(2,1)}, bf16[2,256,512]{2,1,0:T(8,128)(2,1)}, u32[]{:S(2)}, u32[]{:S(2)}) collective-permute-start(bf16[2,256,512]{2,1,0:T(8,128)(2,1)} %get-tuple-element.106), channel_id=1, source_target_pairs={{0,8},{1,9},{2,10},{3,11},{4,12},{5,13},{6,14},{7,15},{8,0},{9,1},... | collective-permute-start | bytes 1572872 | tf_op jit(solution)/shard_map/ppermute | solution.py:35
  450.3 36.2 %collective-permute-start.65 = (bf16[2,256,512]{2,1,0:T(8,128)(2,1)}, bf16[2,256,512]{2,1,0:T(8,128)(2,1)}, u32[]{:S(2)}, u32[]{:S(2)}) collective-permute-start(bf16[2,256,512]{2,1,0:T(8,128)(2,1)} %get-tuple-element.105), channel_id=1, source_target_pairs={{0,8},{1,9},{2,10},{3,11},{4,12},{5,13},{6,14},{7,15},{8,0},{9,1},... | collective-permute-start | bytes 1572872 | tf_op jit(solution)/shard_map/ppermute | solution.py:35
  454.7 26.0 %collective-permute-start.73 = (bf16[4,144,512]{2,1,0:T(8,128)(2,1)S(1)}, bf16[4,144,512]{2,1,0:T(8,128)(2,1)S(1)}, u32[]{:S(2)}, u32[]{:S(2)}) collective-permute-start(bf16[4,144,512]{2,1,0:T(8,128)(2,1)S(1)} %get-tuple-element.113), channel_id=1, source_target_pairs={{0,2},{1,3},{2,0},{3,1},{4,6},{5,7},{6,4},{7,5},{8,10},{9,11},{10,... | collective-permute-start | bytes 1769480 | tf_op jit(solution)/shard_map/ppermute | solution.py:35
  456.1 24.6 %collective-permute-start.74 = (bf16[4,144,512]{2,1,0:T(8,128)(2,1)S(1)}, bf16[4,144,512]{2,1,0:T(8,128)(2,1)}, u32[]{:S(2)}, u32[]{:S(2)}) collective-permute-start(bf16[4,144,512]{2,1,0:T(8,128)(2,1)S(1)} %get-tuple-element.114), channel_id=1, source_target_pairs={{0,4},{1,5},{2,6},{3,7},{4,0},{5,1},{6,2},{7,3},{8,12},{9,13},{10,... | collective-permute-start | bytes 1769480 | tf_op jit(solution)/shard_map/ppermute | solution.py:35
  457.3 25.1 %collective-permute-start.75 = (bf16[4,144,512]{2,1,0:T(8,128)(2,1)}, bf16[4,144,512]{2,1,0:T(8,128)(2,1)}, u32[]{:S(2)}, u32[]{:S(2)}) collective-permute-start(bf16[4,144,512]{2,1,0:T(8,128)(2,1)} %get-tuple-element.115), channel_id=1, source_target_pairs={{0,6},{1,7},{2,4},{3,5},{4,2},{5,3},{6,0},{7,1},{8,14},{9,15},{10,... | collective-permute-start | bytes 1769480 | tf_op jit(solution)/shard_map/ppermute | solution.py:35
  489.3 13.4 %collective-permute-start.67 = (bf16[2,128,512]{2,1,0:T(8,128)(2,1)S(1)}, bf16[2,128,512]{2,1,0:T(8,128)(2,1)S(1)}, u32[]{:S(2)}, u32[]{:S(2)}) collective-permute-start(bf16[2,128,512]{2,1,0:T(8,128)(2,1)S(1)} %get-tuple-element.108), channel_id=1, source_target_pairs={{0,2},{1,3},{2,0},{3,1},{4,6},{5,7},{6,4},{7,5},{8,10},{9,11},{10,... | collective-permute-start | bytes 786440 | tf_op jit(solution)/shard_map/ppermute | solution.py:35
  501.5 15.1 %collective-permute-start.79 = (bf16[144,512]{1,0:T(8,128)(2,1)S(1)}, bf16[144,512]{1,0:T(8,128)(2,1)S(1)}, u32[]{:S(2)}, u32[]{:S(2)}) collective-permute-start(bf16[144,512]{1,0:T(8,128)(2,1)S(1)} %bitcast.195), channel_id=1, source_target_pairs={{0,2},{1,3},{2,0},{3,1},{4,6},{5,7},{6,4},{7,5},{8,10},{9,11},{10,... | collective-permute-start | bytes 442376 | tf_op jit(solution)/shard_map/ppermute | solution.py:35
  502.9 13.2 %collective-permute-start.70 = (bf16[1,128,512]{2,1,0:T(8,128)(2,1)S(1)}, bf16[1,128,512]{2,1,0:T(8,128)(2,1)S(1)}, u32[]{:S(2)}, u32[]{:S(2)}) collective-permute-start(bf16[1,128,512]{2,1,0:T(8,128)(2,1)S(1)} %get-tuple-element.112), channel_id=1, source_target_pairs={{0,16},{1,17},{2,18},{3,19},{4,20},{5,21},{6,22},{7,23},{8,24},{9,... | collective-permute-start | bytes 393224 | tf_op jit(solution)/shard_map/ppermute | solution.py:35
  (133 other events, 1048.4 us)
Sparse Core Ops, SparseCore 0:
  11.4 82.1 all-gather.11
  97.1 84.0 all-gather.5
  233.7 69.7 all-gather.7
  318.2 77.9 all-gather.9

commit v4 on v3

--- a/solution.py
+++ b/solution.py
@@ -1290,8 +1290,9 @@
     alpha, beta, gamma, grad_gain_two = back_consts(
         gain_two, mean_two, spread_two, valid_count, grad_bias_two, sums_two_back[1]
     )
+    expand_core = core_exchange(grad_w_expand)
     grad_pre_two, total_two = second_back(
-        grad_act_two, pre_two, mask_planes, alpha, beta, gamma, ()
+        grad_act_two, pre_two, mask_planes, alpha, beta, gamma, (expand_core[0],)
     )
     above_two, below_two = edge_rows(grad_pre_two)
     part_one = conv_local(grad_pre_two, full_spatial, True)
@@ -1324,7 +1325,8 @@
     )
     near = near_exchange([spatial_core], [spatial_rows])
     lines = [
-        line_exchange(core_exchange(g), n) for g, n in zip((grad_w_reduce, grad_w_expand), lane_rows)
+        line_exchange(parts, n)
+        for parts, n in zip((core_exchange(grad_w_reduce), expand_core), lane_rows)
     ]
     grad_features = last_grads(
         grad_pre_one,

time: 543 us -> 540 us (level)
  blocking collectives: 49.1 us -> 38.5 us
    all_to_all x1 -> x0, blocking collectives: 10.6 us -> none  [total_narrow(): return jnp.sum(lax.all_to_all(copies, BOTH, 0, 0, tiled=True), axis=0)]
    all_to_all x3 -> x4, waiting for transfers between devices: 17 us -> 21.6 us  [total_narrow(): return jnp.sum(lax.all_to_all(copies, BOTH, 0, 0, tiled=True), axis=0)]
    all_to_all x3 -> x4, starting transfers between devices: 13.7 us -> 15.3 us  [total_narrow(): return jnp.sum(lax.all_to_all(copies, BOTH, 0, 0, tiled=True), axis=0)]
  transfers between devices with their start and end apart: 88 -> 89, of which waited for: 41 -> 42; matrix products, arithmetic and copies ran while one was open for 15% -> 15% of each run, Pallas kernels for 27% -> 27%
where the time goes in v4:
time: 540 us; the launch traced here: 530 us
  Pallas kernels  145 us (27%)
  starting transfers between devices  141 us (26%)
  waiting for transfers between devices  84.6 us (16%)
  matrix products  40.2 us (7%)
  blocking collectives  38.5 us (7%)
  local copies, waits for them, and re-layouts  36 us (7%)
  other arithmetic  27.7 us (5%)
  between operations  16.6 us (3%)
    pallas_call x14, Pallas kernels, kernel_call(): pl.pallas_call(inner, grid=(grid,), in_specs=ins + [pl.BlockSpec(memory_s...  120 us
    ppermute x77, starting transfers between devices, xor_permute(): return lax.ppermute(values, BOTH, pairs)  104 us
    ppermute x77, waiting for transfers between devices, xor_permute(): return lax.ppermute(values, BOTH, pairs)  58 us
    all_to_all x1, blocking collectives, gather_first(): lax.all_to_all(jnp.broadcast_to(mine[None], (crop_total, size, cols)), 'c...  38.5 us
    pallas_call x11, Pallas kernels, merge_split(): pl.pallas_call(body, grid_spec=pltpu.PrefetchScalarGridSpec(num_scalar_pr...  25.4 us
    all_to_all x4, waiting for transfers between devices, total_narrow(): return jnp.sum(lax.all_to_all(copies, BOTH, 0, 0, tiled=True), axis=0)  21.6 us
    all_to_all x4, starting transfers between devices, total_narrow(): return jnp.sum(lax.all_to_all(copies, BOTH, 0, 0, tiled=True), axis=0)  15.3 us
    dot_general x4, matrix products, split_dot(): lax.dot_general(split_parts(x, parts), matrix, (((1,), (dim,)), ((), ()))...  13.6 us
  transfers between devices with their start and end apart: 89, of which 42 were waited for; matrix products, arithmetic and copies ran while one was open for 15% of the time, Pallas kernels for 27%

profile of v4, /device:TPU:1, one launch (start us, length us, event | category | flops | bytes accessed | tf_op | source)
XLA Modules:
  0.0 530.0 jit_solution(18097897660861401836)
XLA Ops:
  12.6 38.5 %all_to_all.25 = bf16[8,128,512]{2,1,0:T(8,128)(2,1)S(1)} all-to-all(bf16[8,128,512]{2,1,0:T(8,128)(2,1)S(1)} %broadcast_in_dim.68), channel_id=1, replica_groups=mesh['crops'=8,'rows'=4] {'crops'}, dimensions={0} | all-to-all | bytes 2097152 | tf_op jit(solution)/shard_map/all_to_all | solution.py:136
  59.5 7.8 %multiply_reduce_fusion = (f32[512]{0:T(512)S(1)}, f32[512]{0:T(512)S(1)}, f32[1280,512]{0,1:T(8,128)}) fusion(f32[1280]{0:T(1024)S(1)} %convert_element_type.79, bf16[2048,512]{1,0:T(8,128)(2,1)S(1)} %bitcast.219, bf16[1280,2048]{1,0:T(8,128)(2,1)} %bitcast.222), kind=kOutput, calls=%fused_computation.8 | convolution fusion | flops 2686974976 | bytes 9970688 | tf_op jit(solution)/shard_map/dot_general | solution.py:1137
  80.5 7.0 %all-to-all-done.1 = f32[32,3,512]{2,1,0:T(4,128)S(1)} async-done(((f32[32,3,512]{2,1,0:T(4,128)}), f32[32,3,512]{2,1,0:T(4,128)S(1)}, u32[]{:S(2)}, u32[]{:S(2)}) %all-to-all-start.1) | async-done | bytes 196640 | tf_op jit(solution)/shard_map/all_to_all | solution.py:91
  89.8 6.1 %shard_map.297 = (bf16[640,512]{1,0:T(8,128)(2,1)}, bf16[640,512]{1,0:T(8,128)(2,1)}, f32[2,640,512]{2,1,0:T(8,128)}, f32[8,512]{1,0:T(8,128)S(1)}) custom-call(f32[80,2,8,512]{3,2,1,0:T(8,128)} %bitcast.210, f32[2,640,1]{2,1,0:T(8,128)} %convert_element_type.104.refs_1_.refs_4_.refs_2_, f32[32,512]{1,0:T(8,128)S(1)} %pad_maximum_fusion.10.refs_2_, ...), custom_call_target="tpu_custom_call" | custom-call | flops 26214400 | bytes 6640640 | tf_op jit(solution)/shard_map/pallas_call | solution.py:208
  101.3 8.9 %shard_map.298.refs_0_ = f32[2,640,512]{2,1,0:T(8,128)} custom-call(bf16[640,512]{1,0:T(8,128)(2,1)} %get-tuple-element.68.refs_0_, bf16[640,512]{1,0:T(8,128)(2,1)} %get-tuple-element.69.refs_1_, bf16[32,208,512]{2,1,0:T(8,128)(2,1)} %bitcast.213), custom_call_target="tpu_custom_call" | custom-call | flops 4026531840 | bytes 10747904 | tf_op jit(solution)/shard_map/pallas_call | solution.py:208
  113.9 9.0 %shard_map.299 = (f32[2,640,512]{2,1,0:T(8,128)}, f32[8,512]{1,0:T(8,128)S(1)}, f32[8,512]{1,0:T(8,128)S(1)}) custom-call(f32[2,640,512]{2,1,0:T(8,128)} %shard_map.298.refs_0_, bf16[640,512]{1,0:T(8,128)(2,1)S(1)} %collective-permute-done.1.refs_1_.refs_2_, bf16[640,512]{1,0:T(8,128)(2,1)S(1)} %collective-permute-done.2.refs_2_.refs_3_, ...), custom_call_target="tpu_custom_call" | custom-call | flops 2013265920 | bytes 13407232 | tf_op jit(solution)/shard_map/pallas_call | solution.py:208
  132.7 10.1 %all-to-all-done.2 = f32[32,3,512]{2,1,0:T(4,128)S(1)} async-done(((f32[32,3,512]{2,1,0:T(4,128)}), f32[32,3,512]{2,1,0:T(4,128)S(1)}, u32[]{:S(2)}, u32[]{:S(2)}) %all-to-all-start.2) | async-done | bytes 196640 | tf_op jit(solution)/shard_map/all_to_all | solution.py:91
  144.7 8.2 %shard_map.300 = (bf16[1280,512]{1,0:T(8,128)(2,1)}, f32[2,640,512]{2,1,0:T(8,128)}, f32[8,2048]{1,0:T(8,128)S(1)}, f32[8,2048]{1,0:T(8,128)S(1)}, f32[8,512]{1,0:T(8,128)S(1)}) custom-call(f32[2,640,512]{2,1,0:T(8,128)} %get-tuple-element.70.refs_0_.refs_7_.refs_1_, f32[1280,1]{1,0:T(8,128)S(1)} %convert_element_type.105.refs_1_.refs_3_.refs_2_, ...), custom_call_target="tpu_custom_call" | custom-call | flops 2684354560 | bytes 8868864 | tf_op jit(solution)/shard_map/pallas_call | solution.py:208
  169.2 17.0 %shard_map.301 = (bf16[1280,2048]{1,0:T(8,128)(2,1)}, f32[96,2048]{1,0:T(8,128)S(1)}, f32[96,4096]{1,0:T(8,128)}) custom-call(bf16[1280,512]{1,0:T(8,128)(2,1)} %get-tuple-element.74.refs_0_, bf16[4,512,512]{2,1,0:T(8,128)(2,1)} %bitcast.230, bf16[1280,2048]{1,0:T(8,128)(2,1)} %bitcast.223, f32[1280,1]{1,0:T(8,128)S(1)} %convert_element_type.105.refs_1_.refs_3_.refs_2_, ...), custom_call_target="tpu_custom_call" | custom-call | flops 2789212160 | bytes 16520192 | tf_op jit(solution)/shard_map/pallas_call | solution.py:208
  201.4 5.0 fusion.2
  233.5 12.2 %all-gather.10.cloned.1.call-start = ((), (), s32[]{:S(2)}) async-start(), calls=%async_computation.7 | async-start | bytes 8312832 | tf_op jit(solution)/shard_map/all_gather | solution.py:420
  311.1 6.0 %fusion = f32[40,2048]{1,0:T(8,128)S(1)} fusion(bf16[2048,2176]{1,0:T(8,128)(2,1)} %all-gather.6.cloned.1.call-done, bf16[20,2048]{1,0:T(8,128)(2,1)S(1)} %fusion.33, bf16[20,2048]{1,0:T(8,128)(2,1)S(1)} %get-tuple-element.145), kind=kOutput, calls=%fused_computation.1 | convolution fusion | flops 335872000 | bytes 8880128 | tf_op jit(solution)/shard_map/dot_general | solution.py:184
  342.8 15.3 %shard_map.302 = (bf16[2048,512]{1,0:T(8,128)(2,1)}, f32[8,2048]{1,0:T(8,128)S(1)}, f32[2,640,512]{2,1,0:T(8,128)}, f32[8,512]{1,0:T(8,128)S(1)}, f32[8,512]{1,0:T(8,128)S(1)}) custom-call(bf16[1280,512]{1,0:T(8,128)(2,1)} %get-tuple-element.74.refs_0_, bf16[4,512,512]{2,1,0:T(8,128)(2,1)} %bitcast.231, bf16[1280,2048]{1,0:T(8,128)(2,1)} %get-tuple-element.79.refs_2_, ...), custom_call_target="tpu_custom_call" | custom-call | flops 8053063680 | bytes 19635200 | tf_op jit(solution)/shard_map/pallas_call | solution.py:208
  365.1 4.6 all-to-all-done.3
  371.1 5.2 shard_map.304
  380.9 8.8 %shard_map.305.refs_0_ = f32[2,640,512]{2,1,0:T(8,128)} custom-call(bf16[640,512]{1,0:T(8,128)(2,1)S(1)} %get-tuple-element.87.refs_0_.refs_4_, bf16[640,512]{1,0:T(8,128)(2,1)} %get-tuple-element.88.refs_1_.refs_5_, bf16[32,208,512]{2,1,0:T(8,128)(2,1)} %bitcast.216), custom_call_target="tpu_custom_call" | custom-call | flops 4026531840 | bytes 10747904 | tf_op jit(solution)/shard_map/pallas_call | solution.py:208
  390.8 8.6 %shard_map.306 = (f32[2,640,512]{2,1,0:T(8,128)}, f32[8,512]{1,0:T(8,128)S(1)}, f32[8,512]{1,0:T(8,128)S(1)}) custom-call(f32[2,640,512]{2,1,0:T(8,128)} %shard_map.305.refs_0_, bf16[640,512]{1,0:T(8,128)(2,1)S(1)} %collective-permute-done.60.refs_1_, bf16[640,512]{1,0:T(8,128)(2,1)S(1)} %collective-permute-done.61.refs_2_, bf16[32,208,512]{2,1,0:T(8,128)(2,1)} %bitcast.217, ...), custom_call_target="tpu_custom_call" | custom-call | flops 2013265920 | bytes 18644992 | tf_op jit(solution)/shard_map/pallas_call | solution.py:208
  404.2 13.1 %shard_map.307 = bf16[3,3,512,512]{3,2,1,0:T(8,128)(2,1)} custom-call(bf16[640,512]{1,0:T(8,128)(2,1)} %get-tuple-element.68.refs_0_, bf16[640,512]{1,0:T(8,128)(2,1)} %get-tuple-element.69.refs_1_, bf16[640,512]{1,0:T(8,128)(2,1)} %copy-done.6, bf16[640,512]{1,0:T(8,128)(2,1)} %copy-done.7, bf16[640,512]{1,0:T(8,128)(2,1)} %copy-done.9, ...), custom_call_target="tpu_custom_call" | custom-call | flops 6039797760 | bytes 8654848 | tf_op jit(solution)/shard_map/pallas_call | solution.py:208
  417.4 5.0 shard_map.308
  424.7 9.2 %shard_map.309 = (bf16[1280,512]{1,0:T(8,128)(2,1)}, bf16[2048,512]{1,0:T(8,128)(2,1)}) custom-call(f32[2,640,512]{2,1,0:T(8,128)} %get-tuple-element.90.refs_8_.refs_0_, f32[80,2,8,512]{3,2,1,0:T(8,128)} %bitcast.212, f32[1280,1]{1,0:T(8,128)S(1)} %convert_element_type.105.refs_1_.refs_3_.refs_2_, f32[48,512]{1,0:T(8,128)S(1)} %pad_maximum_fusion.9.refs_3_, ...), custom_call_target="tpu_custom_call" | custom-call | flops 2684354560 | bytes 13997056 | tf_op jit(solution)/shard_map/pallas_call | solution.py:208
  453.5 5.5 %fusion.4 = f32[128,3000]{0,1:T(8,128)} fusion(bf16[768,5248]{1,0:T(8,128)(2,1)} %all-gather.10.cloned.1.call-done, bf16[768,4224]{1,0:T(8,128)(2,1)} %all-gather.8.cloned.1.call-done.refs_4_), kind=kOutput, calls=%fused_computation.5 | convolution fusion | flops 589824000 | bytes 6451200 | tf_op jit(solution)/shard_map/dot_general | solution.py:1259
  467.7 9.1 %shard_map.316.refs_4_ = bf16[1280,2048]{1,0:T(8,128)(2,1)} custom-call(bf16[1280,512]{1,0:T(8,128)(2,1)} %get-tuple-element.96.refs_0_, bf16[2048,512]{1,0:T(8,128)(2,1)} %bitcast.220, bf16[1280,2048]{1,0:T(8,128)(2,1)} %get-tuple-element.79.refs_2_, f32[80,2048]{1,0:T(8,128)} %copy-done.13, f32[256,2048]{1,0:T(8,128)} %fusion.8.refs_4_, ...), custom_call_target="tpu_custom_call" | custom-call | flops 2684354560 | bytes 14548992 | tf_op jit(solution)/shard_map/pallas_call | solution.py:208
  499.7 6.5 %collective-permute-start.70 = (bf16[1,128,512]{2,1,0:T(8,128)(2,1)S(1)}, bf16[1,128,512]{2,1,0:T(8,128)(2,1)S(1)}, u32[]{:S(2)}, u32[]{:S(2)}) collective-permute-start(bf16[1,128,512]{2,1,0:T(8,128)(2,1)S(1)} %get-tuple-element.112), channel_id=1, source_target_pairs={{0,16},{1,17},{2,18},{3,19},{4,20},{5,21},{6,22},{7,23},{8,24},{9,... | collective-permute-start | bytes 393224 | tf_op jit(solution)/shard_map/ppermute | solution.py:35
  506.2 6.2 %collective-permute-done.70 = bf16[1,128,512]{2,1,0:T(8,128)(2,1)S(1)} collective-permute-done((bf16[1,128,512]{2,1,0:T(8,128)(2,1)S(1)}, bf16[1,128,512]{2,1,0:T(8,128)(2,1)S(1)}, u32[]{:S(2)}, u32[]{:S(2)}) %collective-permute-start.70) | collective-permute-done | bytes 131104 | tf_op jit(solution)/shard_map/ppermute | solution.py:35
  (540 shorter events, 280.8 us)
Async XLA Ops:
  7.2 94.1 %all-gather.12.cloned.1.call-start = ((), (), s32[]{:S(2)}) async-start(), calls=%async_computation.8 | async-start | bytes 7028736 | tf_op jit(solution)/shard_map/all_gather | solution.py:151
  10.0 191.4 %all-gather.6.cloned.1.call-start = ((), (), s32[]{:S(2)}) async-start(), calls=%async_computation.5 | async-start | bytes 9191424 | tf_op jit(solution)/shard_map/all_gather | solution.py:1115
  68.2 19.2 %all-to-all-start.1 = ((f32[32,3,512]{2,1,0:T(4,128)}), f32[32,3,512]{2,1,0:T(4,128)S(1)}, u32[]{:S(2)}, u32[]{:S(2)}) async-start(f32[32,3,512]{2,1,0:T(4,128)} %broadcast_in_dim.69), calls=%async_computation.1 | async-start | bytes 524288 | tf_op jit(solution)/shard_map/all_to_all | solution.py:91
  96.0 14.3 %collective-permute-start.1 = (bf16[640,512]{1,0:T(8,128)(2,1)}, bf16[640,512]{1,0:T(8,128)(2,1)S(1)}, u32[]{:S(2)}, u32[]{:S(2)}) collective-permute-start(bf16[640,512]{1,0:T(8,128)(2,1)} %get-tuple-element.69.refs_1_), channel_id=1, source_target_pairs={{0,1},{1,2},{2,3},{4,5},{5,6},{6,7},{8,9},{9,10},{10,11},{12,13},{... | collective-permute-start | bytes 1966088 | tf_op jit(solution)/shard_map/ppermute | solution.py:1074
  99.4 14.5 %collective-permute-start.2 = (bf16[640,512]{1,0:T(8,128)(2,1)}, bf16[640,512]{1,0:T(8,128)(2,1)S(1)}, u32[]{:S(2)}, u32[]{:S(2)}) collective-permute-start(bf16[640,512]{1,0:T(8,128)(2,1)} %get-tuple-element.68.refs_0_), channel_id=1, source_target_pairs={{1,0},{2,1},{3,2},{5,4},{6,5},{7,6},{9,8},{10,9},{11,10},{13,12},{... | collective-permute-start | bytes 1966088 | tf_op jit(solution)/shard_map/ppermute | solution.py:1075
  123.6 19.2 %all-to-all-start.2 = ((f32[32,3,512]{2,1,0:T(4,128)}), f32[32,3,512]{2,1,0:T(4,128)S(1)}, u32[]{:S(2)}, u32[]{:S(2)}) async-start(f32[32,3,512]{2,1,0:T(4,128)} %broadcast_in_dim.72), calls=%async_computation.2 | async-start | bytes 524288 | tf_op jit(solution)/shard_map/all_to_all | solution.py:91
  127.8 189.5 %all-gather.8.cloned.1.call-start = ((), (), s32[]{:S(2)}) async-start(), calls=%async_computation.6 | async-start | bytes 6690816 | tf_op jit(solution)/shard_map/all_gather | solution.py:420
  229.5 16.2 %collective-permute-start.23 = (f32[1,3000]{1,0:T(1,128)S(1)}, f32[1,3000]{1,0:T(1,128)S(1)}, u32[]{:S(2)}, u32[]{:S(2)}) collective-permute-start(f32[1,3000]{1,0:T(1,128)S(1)} %slice_add_fusion.8), channel_id=1, source_target_pairs={{0,4},{1,5},{2,6},{3,7},{4,0},{5,1},{6,2},{7,3},{8,12},{9,13},{10,... | collective-permute-start | bytes 36008 | tf_op jit(solution)/shard_map/ppermute | solution.py:35
  231.1 14.6 %collective-permute-start.24 = (f32[1,3000]{1,0:T(1,128)S(1)}, f32[1,3000]{1,0:T(1,128)S(1)}, u32[]{:S(2)}, u32[]{:S(2)}) collective-permute-start(f32[1,3000]{1,0:T(1,128)S(1)} %slice_add_fusion.8), channel_id=1, source_target_pairs={{0,6},{1,7},{2,4},{3,5},{4,2},{5,3},{6,0},{7,1},{8,14},{9,15},{10,... | collective-permute-start | bytes 36008 | tf_op jit(solution)/shard_map/ppermute | solution.py:35
  231.4 14.3 %collective-permute-start.22 = (f32[1,8120]{1,0:T(1,128)S(1)}, f32[1,8120]{1,0:T(1,128)S(1)}, u32[]{:S(2)}, u32[]{:S(2)}) collective-permute-start(f32[1,8120]{1,0:T(1,128)S(1)} %concatenate.63), channel_id=1, source_target_pairs={{0,2},{1,3},{2,0},{3,1},{4,6},{5,7},{6,4},{7,5},{8,10},{9,11},{10,... | collective-permute-start | bytes 97448 | tf_op jit(solution)/shard_map/ppermute | solution.py:35
  233.5 220.0 %all-gather.10.cloned.1.call-start = ((), (), s32[]{:S(2)}) async-start(), calls=%async_computation.7 | async-start | bytes 8312832 | tf_op jit(solution)/shard_map/all_gather | solution.py:420
  280.5 19.0 %collective-permute-start.51 = (f32[2,24,4096]{2,1,0:T(8,128)}, f32[2,24,4096]{2,1,0:T(8,128)}, u32[]{:S(2)}, u32[]{:S(2)}) collective-permute-start(f32[2,24,4096]{2,1,0:T(8,128)} %dynamic-slice_bitcast_fusion), channel_id=1, source_target_pairs={{0,1},{1,0},{2,3},{3,2},{4,5},{5,4},{6,7},{7,6},{8,9},{9,8},{10,11... | collective-permute-start | bytes 2359304 | tf_op jit(solution)/shard_map/ppermute | solution.py:35
  376.3 13.3 %collective-permute-start.60 = (bf16[640,512]{1,0:T(8,128)(2,1)}, bf16[640,512]{1,0:T(8,128)(2,1)S(1)}, u32[]{:S(2)}, u32[]{:S(2)}) collective-permute-start(bf16[640,512]{1,0:T(8,128)(2,1)} %get-tuple-element.88.refs_1_.refs_5_), channel_id=1, source_target_pairs={{0,1},{1,2},{2,3},{4,5},{5,6},{6,7},{8,9},{9,10},{10,11},{12,13},{... | collective-permute-start | bytes 1966088 | tf_op jit(solution)/shard_map/ppermute | solution.py:1074
  400.3 22.5 %all-to-all-start.4 = ((f32[32,7,512]{2,1,0:T(8,128)}), f32[32,7,512]{2,1,0:T(8,128)S(1)}, u32[]{:S(2)}, u32[]{:S(2)}) async-start(f32[32,7,512]{2,1,0:T(8,128)} %broadcast_in_dim.88), calls=%async_computation.4 | async-start | bytes 1048576 | tf_op jit(solution)/shard_map/all_to_all | solution.py:91
  422.3 24.1 %collective-permute-start.62 = (bf16[16,144,512]{2,1,0:T(8,128)(2,1)}, bf16[16,144,512]{2,1,0:T(8,128)(2,1)}, u32[]{:S(2)}, u32[]{:S(2)}) collective-permute-start(bf16[16,144,512]{2,1,0:T(8,128)(2,1)} %get-tuple-element.97), channel_id=1, source_target_pairs={{0,1},{1,0},{2,3},{3,2},{4,5},{5,4},{6,7},{7,6},{8,9},{9,8},{10,11... | collective-permute-start | bytes 7077896 | tf_op jit(solution)/shard_map/ppermute | solution.py:35
  422.5 15.3 %collective-permute-start.64 = (bf16[16,64,512]{2,1,0:T(8,128)(2,1)}, bf16[16,64,512]{2,1,0:T(8,128)(2,1)S(1)}, u32[]{:S(2)}, u32[]{:S(2)}) collective-permute-start(bf16[16,64,512]{2,1,0:T(8,128)(2,1)} %get-tuple-element.103), channel_id=1, source_target_pairs={{0,1},{1,0},{2,3},{3,2},{4,5},{5,4},{6,7},{7,6},{8,9},{9,8},{10,11... | collective-permute-start | bytes 3145736 | tf_op jit(solution)/shard_map/ppermute | solution.py:35
  441.3 41.3 %collective-permute-start.66 = (bf16[2,256,512]{2,1,0:T(8,128)(2,1)}, bf16[2,256,512]{2,1,0:T(8,128)(2,1)}, u32[]{:S(2)}, u32[]{:S(2)}) collective-permute-start(bf16[2,256,512]{2,1,0:T(8,128)(2,1)} %get-tuple-element.106), channel_id=1, source_target_pairs={{0,8},{1,9},{2,10},{3,11},{4,12},{5,13},{6,14},{7,15},{8,0},{9,1},... | collective-permute-start | bytes 1572872 | tf_op jit(solution)/shard_map/ppermute | solution.py:35
  446.4 36.2 %collective-permute-start.65 = (bf16[2,256,512]{2,1,0:T(8,128)(2,1)}, bf16[2,256,512]{2,1,0:T(8,128)(2,1)}, u32[]{:S(2)}, u32[]{:S(2)}) collective-permute-start(bf16[2,256,512]{2,1,0:T(8,128)(2,1)} %get-tuple-element.105), channel_id=1, source_target_pairs={{0,8},{1,9},{2,10},{3,11},{4,12},{5,13},{6,14},{7,15},{8,0},{9,1},... | collective-permute-start | bytes 1572872 | tf_op jit(solution)/shard_map/ppermute | solution.py:35
  450.8 26.0 %collective-permute-start.73 = (bf16[4,144,512]{2,1,0:T(8,128)(2,1)S(1)}, bf16[4,144,512]{2,1,0:T(8,128)(2,1)S(1)}, u32[]{:S(2)}, u32[]{:S(2)}) collective-permute-start(bf16[4,144,512]{2,1,0:T(8,128)(2,1)S(1)} %get-tuple-element.113), channel_id=1, source_target_pairs={{0,2},{1,3},{2,0},{3,1},{4,6},{5,7},{6,4},{7,5},{8,10},{9,11},{10,... | collective-permute-start | bytes 1769480 | tf_op jit(solution)/shard_map/ppermute | solution.py:35
  452.3 24.6 %collective-permute-start.74 = (bf16[4,144,512]{2,1,0:T(8,128)(2,1)S(1)}, bf16[4,144,512]{2,1,0:T(8,128)(2,1)}, u32[]{:S(2)}, u32[]{:S(2)}) collective-permute-start(bf16[4,144,512]{2,1,0:T(8,128)(2,1)S(1)} %get-tuple-element.114), channel_id=1, source_target_pairs={{0,4},{1,5},{2,6},{3,7},{4,0},{5,1},{6,2},{7,3},{8,12},{9,13},{10,... | collective-permute-start | bytes 1769480 | tf_op jit(solution)/shard_map/ppermute | solution.py:35
  453.5 25.1 %collective-permute-start.75 = (bf16[4,144,512]{2,1,0:T(8,128)(2,1)}, bf16[4,144,512]{2,1,0:T(8,128)(2,1)}, u32[]{:S(2)}, u32[]{:S(2)}) collective-permute-start(bf16[4,144,512]{2,1,0:T(8,128)(2,1)} %get-tuple-element.115), channel_id=1, source_target_pairs={{0,6},{1,7},{2,4},{3,5},{4,2},{5,3},{6,0},{7,1},{8,14},{9,15},{10,... | collective-permute-start | bytes 1769480 | tf_op jit(solution)/shard_map/ppermute | solution.py:35
  485.4 14.0 %collective-permute-start.67 = (bf16[2,128,512]{2,1,0:T(8,128)(2,1)S(1)}, bf16[2,128,512]{2,1,0:T(8,128)(2,1)S(1)}, u32[]{:S(2)}, u32[]{:S(2)}) collective-permute-start(bf16[2,128,512]{2,1,0:T(8,128)(2,1)S(1)} %get-tuple-element.108), channel_id=1, source_target_pairs={{0,2},{1,3},{2,0},{3,1},{4,6},{5,7},{6,4},{7,5},{8,10},{9,11},{10,... | collective-permute-start | bytes 786440 | tf_op jit(solution)/shard_map/ppermute | solution.py:35
  486.7 12.7 %collective-permute-start.68 = (bf16[2,128,512]{2,1,0:T(8,128)(2,1)S(1)}, bf16[2,128,512]{2,1,0:T(8,128)(2,1)S(1)}, u32[]{:S(2)}, u32[]{:S(2)}) collective-permute-start(bf16[2,128,512]{2,1,0:T(8,128)(2,1)S(1)} %get-tuple-element.109), channel_id=1, source_target_pairs={{0,4},{1,5},{2,6},{3,7},{4,0},{5,1},{6,2},{7,3},{8,12},{9,13},{10,... | collective-permute-start | bytes 786440 | tf_op jit(solution)/shard_map/ppermute | solution.py:35
  497.7 15.0 %collective-permute-start.79 = (bf16[144,512]{1,0:T(8,128)(2,1)S(1)}, bf16[144,512]{1,0:T(8,128)(2,1)S(1)}, u32[]{:S(2)}, u32[]{:S(2)}) collective-permute-start(bf16[144,512]{1,0:T(8,128)(2,1)S(1)} %bitcast.195), channel_id=1, source_target_pairs={{0,2},{1,3},{2,0},{3,1},{4,6},{5,7},{6,4},{7,5},{8,10},{9,11},{10,... | collective-permute-start | bytes 442376 | tf_op jit(solution)/shard_map/ppermute | solution.py:35
  (134 other events, 1022.8 us)
Sparse Core Ops, SparseCore 0:
  11.4 82.1 all-gather.11
  97.1 83.7 all-gather.5
  233.6 69.8 all-gather.7
  318.4 77.0 all-gather.9
